TPU v7x, 32 devices: a whole 2x2x4 slice. The times are simulated.
32 devices in a mesh: design: 2 (over x), gx: 16 (over z, y, core).
Axes of the slice: x: 2, y: 2, z: 4, core: 2. Of those that a mesh axis runs over, the one named last changes fastest.
Arguments:
- electric: float32 [3, 128, 128, 128], P(None, ('design', 'gx')), parts along dimension 1, may hold values from -6 to 6
- magnetic: float32 [3, 128, 128, 128], P(None, ('design', 'gx')), parts along dimension 1, may hold values from -6 to 6
- inv_eps: float32 [128, 128, 128], P(('design', 'gx')), parts along dimension 0, may hold values from 0.08 to 1
- accum: float32 [6, 128, 128, 128], P(None, ('design', 'gx')), parts along dimension 1, may hold values from -6 to 6
- forward: float32 [6, 32, 128, 128], P(None, None, ('design', 'gx')), parts along dimension 2, may hold values from -6 to 6
- pillar_ids: int32 [64, 128], P('gx'), may hold values from 0 to 2047, as said below
Outputs:
- electric_out: float32 [3, 128, 128, 128], P(None, ('design', 'gx')), parts along dimension 1
- magnetic_out: float32 [3, 128, 128, 128], P(None, ('design', 'gx')), parts along dimension 1
- accum_out: float32 [6, 128, 128, 128], P(None, ('design', 'gx')), parts along dimension 1
- pillar_grad: float32 [4096], P(('design', 'gx')), parts along dimension 0
There are 2 independent parts, one for each index of `design`. A program takes and returns all parts, laid end to end along the dimension named above; an argument that names none is the same for every part. Nothing has to cross between parts.
Inputs may be any that keep to these rules, and one draw needn't show every extreme that they name: `pillar_ids`: pillars 128 * d to 128 * (d + 1) - 1 are owned by device block d; a column may belong to a pillar of any owner.
All inputs are finite; a program needn't handle non-finite values.
Results may differ from a plain program's by a relative error of at most 0.000076.
Values sent between devices are 32-bit elements; how exact they have to be, the bound alone decides.
No kernel may reach another device: no remote copies, remote signals or barrier semaphores. Data moves between devices by JAX's collectives and lax.ppermute only.
A program may use at most 64 MiB of HBM per device.

v0:
```python
import math

import jax
import jax.numpy as jnp
from jax import lax
from jax.sharding import PartitionSpec as P

STEPS = 5
PIL_DEV = 128


courant = 0.5
angular = 0.3
sens_scale = 0.05


def passed_along(block, axis, distance):
    devices = range(lax.axis_size(axis))
    route = [(i - distance, i) for i in devices if i - distance in devices]
    return lax.ppermute(block, axis, route)


def next_along(field, axis):
    size = field.shape[axis]
    rest = lax.slice_in_dim(field, 1, size, axis=axis)
    return jnp.concatenate([rest, jnp.zeros_like(lax.slice_in_dim(field, 0, 1, axis=axis))], axis)


def prev_along(field, axis):
    size = field.shape[axis]
    rest = lax.slice_in_dim(field, 0, size - 1, axis=axis)
    return jnp.concatenate([jnp.zeros_like(lax.slice_in_dim(field, 0, 1, axis=axis)), rest], axis)


def owner_terms(flat_ids, flat_sens, count):
    labels = jnp.arange(count, dtype=jnp.int32)
    onehot = (flat_ids[None, :] == labels[:, None]).astype(jnp.float32)
    return jnp.dot(
        onehot, flat_sens, precision=lax.Precision.HIGHEST, preferred_element_type=jnp.float32
    )


def per_device(electric, magnetic, inv_eps, accum, forward, pillar_ids):
    for instant in range(STEPS):
        face_elec = passed_along(electric[1:3, 0:1], "gx", -1)
        elec_x, elec_y, elec_z = (electric[0], electric[1], electric[2])
        beyond_y = jnp.concatenate([elec_y[1:], face_elec[0]], 0)
        beyond_z = jnp.concatenate([elec_z[1:], face_elec[1]], 0)
        curl_x = next_along(elec_z, 1) - elec_z - (next_along(elec_y, 2) - elec_y)
        curl_y = next_along(elec_x, 2) - elec_x - (beyond_z - elec_z)
        curl_z = beyond_y - elec_y - (next_along(elec_x, 1) - elec_x)
        magnetic = magnetic - courant * jnp.stack([curl_x, curl_y, curl_z])
        face_mag = passed_along(magnetic[1:3, -1:], "gx", 1)
        mag_x, mag_y, mag_z = (magnetic[0], magnetic[1], magnetic[2])
        before_y = jnp.concatenate([face_mag[0], mag_y[:-1]], 0)
        before_z = jnp.concatenate([face_mag[1], mag_z[:-1]], 0)
        rot_x = mag_z - prev_along(mag_z, 1) - (mag_y - prev_along(mag_y, 2))
        rot_y = mag_x - prev_along(mag_x, 2) - (mag_z - before_z)
        rot_z = mag_y - before_y - (mag_x - prev_along(mag_x, 1))
        electric = electric + courant * inv_eps[None] * jnp.stack([rot_x, rot_y, rot_z])
        phase = angular * (instant + 1)
        accum = accum + jnp.concatenate([math.cos(phase) * electric, math.sin(phase) * electric])
    depth = forward.shape[1]
    start_z = (accum.shape[3] - depth) // 2
    slab = accum[:, :, :, start_z : start_z + depth]
    real_part = jnp.einsum(
        "cxyz,czxy->xy", slab[0:3], forward[0:3], precision=lax.Precision.HIGHEST
    )
    imag_part = jnp.einsum(
        "cxyz,czxy->xy", slab[3:6], forward[3:6], precision=lax.Precision.HIGHEST
    )
    sens = sens_scale * (real_part - imag_part)
    flat_ids = pillar_ids.reshape(-1)
    flat_sens = sens.reshape(-1)
    pillar_grad = lax.psum_scatter(
        owner_terms(flat_ids, flat_sens, PIL_DEV * lax.axis_size("gx")),
        "gx",
        scatter_dimension=0,
        tiled=True,
    )
    return (electric, magnetic, accum, pillar_grad)


def solution(mesh):
    return jax.shard_map(
        per_device,
        mesh=mesh,
        in_specs=(
            P(None, ("design", "gx"), None, None),
            P(None, ("design", "gx"), None, None),
            P(("design", "gx"), None, None),
            P(None, ("design", "gx"), None, None),
            P(None, None, ("design", "gx"), None),
            P("gx", None),
        ),
        out_specs=(
            P(None, ("design", "gx"), None, None),
            P(None, ("design", "gx"), None, None),
            P(None, ("design", "gx"), None, None),
            P(("design", "gx")),
        ),
        check_vma=False,
    )
```

profile of v0, /device:TPU:0, one launch (start us, length us, event | category | flops | bytes accessed | tf_op | source)
XLA Modules:
  0.0 106.6 jit_solution(11251795515599658447)
XLA Ops:
  0.6 1.0 slice.463
  1.6 1.3 %collective-permute-start = (f32[2,1,128,128]{3,2,1,0:T(8,128)S(1)}, f32[2,1,128,128]{3,2,1,0:T(8,128)S(1)}, u32[]{:S(2)}, u32[]{:S(2)}) collective-permute-start(f32[2,1,128,128]{3,2,1,0:T(8,128)S(1)} %slice.463), channel_id=1, source_target_pairs={{1,0},{2,1},{3,2},{4,3},{5,4},{6,5},{7,6},{8,7},{9,8},{10,9},{11,1... | collective-permute-start | bytes 393224 | tf_op jit(solution)/shard_map/ppermute | solution.py:20
  2.9 1.2 %slice_bitcast_fusion.31 = (f32[4,128,128]{2,1,0:T(8,128)S(1)}, f32[4,128,128]{2,1,0:T(8,128)S(1)}, f32[4,128,128]{2,1,0:T(8,128)S(1)}) fusion(f32[3,4,128,128]{3,2,1,0:T(8,128)} %param.6), kind=kLoop, calls=%fused_computation.139 | loop fusion | bytes 1572864 | tf_op jit(solution)/shard_map/squeeze | solution.py:46
  4.3 0.8 slice_bitcast_fusion.51
  5.1 0.8 slice.600
  5.9 0.6 dynamic-slice
  7.2 1.3 %subtract_bitcast_fusion.9 = (f32[1,4,128,128]{3,2,1,0:T(8,128)S(1)}, f32[1,4,128,128]{3,2,1,0:T(8,128)S(1)}, f32[1,4,128,128]{3,2,1,0:T(8,128)S(1)}) fusion(f32[4,128,127]{2,1,0:T(8,128)} %slice.600, f32[4,127,128]{2,1,0:T(8,128)S(1)} %slice.599, f32[3,4,128,128]{3,2,1,0:T(8,128)S(1)} %copy-done.1, f32[4,127,128]{2,1,0:T(8,128)S(1)} %slice.604, ...), kind=kLoop, calls=%fused_computation.137 | loop fusion | flops 720896 | bytes 3137536 | tf_op jit(solution)/shard_map/stack | solution.py:52
  8.8 4.0 %collective-permute-start.1 = (f32[2,1,128,128]{3,2,1,0:T(8,128)S(1)}, f32[2,1,128,128]{3,2,1,0:T(8,128)S(1)}, u32[]{:S(2)}, u32[]{:S(2)}) collective-permute-start(f32[2,1,128,128]{3,2,1,0:T(8,128)S(1)} %slice.611), channel_id=1, source_target_pairs={{0,1},{1,2},{2,3},{3,4},{4,5},{5,6},{6,7},{7,8},{8,9},{9,10},{10,1... | collective-permute-start | bytes 393224 | tf_op jit(solution)/shard_map/ppermute | solution.py:20
  12.8 0.9 collective-permute-done.1
  13.8 0.3 subtract_bitcast_fusion.8
  14.7 1.3 %collective-permute-start.2 = (f32[2,1,128,128]{3,2,1,0:T(8,128)S(1)}, f32[2,1,128,128]{3,2,1,0:T(8,128)S(1)}, u32[]{:S(2)}, u32[]{:S(2)}) collective-permute-start(f32[2,1,128,128]{3,2,1,0:T(8,128)S(1)} %slice.624), channel_id=1, source_target_pairs={{1,0},{2,1},{3,2},{4,3},{5,4},{6,5},{7,6},{8,7},{9,8},{10,9},{11,1... | collective-permute-start | bytes 393224 | tf_op jit(solution)/shard_map/ppermute | solution.py:20
  16.0 4.0 %collective-permute-done.2 = f32[2,1,128,128]{3,2,1,0:T(8,128)S(1)} collective-permute-done((f32[2,1,128,128]{3,2,1,0:T(8,128)S(1)}, f32[2,1,128,128]{3,2,1,0:T(8,128)S(1)}, u32[]{:S(2)}, u32[]{:S(2)}) %collective-permute-start.2) | collective-permute-done | bytes 131104 | tf_op jit(solution)/shard_map/ppermute | solution.py:20
  20.1 0.2 subtract_bitcast_fusion.7
  20.4 6.2 %collective-permute-start.3 = (f32[2,1,128,128]{3,2,1,0:T(8,128)S(1)}, f32[2,1,128,128]{3,2,1,0:T(8,128)S(1)}, u32[]{:S(2)}, u32[]{:S(2)}) collective-permute-start(f32[2,1,128,128]{3,2,1,0:T(8,128)S(1)} %slice.635), channel_id=1, source_target_pairs={{0,1},{1,2},{2,3},{3,4},{4,5},{5,6},{6,7},{7,8},{8,9},{9,10},{10,1... | collective-permute-start | bytes 393224 | tf_op jit(solution)/shard_map/ppermute | solution.py:20
  26.7 0.9 collective-permute-done.3
  27.6 0.3 subtract_bitcast_fusion.6
  27.9 0.2 broadcast_multiply_fusion.7
  28.6 1.3 %collective-permute-start.4 = (f32[2,1,128,128]{3,2,1,0:T(8,128)S(1)}, f32[2,1,128,128]{3,2,1,0:T(8,128)S(1)}, u32[]{:S(2)}, u32[]{:S(2)}) collective-permute-start(f32[2,1,128,128]{3,2,1,0:T(8,128)S(1)} %slice.648), channel_id=1, source_target_pairs={{1,0},{2,1},{3,2},{4,3},{5,4},{6,5},{7,6},{8,7},{9,8},{10,9},{11,1... | collective-permute-start | bytes 393224 | tf_op jit(solution)/shard_map/ppermute | solution.py:20
  29.9 2.4 %collective-permute-done.4 = f32[2,1,128,128]{3,2,1,0:T(8,128)S(1)} collective-permute-done((f32[2,1,128,128]{3,2,1,0:T(8,128)S(1)}, f32[2,1,128,128]{3,2,1,0:T(8,128)S(1)}, u32[]{:S(2)}, u32[]{:S(2)}) %collective-permute-start.4) | collective-permute-done | bytes 131104 | tf_op jit(solution)/shard_map/ppermute | solution.py:20
  32.5 0.2 fusion.10
  32.8 6.2 %collective-permute-start.5 = (f32[2,1,128,128]{3,2,1,0:T(8,128)S(1)}, f32[2,1,128,128]{3,2,1,0:T(8,128)S(1)}, u32[]{:S(2)}, u32[]{:S(2)}) collective-permute-start(f32[2,1,128,128]{3,2,1,0:T(8,128)S(1)} %slice.659), channel_id=1, source_target_pairs={{0,1},{1,2},{2,3},{3,4},{4,5},{5,6},{6,7},{7,8},{8,9},{9,10},{10,1... | collective-permute-start | bytes 393224 | tf_op jit(solution)/shard_map/ppermute | solution.py:20
  39.0 0.9 collective-permute-done.5
  39.9 0.3 subtract_bitcast_fusion.4
  40.3 0.2 broadcast_multiply_fusion.5
  40.9 1.3 %collective-permute-start.6 = (f32[2,1,128,128]{3,2,1,0:T(8,128)S(1)}, f32[2,1,128,128]{3,2,1,0:T(8,128)S(1)}, u32[]{:S(2)}, u32[]{:S(2)}) collective-permute-start(f32[2,1,128,128]{3,2,1,0:T(8,128)S(1)} %slice.672), channel_id=1, source_target_pairs={{1,0},{2,1},{3,2},{4,3},{5,4},{6,5},{7,6},{8,7},{9,8},{10,9},{11,1... | collective-permute-start | bytes 393224 | tf_op jit(solution)/shard_map/ppermute | solution.py:20
  42.3 2.4 %collective-permute-done.6 = f32[2,1,128,128]{3,2,1,0:T(8,128)S(1)} collective-permute-done((f32[2,1,128,128]{3,2,1,0:T(8,128)S(1)}, f32[2,1,128,128]{3,2,1,0:T(8,128)S(1)}, u32[]{:S(2)}, u32[]{:S(2)}) %collective-permute-start.6) | collective-permute-done | bytes 131104 | tf_op jit(solution)/shard_map/ppermute | solution.py:20
  44.8 0.3 fusion.12
  45.2 7.0 %collective-permute-start.7 = (f32[2,1,128,128]{3,2,1,0:T(8,128)S(1)}, f32[2,1,128,128]{3,2,1,0:T(8,128)S(1)}, u32[]{:S(2)}, u32[]{:S(2)}) collective-permute-start(f32[2,1,128,128]{3,2,1,0:T(8,128)S(1)} %slice.683), channel_id=1, source_target_pairs={{0,1},{1,2},{2,3},{3,4},{4,5},{5,6},{6,7},{7,8},{8,9},{9,10},{10,1... | collective-permute-start | bytes 393224 | tf_op jit(solution)/shard_map/ppermute | solution.py:20
  52.3 0.9 collective-permute-done.7
  53.2 0.4 subtract_bitcast_fusion.2
  53.6 0.2 broadcast_multiply_fusion.3
  54.2 1.3 %collective-permute-start.8 = (f32[2,1,128,128]{3,2,1,0:T(8,128)S(1)}, f32[2,1,128,128]{3,2,1,0:T(8,128)S(1)}, u32[]{:S(2)}, u32[]{:S(2)}) collective-permute-start(f32[2,1,128,128]{3,2,1,0:T(8,128)S(1)} %slice.696), channel_id=1, source_target_pairs={{1,0},{2,1},{3,2},{4,3},{5,4},{6,5},{7,6},{8,7},{9,8},{10,9},{11,1... | collective-permute-start | bytes 393224 | tf_op jit(solution)/shard_map/ppermute | solution.py:20
  55.5 2.4 %collective-permute-done.8 = f32[2,1,128,128]{3,2,1,0:T(8,128)S(1)} collective-permute-done((f32[2,1,128,128]{3,2,1,0:T(8,128)S(1)}, f32[2,1,128,128]{3,2,1,0:T(8,128)S(1)}, u32[]{:S(2)}, u32[]{:S(2)}) %collective-permute-start.8) | collective-permute-done | bytes 131104 | tf_op jit(solution)/shard_map/ppermute | solution.py:20
  58.1 0.4 fusion.14
  58.6 7.1 %collective-permute-start.9 = (f32[2,1,128,128]{3,2,1,0:T(8,128)S(1)}, f32[2,1,128,128]{3,2,1,0:T(8,128)S(1)}, u32[]{:S(2)}, u32[]{:S(2)}) collective-permute-start(f32[2,1,128,128]{3,2,1,0:T(8,128)S(1)} %slice.707), channel_id=1, source_target_pairs={{0,1},{1,2},{2,3},{3,4},{4,5},{5,6},{6,7},{7,8},{8,9},{9,10},{10,1... | collective-permute-start | bytes 393224 | tf_op jit(solution)/shard_map/ppermute | solution.py:20
  65.7 0.9 collective-permute-done.9
  66.7 0.4 subtract_bitcast_fusion
  67.0 0.3 broadcast_multiply_fusion.1
  67.4 1.6 %copy-done.5 = f32[6,4,128,128]{3,2,1,0:T(8,128)S(1)} copy-done((f32[6,4,128,128]{3,2,1,0:T(8,128)S(1)}, f32[6,4,128,128]{3,2,1,0:T(8,128)}, u32[]{:S(2)}) %copy-start.5) | copy-done | bytes 1572888
  69.0 1.0 fusion.5
  70.1 0.5 slice_bitcast_fusion.1
  70.6 0.7 copy-done.3
  71.2 0.3 copy.15
  71.5 0.3 copy.21
  71.8 0.5 copy-done.6
  72.4 1.9 %fusion = f32[1,2048]{1,0:T(1,128)S(1)} fusion(f32[512,1]{0,1:T(1,128)S(1)} %bitcast.376, s32[512]{0:T(512)S(1)} %bitcast.377), kind=kOutput, calls=%fused_computation.1 | convolution fusion | flops 13631488 | bytes 12288 | tf_op jit(solution)/shard_map/dot_general | solution.py:38
  74.3 31.8 %all-reduce.40 = f32[2048]{0:T(1024)S(1)} all-reduce(f32[2048]{0:T(1024)S(1)} %bitcast.375), channel_id=2, replica_groups=mesh['design'=2,'gx'=16] {'gx'}, use_global_device_ids=true, to_apply=%region_0.0.clone | all-reduce | flops 2048 | bytes 16384
  106.0 0.6 dynamic-slice.1
  (84 shorter events, 3.5 us)
Async XLA Ops:
  0.6 3.7 %copy-start.1 = (f32[3,4,128,128]{3,2,1,0:T(8,128)S(1)}, f32[3,4,128,128]{3,2,1,0:T(8,128)}, u32[]{:S(2)}) copy-start(f32[3,4,128,128]{3,2,1,0:T(8,128)} %param.6) | copy-start | bytes 2359300
  1.6 5.6 %collective-permute-start = (f32[2,1,128,128]{3,2,1,0:T(8,128)S(1)}, f32[2,1,128,128]{3,2,1,0:T(8,128)S(1)}, u32[]{:S(2)}, u32[]{:S(2)}) collective-permute-start(f32[2,1,128,128]{3,2,1,0:T(8,128)S(1)} %slice.463), channel_id=1, source_target_pairs={{1,0},{2,1},{3,2},{4,3},{5,4},{6,5},{7,6},{8,7},{9,8},{10,9},{11,1... | collective-permute-start | bytes 393224 | tf_op jit(solution)/shard_map/ppermute | solution.py:20
  4.1 1.8 %copy-start.9 = (u32[32]{0:T(128)S(1)}, u32[32]{0:T(128)}, u32[]{:S(2)}) copy-start(u32[32]{0:T(128)} %constant.118) | copy-start | bytes 388
  4.1 3.1 %copy-start.7 = (f32[4,128,128]{2,1,0:T(8,128)S(1)}, f32[4,128,128]{2,1,0:T(8,128)}, u32[]{:S(2)}) copy-start(f32[4,128,128]{2,1,0:T(8,128)} %param.8) | copy-start | bytes 786436
  7.2 1.4 %copy-start = (f32[3,4,128,128]{3,2,1,0:T(8,128)S(1)}, f32[3,4,128,128]{3,2,1,0:T(8,128)}, u32[]{:S(2)}) copy-start(f32[3,4,128,128]{3,2,1,0:T(8,128)} %param.7) | copy-start | bytes 2359300
  8.8 4.9 %collective-permute-start.1 = (f32[2,1,128,128]{3,2,1,0:T(8,128)S(1)}, f32[2,1,128,128]{3,2,1,0:T(8,128)S(1)}, u32[]{:S(2)}, u32[]{:S(2)}) collective-permute-start(f32[2,1,128,128]{3,2,1,0:T(8,128)S(1)} %slice.611), channel_id=1, source_target_pairs={{0,1},{1,2},{2,3},{3,4},{4,5},{5,6},{6,7},{7,8},{8,9},{9,10},{10,1... | collective-permute-start | bytes 393224 | tf_op jit(solution)/shard_map/ppermute | solution.py:20
  14.7 5.4 %collective-permute-start.2 = (f32[2,1,128,128]{3,2,1,0:T(8,128)S(1)}, f32[2,1,128,128]{3,2,1,0:T(8,128)S(1)}, u32[]{:S(2)}, u32[]{:S(2)}) collective-permute-start(f32[2,1,128,128]{3,2,1,0:T(8,128)S(1)} %slice.624), channel_id=1, source_target_pairs={{1,0},{2,1},{3,2},{4,3},{5,4},{6,5},{7,6},{8,7},{9,8},{10,9},{11,1... | collective-permute-start | bytes 393224 | tf_op jit(solution)/shard_map/ppermute | solution.py:20
  20.4 7.1 %collective-permute-start.3 = (f32[2,1,128,128]{3,2,1,0:T(8,128)S(1)}, f32[2,1,128,128]{3,2,1,0:T(8,128)S(1)}, u32[]{:S(2)}, u32[]{:S(2)}) collective-permute-start(f32[2,1,128,128]{3,2,1,0:T(8,128)S(1)} %slice.635), channel_id=1, source_target_pairs={{0,1},{1,2},{2,3},{3,4},{4,5},{5,6},{6,7},{7,8},{8,9},{9,10},{10,1... | collective-permute-start | bytes 393224 | tf_op jit(solution)/shard_map/ppermute | solution.py:20
  28.6 3.7 %collective-permute-start.4 = (f32[2,1,128,128]{3,2,1,0:T(8,128)S(1)}, f32[2,1,128,128]{3,2,1,0:T(8,128)S(1)}, u32[]{:S(2)}, u32[]{:S(2)}) collective-permute-start(f32[2,1,128,128]{3,2,1,0:T(8,128)S(1)} %slice.648), channel_id=1, source_target_pairs={{1,0},{2,1},{3,2},{4,3},{5,4},{6,5},{7,6},{8,7},{9,8},{10,9},{11,1... | collective-permute-start | bytes 393224 | tf_op jit(solution)/shard_map/ppermute | solution.py:20
  32.8 7.1 %collective-permute-start.5 = (f32[2,1,128,128]{3,2,1,0:T(8,128)S(1)}, f32[2,1,128,128]{3,2,1,0:T(8,128)S(1)}, u32[]{:S(2)}, u32[]{:S(2)}) collective-permute-start(f32[2,1,128,128]{3,2,1,0:T(8,128)S(1)} %slice.659), channel_id=1, source_target_pairs={{0,1},{1,2},{2,3},{3,4},{4,5},{5,6},{6,7},{7,8},{8,9},{9,10},{10,1... | collective-permute-start | bytes 393224 | tf_op jit(solution)/shard_map/ppermute | solution.py:20
  40.9 3.7 %collective-permute-start.6 = (f32[2,1,128,128]{3,2,1,0:T(8,128)S(1)}, f32[2,1,128,128]{3,2,1,0:T(8,128)S(1)}, u32[]{:S(2)}, u32[]{:S(2)}) collective-permute-start(f32[2,1,128,128]{3,2,1,0:T(8,128)S(1)} %slice.672), channel_id=1, source_target_pairs={{1,0},{2,1},{3,2},{4,3},{5,4},{6,5},{7,6},{8,7},{9,8},{10,9},{11,1... | collective-permute-start | bytes 393224 | tf_op jit(solution)/shard_map/ppermute | solution.py:20
  45.2 8.0 %collective-permute-start.7 = (f32[2,1,128,128]{3,2,1,0:T(8,128)S(1)}, f32[2,1,128,128]{3,2,1,0:T(8,128)S(1)}, u32[]{:S(2)}, u32[]{:S(2)}) collective-permute-start(f32[2,1,128,128]{3,2,1,0:T(8,128)S(1)} %slice.683), channel_id=1, source_target_pairs={{0,1},{1,2},{2,3},{3,4},{4,5},{5,6},{6,7},{7,8},{8,9},{9,10},{10,1... | collective-permute-start | bytes 393224 | tf_op jit(solution)/shard_map/ppermute | solution.py:20
  54.2 3.7 %collective-permute-start.8 = (f32[2,1,128,128]{3,2,1,0:T(8,128)S(1)}, f32[2,1,128,128]{3,2,1,0:T(8,128)S(1)}, u32[]{:S(2)}, u32[]{:S(2)}) collective-permute-start(f32[2,1,128,128]{3,2,1,0:T(8,128)S(1)} %slice.696), channel_id=1, source_target_pairs={{1,0},{2,1},{3,2},{4,3},{5,4},{6,5},{7,6},{8,7},{9,8},{10,9},{11,1... | collective-permute-start | bytes 393224 | tf_op jit(solution)/shard_map/ppermute | solution.py:20
  58.5 8.5 %copy-start.2 = (f32[3,4,128,128]{3,2,1,0:T(8,128)}, f32[3,4,128,128]{3,2,1,0:T(8,128)S(1)}, u32[]{:S(2)}) copy-start(f32[3,4,128,128]{3,2,1,0:T(8,128)S(1)} %fusion.14) | copy-start | bytes 2359300
  58.6 8.0 %collective-permute-start.9 = (f32[2,1,128,128]{3,2,1,0:T(8,128)S(1)}, f32[2,1,128,128]{3,2,1,0:T(8,128)S(1)}, u32[]{:S(2)}, u32[]{:S(2)}) collective-permute-start(f32[2,1,128,128]{3,2,1,0:T(8,128)S(1)} %slice.707), channel_id=1, source_target_pairs={{0,1},{1,2},{2,3},{3,4},{4,5},{5,6},{6,7},{7,8},{8,9},{9,10},{10,1... | collective-permute-start | bytes 393224 | tf_op jit(solution)/shard_map/ppermute | solution.py:20
  67.3 2.8 %copy-start.4 = (f32[3,4,128,128]{3,2,1,0:T(8,128)}, f32[3,4,128,128]{3,2,1,0:T(8,128)S(1)}, u32[]{:S(2)}) copy-start(f32[3,4,128,128]{3,2,1,0:T(8,128)S(1)} %get-tuple-element.7) | copy-start | bytes 2359300
  67.3 1.7 %copy-start.5 = (f32[6,4,128,128]{3,2,1,0:T(8,128)S(1)}, f32[6,4,128,128]{3,2,1,0:T(8,128)}, u32[]{:S(2)}) copy-start(f32[6,4,128,128]{3,2,1,0:T(8,128)} %param.9) | copy-start | bytes 4718596
  70.1 1.1 %copy-start.3 = (f32[6,4,128,128]{3,2,1,0:T(8,128)}, f32[6,4,128,128]{3,2,1,0:T(8,128)S(1)}, u32[]{:S(2)}) copy-start(f32[6,4,128,128]{3,2,1,0:T(8,128)S(1)} %fusion.5) | copy-start | bytes 4718596
  71.2 1.0 copy-start.6
  71.2 1.1 %copy-start.8 = (s32[4,128]{1,0:T(4,128)S(1)}, s32[4,128]{1,0:T(4,128)}, u32[]{:S(2)}) copy-start(s32[4,128]{1,0:T(4,128)} %param.11) | copy-start | bytes 6148
where the time goes:
time: 107 us
  starting transfers between devices  36.8 us (34%)
  blocking collectives  31.8 us (30%)
  waiting for transfers between devices  15.8 us (15%)
  local copies, waits for them, and re-layouts  11 us (10%)
  other arithmetic  7.26 us (7%)
  between operations  2.04 us (2%)
  matrix products  1.92 us (2%)
    ppermute x10, starting transfers between devices, passed_along(): return lax.ppermute(block, axis, route)  36.8 us
    unnamed x1, blocking collectives  31.8 us
    ppermute x10, waiting for transfers between devices, passed_along(): return lax.ppermute(block, axis, route)  15.8 us
    unnamed x25, local copies, waits for them, and re-layouts  5.02 us
    slice x20, local copies, waits for them, and re-layouts, next_along(): rest = lax.slice_in_dim(field, 1, size, axis=axis)  2.17 us
  transfers between devices with their start and end apart: 10, of which 9 were waited for; matrix products, arithmetic and copies ran while one was open for 4% of the time, Pallas kernels for 0%

commit v1 on v0

v1 whole, which is shorter than its diff:
```python
import functools
import math

import jax
import jax.numpy as jnp
from jax import lax
from jax.experimental import pallas as pl
from jax.experimental.pallas import tpu as pltpu
from jax.sharding import PartitionSpec as P

STEPS = 5
COURANT = 0.5
ANGULAR = 0.3
SENS_SCALE = 0.05
X, Y, Z = 0, 1, 2
VMEM = pl.BlockSpec(memory_space=pltpu.VMEM)
SMEM = pl.BlockSpec(memory_space=pltpu.SMEM)


def shifted(field, axis, ahead):
    size = field.shape[axis]
    where = lax.broadcasted_iota(jnp.int32, field.shape, axis)
    if ahead:
        return jnp.where(where == size - 1, 0.0, pltpu.roll(field, size - 1, axis))
    return jnp.where(where == 0, 0.0, pltpu.roll(field, 1, axis))


def magnetic_plane(elec, beyond, mag):
    ex, ey, ez = elec
    curl_x = shifted(ez, 0, True) - ez - (shifted(ey, 1, True) - ey)
    far_y, far_z = beyond if beyond is not None else (0.0, 0.0)
    curl_y = shifted(ex, 1, True) - ex - (far_z - ez)
    curl_z = far_y - ey - (shifted(ex, 0, True) - ex)
    return [
        None if m is None else m - COURANT * c
        for m, c in zip(mag, (curl_x, curl_y, curl_z))
    ]


def electric_plane(mag, before, elec, eps):
    hx, hy, hz = mag
    past_y, past_z = before if before is not None else (0.0, 0.0)
    rot_x = hz - shifted(hz, 0, False) - (hy - shifted(hy, 1, False))
    rot_y = hx - shifted(hx, 1, False) - (hz - past_z)
    rot_z = hy - past_y - (hx - shifted(hx, 0, False))
    half = COURANT * eps
    return [e + half * r for e, r in zip(elec, (rot_x, rot_y, rot_z))]


def planes(ref, p):
    return [ref[c, p] for c in range(3)]


def store(ref, p, values):
    for c, v in enumerate(values):
        ref[c, p] = v


def magnetic_all(elec, mag, count, beyond):
    for p in range(count):
        far = (elec[Y, p + 1], elec[Z, p + 1]) if p + 1 < count else beyond
        store(mag, p, magnetic_plane(planes(elec, p), far, planes(mag, p)))


def electric_all(elec, mag, eps, count, before):
    for p in range(count):
        past = (mag[Y, p - 1], mag[Z, p - 1]) if p else before
        store(elec, p, electric_plane(planes(mag, p), past, planes(elec, p), eps[p]))


def opening_kernel(role, elec, mag, eps, far_msg, near_msg):
    last = elec.shape[1] - 1
    even = role[0] == 0
    mid = magnetic_plane(planes(elec, last), None, (None, mag[Y, last], mag[Z, last]))
    mine = (elec[Y, 0], elec[Z, 0])

    @pl.when(even)
    def _():
        for k in range(2):
            near_msg[k] = mid[1 + k]
            far_msg[k] = mine[k]
            far_msg[2 + k] = eps[k]

    @pl.when(jnp.logical_not(even))
    def _():
        for k in range(2):
            near_msg[k] = mine[k]
            far_msg[k] = mid[1 + k]
            far_msg[2 + k] = eps[last - k]


def closed_kernel(role, elec_in, mag_in, eps, near, *rest):
    outs, (elec, mag) = rest[:-2], rest[-2:]
    count = elec_in.shape[1]
    last = count - 1
    even = role[0] == 0

    def send(step, k, value):
        ref = outs[(step - 2) // 2]
        ref[(step % 2) * 2 + k] = value

    @pl.when(even)
    def _():
        src_e, src_m = elec_in, mag_in
        for step in range(1, STEPS):
            keep = min(count, STEPS - step)
            for p in range(keep):
                if p + 1 < count:
                    far = (src_e[Y, p + 1], src_e[Z, p + 1])
                else:
                    far = (near[0], near[1])
                store(mag, p, magnetic_plane(planes(src_e, p), far, planes(src_m, p)))
            for p in range(keep):
                past = (mag[Y, p - 1], mag[Z, p - 1]) if p else None
                new = electric_plane(planes(mag, p), past, planes(src_e, p), eps[p])
                store(elec, p, new)
                if p == 0:
                    send(step + 1, 0, new[Y])
                    send(step + 1, 1, new[Z])
            src_e, src_m = elec, mag

    @pl.when(jnp.logical_not(even))
    def _():
        src_e, src_m = elec_in, mag_in
        for step in range(1, STEPS + 1):
            low = max(0, count - (STEPS + 1 - step))
            for p in range(low, count):
                far = (src_e[Y, p + 1], src_e[Z, p + 1]) if p < last else None
                new = magnetic_plane(planes(src_e, p), far, planes(src_m, p))
                store(mag, p, new)
                if p == last and step > 1:
                    send(step, 0, new[Y])
                    send(step, 1, new[Z])
            if step == STEPS:
                break
            low = max(0, count - (STEPS - step))
            for p in range(low, count):
                if p:
                    past = (mag[Y, p - 1], mag[Z, p - 1])
                else:
                    past = (
                        near[0] + COURANT * src_e[Z, 0],
                        near[1] - COURANT * src_e[Y, 0],
                    )
                store(elec, p, electric_plane(planes(mag, p), past, planes(src_e, p), eps[p]))
            src_e, src_m = elec, mag


LEFT_MAG = {1: 1, 2: 2, 3: 3, 4: 2, 5: 1}
LEFT_ELEC = {1: 1, 2: 2, 3: 2, 4: 1, 5: 0}
RIGHT_MAG = {1: 0, 2: 1, 3: 2, 4: 1, 5: 0}
RIGHT_ELEC = {1: 1, 2: 2, 3: 2, 4: 1, 5: 0}


def beyond_left(step, elec, side_e, side_m):
    for j in range(LEFT_MAG[step]):
        if j == 0:
            far = (elec[Y, 0], elec[Z, 0])
        else:
            far = (side_e[Y, j - 1], side_e[Z, j - 1])
        new = magnetic_plane(planes(side_e, j), far, planes(side_m, j))
        store(side_m, j, new)


def beyond_left_electric(step, side_e, side_m, side_eps):
    for j in range(LEFT_ELEC[step]):
        past = (side_m[Y, j + 1], side_m[Z, j + 1])
        store(side_e, j, electric_plane(planes(side_m, j), past, planes(side_e, j), side_eps[j]))


def beyond_right(step, mag, side_e, side_m, side_eps, last):
    for j in range(RIGHT_MAG[step]):
        far = (side_e[Y, j + 1], side_e[Z, j + 1])
        store(side_m, j, magnetic_plane(planes(side_e, j), far, planes(side_m, j)))
    for j in range(RIGHT_ELEC[step]):
        if j == 0:
            past = (mag[Y, last], mag[Z, last])
        else:
            past = (side_m[Y, j - 1], side_m[Z, j - 1])
        store(side_e, j, electric_plane(planes(side_m, j), past, planes(side_e, j), side_eps[j]))


def open_kernel(step, *refs):
    names = ["role", "elec_in", "mag_in", "eps", "accum_in", "near", "far", "opening"]
    if step > 1:
        names += ["side_e_in", "side_m_in"]
    if step == STEPS:
        names += ["weights", "high", "low"]
    names += ["elec", "mag", "accum"]
    names += ["next_msg", "side_e", "side_m"] if step < STEPS else ["pillars", "side_e", "side_m"]
    r = dict(zip(names, refs, strict=True))
    role, near, far, eps = r["role"], r["near"], r["far"], r["eps"]
    elec_in, mag_in, elec, mag = r["elec_in"], r["mag_in"], r["elec"], r["mag"]
    side_e, side_m = r["side_e"], r["side_m"]
    side_eps = r["opening"].at[2:4]
    count = elec.shape[1]
    last = count - 1
    even = role[0] == 0
    at = 0 if step == 1 else (step % 2) * 2
    if step == 1:
        side_e[...] = jnp.zeros_like(side_e)
        side_m[...] = jnp.zeros_like(side_m)
    else:
        side_e[...] = r["side_e_in"][...]
        side_m[...] = r["side_m_in"][...]

    scale_far = jnp.where(even, role[1], role[2]).astype(jnp.float32)

    def run(is_even):
        if is_even:
            beyond = (near[0], near[1])
            beyond_left(step, elec_in, side_e, side_m)
            past0 = (
                (far[at] + side_m[Y, 0]) * scale_far,
                (far[at + 1] + side_m[Z, 0]) * scale_far,
            )
        else:
            beyond = (
                (far[at] + side_e[Y, 0]) * scale_far,
                (far[at + 1] + side_e[Z, 0]) * scale_far,
            )
            past0 = (
                near[0] + COURANT * elec_in[Z, 0],
                near[1] - COURANT * elec_in[Y, 0],
            )
        for p in range(count):
            nxt = (elec_in[Y, p + 1], elec_in[Z, p + 1]) if p < last else beyond
            store(mag, p, magnetic_plane(planes(elec_in, p), nxt, planes(mag_in, p)))
        if is_even:
            beyond_left_electric(step, side_e, side_m, side_eps)
        else:
            beyond_right(step, mag, side_e, side_m, side_eps, last)
        phase = ANGULAR * step
        for p in range(count):
            past = (mag[Y, p - 1], mag[Z, p - 1]) if p else past0
            new = electric_plane(planes(mag, p), past, planes(elec_in, p), eps[p])
            store(elec, p, new)
            total = None
            for c in range(3):
                for part, wave in ((0, math.cos(phase)), (3, math.sin(phase))):
                    value = r["accum_in"][part + c, p] + wave * new[c]
                    r["accum"][part + c, p] = value
                    if step == STEPS:
                        term = value * r["weights"][part + c, p]
                        total = term if total is None else total + term
            if step == STEPS:
                yield p, total
        if step < STEPS:
            if is_even:
                mid = magnetic_plane(
                    planes(elec, last), None, (None, mag[Y, last], mag[Z, last])
                )
                r["next_msg"][0] = mid[1]
                r["next_msg"][1] = mid[2]
            else:
                r["next_msg"][0] = elec[Y, 0]
                r["next_msg"][1] = elec[Z, 0]

    def whole(is_even):
        sums = None
        for p, total in run(is_even):
            row = lax.dot_general(
                jnp.ones((8, total.shape[1]), jnp.float32), total, (((1,), (1,)), ((), ())),
                precision=lax.Precision.HIGHEST, preferred_element_type=jnp.float32,
            )[0:1]
            owners = r["pillars"].shape[0]
            label = lax.broadcasted_iota(jnp.int32, (owners, total.shape[0]), 0)
            spread = jnp.where(label == r["high"][p : p + 1], row, 0.0)
            term = lax.dot_general(
                spread, r["low"][p], (((1,), (0,)), ((), ())),
                precision=lax.Precision.HIGHEST, preferred_element_type=jnp.float32,
            )
            sums = term if sums is None else sums + term
        if sums is not None:
            r["pillars"][...] = sums

    pl.when(even)(functools.partial(whole, True))
    pl.when(jnp.logical_not(even))(functools.partial(whole, False))


def call(kernel, args, outs, scratch=(), aliases=None, flops=10**6):
    return pl.pallas_call(
        kernel,
        out_shape=outs,
        in_specs=[SMEM] + [VMEM] * (len(args) - 1),
        out_specs=[VMEM] * len(outs),
        scratch_shapes=scratch,
        input_output_aliases=aliases or {},
        compiler_params=pltpu.CompilerParams(vmem_limit_bytes=40 * 2**20),
        cost_estimate=pl.CostEstimate(flops=flops, bytes_accessed=10**6, transcendentals=0),
    )(*args)


def shape_of(*dims):
    return jax.ShapeDtypeStruct(dims, jnp.float32)


def halved(sums, axis):
    size = lax.axis_size(axis)
    me = lax.axis_index(axis)
    bits = size.bit_length() - 1
    block = sums
    for bit in range(bits):
        pair = block.reshape(-1, 2, block.shape[-1])
        mine = (me >> bit) & 1
        keep = jnp.where(mine == 0, pair[:, 0], pair[:, 1])
        give = jnp.where(mine == 0, pair[:, 1], pair[:, 0])
        block = keep + lax.ppermute(give, axis, [(i, i ^ (1 << bit)) for i in range(size)])
    return block.reshape(-1)


def per_device(electric, magnetic, inv_eps, accum, forward, pillar_ids):
    size = lax.axis_size("gx")
    me = lax.axis_index("gx")
    role = jnp.stack([me % 2, jnp.where(me == 0, 0, 1), jnp.where(me == size - 1, 0, 1)]).astype(jnp.int32)
    count, ny, nz = inv_eps.shape
    same_chip = [(i, i ^ 1) for i in range(size)]
    inner = range(1, size - 1, 2)
    next_chip = [(i, i + 1) for i in inner] + [(i + 1, i) for i in inner]

    depth = forward.shape[1]
    start_z = (nz - depth) // 2
    signs = SENS_SCALE * jnp.array([1, 1, 1, -1, -1, -1], jnp.float32)[:, None, None, None]
    weights = jnp.pad(
        signs * jnp.transpose(forward, (0, 2, 3, 1)),
        ((0, 0), (0, 0), (0, 0), (start_z, nz - depth - start_z)),
    )
    per_owner = ny
    high = pillar_ids // per_owner
    low = (pillar_ids % per_owner)[:, :, None] == jnp.arange(per_owner, dtype=jnp.int32)
    low = low.astype(jnp.float32)

    opening, near = call(
        opening_kernel, [role, electric, magnetic, inv_eps], [shape_of(4, ny, nz), shape_of(2, ny, nz)]
    )
    far0 = lax.ppermute(opening, "gx", next_chip)
    near = lax.ppermute(near, "gx", same_chip)
    later = call(
        closed_kernel,
        [role, electric, magnetic, inv_eps, near],
        [shape_of(4, ny, nz), shape_of(4, ny, nz)],
        scratch=[pltpu.VMEM(electric.shape, jnp.float32)] * 2,
    )
    fars = [lax.ppermute(m, "gx", next_chip) for m in later]

    field = shape_of(*electric.shape)
    side = shape_of(3, 3, ny, nz)
    sides = []
    for step in range(1, STEPS + 1):
        far = far0 if step == 1 else fars[(step - 2) // 2]
        args = [role, electric, magnetic, inv_eps, accum, near, far, far0] + sides
        if step < STEPS:
            outs = [field, field, shape_of(*accum.shape), shape_of(2, ny, nz), side, side]
            aliases = {} if step == 1 else {1: 0, 2: 1, 4: 2, 8: 4, 9: 5}
            electric, magnetic, accum, near, *sides = call(
                functools.partial(open_kernel, step), args, outs, aliases=aliases
            )
            near = lax.ppermute(near, "gx", same_chip)
        else:
            args += [weights, high, low]
            outs = [field, field, shape_of(*accum.shape), shape_of(size, per_owner)]
            scratch = [pltpu.VMEM(side.shape, jnp.float32)] * 2
            electric, magnetic, accum, sums = call(
                functools.partial(open_kernel, step), args, outs, scratch=scratch
            )
    return electric, magnetic, accum, halved(sums, "gx")


def solution(mesh):
    return jax.shard_map(
        per_device,
        mesh=mesh,
        in_specs=(
            P(None, ("design", "gx"), None, None),
            P(None, ("design", "gx"), None, None),
            P(("design", "gx"), None, None),
            P(None, ("design", "gx"), None, None),
            P(None, None, ("design", "gx"), None),
            P("gx", None),
        ),
        out_specs=(
            P(None, ("design", "gx"), None, None),
            P(None, ("design", "gx"), None, None),
            P(None, ("design", "gx"), None, None),
            P(("design", "gx")),
        ),
        check_vma=False,
    )
```

time: 107 us -> 65.2 us (0.61)
  blocking collectives: 31.8 us -> 0 us
  starting transfers between devices: 36.8 us -> 18.3 us
  Pallas kernels: 0 us -> 17.4 us
  waiting for transfers between devices: 15.8 us -> 10.3 us
  other arithmetic: 7.26 us -> 2.15 us
  local copies, waits for them, and re-layouts: 11 us -> 15.6 us
  matrix products: 1.92 us -> 0 us
  between operations: 2.04 us -> 0.81 us
    unnamed x1 -> x0, blocking collectives: 31.8 us -> none
    ppermute x10 -> x12, starting transfers between devices: 36.8 us -> 18.3 us  [the longest x5 8.75 us: per_device(): near = lax.ppermute(near, 'gx', same_chip)]
    pallas_call x0 -> x7, Pallas kernels: none -> 17.4 us  [call(): pl.pallas_call(kernel, out_shape=outs, in_specs=[SMEM] + [VMEM] * (len(ar...]
    unnamed x25 -> x41, local copies, waits for them, and re-layouts: 5.02 us -> 13.6 us
    ppermute x10 -> x12, waiting for transfers between devices: 15.8 us -> 10.3 us  [the longest x4 6.82 us: halved(): lax.ppermute(give, axis, [(i, i ^ 1 << bit) for i in range(size)])]
    slice x40 -> x1, local copies, waits for them, and re-layouts: 4.27 us -> 0.01 us  [halved(): keep = jnp.where(mine == 0, pair[:, 0], pair[:, 1])]
    another operation x10 -> x1, other arithmetic: 3.72 us -> 0.08 us  [per_device(): jnp.stack([me % 2, jnp.where(me == 0, 0, 1), jnp.where(me == size - 1, 0,...]
    pad x0 -> x1, local copies, waits for them, and re-layouts: none -> 1.99 us  [per_device(): jnp.pad(signs * jnp.transpose(forward, (0, 2, 3, 1)), ((0, 0), (0, 0), (0...]
  transfers between devices with their start and end apart: 10 -> 12, of which waited for: 9 -> 7; matrix products, arithmetic and copies ran while one was open for 4% -> 9% of each run, Pallas kernels for 0% -> 16%
where the time goes in v1:
time: 65.2 us; the launch traced here: 64.6 us
  starting transfers between devices  18.3 us (28%)
  Pallas kernels  17.4 us (27%)
  local copies, waits for them, and re-layouts  15.6 us (24%)
  waiting for transfers between devices  10.3 us (16%)
  other arithmetic  2.15 us (3%)
  between operations  0.81 us (1%)
    pallas_call x7, Pallas kernels, call(): pl.pallas_call(kernel, out_shape=outs, in_specs=[SMEM] + [VMEM] * (len(ar...  17.4 us
    unnamed x41, local copies, waits for them, and re-layouts  13.6 us
    ppermute x5, starting transfers between devices, per_device(): near = lax.ppermute(near, 'gx', same_chip)  8.75 us
    ppermute x4, waiting for transfers between devices, halved(): lax.ppermute(give, axis, [(i, i ^ 1 << bit) for i in range(size)])  6.82 us
    ppermute x4, starting transfers between devices, halved(): lax.ppermute(give, axis, [(i, i ^ 1 << bit) for i in range(size)])  6.19 us
    ppermute x5, waiting for transfers between devices, per_device(): near = lax.ppermute(near, 'gx', same_chip)  3.47 us
    ppermute x2, starting transfers between devices, per_device(): fars = [lax.ppermute(m, 'gx', next_chip) for m in later]  2.72 us
    pad x1, local copies, waits for them, and re-layouts, per_device(): jnp.pad(signs * jnp.transpose(forward, (0, 2, 3, 1)), ((0, 0), (0, 0), (0...  1.99 us
  transfers between devices with their start and end apart: 12, of which 7 were waited for; matrix products, arithmetic and copies ran while one was open for 9% of the time, Pallas kernels for 16%

profile of v1, /device:TPU:0, one launch (start us, length us, event | category | flops | bytes accessed | tf_op | source)
XLA Modules:
  0.0 64.6 jit_solution(16372772519129699719)
XLA Ops:
  0.6 0.1 pad_add_fusion.role.refs_0_
  0.7 0.9 %copy-done = f32[4,128,128]{2,1,0:T(8,128)S(1)} copy-done((f32[4,128,128]{2,1,0:T(8,128)S(1)}, f32[4,128,128]{2,1,0:T(8,128)}, u32[]{:S(2)}) %copy-start) | copy-done | bytes 262168
  1.7 1.1 %copy-done.13 = f32[3,4,128,128]{3,2,1,0:T(8,128)S(1)} copy-done((f32[3,4,128,128]{3,2,1,0:T(8,128)S(1)}, f32[3,4,128,128]{3,2,1,0:T(8,128)}, u32[]{:S(2)}) %copy-start.13) | copy-done | bytes 786456
  2.8 1.1 %copy-done.14 = f32[3,4,128,128]{3,2,1,0:T(8,128)S(1)} copy-done((f32[3,4,128,128]{3,2,1,0:T(8,128)S(1)}, f32[3,4,128,128]{3,2,1,0:T(8,128)}, u32[]{:S(2)}) %copy-start.14) | copy-done | bytes 786456
  3.9 0.6 shard_map.102
  4.6 0.7 %collective-permute-start.1 = (f32[4,128,128]{2,1,0:T(8,128)S(1)}, f32[4,128,128]{2,1,0:T(8,128)S(1)}, u32[]{:S(2)}, u32[]{:S(2)}) collective-permute-start(f32[4,128,128]{2,1,0:T(8,128)S(1)} %get-tuple-element.37), channel_id=1, source_target_pairs={{1,2},{3,4},{5,6},{7,8},{9,10},{11,12},{13,14},{2,1},{4,3},{6,5},{... | collective-permute-start | bytes 786440 | tf_op jit(solution)/shard_map/ppermute | solution.py:336
  5.3 4.4 %collective-permute-start = (f32[2,128,128]{2,1,0:T(8,128)S(1)}, f32[2,128,128]{2,1,0:T(8,128)S(1)}, u32[]{:S(2)}, u32[]{:S(2)}) collective-permute-start(f32[2,128,128]{2,1,0:T(8,128)S(1)} %get-tuple-element.36), channel_id=1, source_target_pairs={{0,1},{1,0},{2,3},{3,2},{4,5},{5,4},{6,7},{7,6},{8,9},{9,8},{10,11... | collective-permute-start | bytes 393224 | tf_op jit(solution)/shard_map/ppermute | solution.py:337
  9.7 1.0 %collective-permute-done.refs_5_.near = f32[2,128,128]{2,1,0:T(8,128)S(1)} collective-permute-done((f32[2,128,128]{2,1,0:T(8,128)S(1)}, f32[2,128,128]{2,1,0:T(8,128)S(1)}, u32[]{:S(2)}, u32[]{:S(2)}) %collective-permute-start) | collective-permute-done | bytes 131104 | tf_op jit(solution)/shard_map/ppermute | solution.py:337
  10.6 2.3 %shard_map.104 = (f32[4,128,128]{2,1,0:T(8,128)}, f32[4,128,128]{2,1,0:T(8,128)S(1)}) custom-call(s32[3]{0:T(128)S(1)} %pad_add_fusion.role.refs_0_, f32[3,4,128,128]{3,2,1,0:T(8,128)S(1)} %copy-done.13, f32[3,4,128,128]{3,2,1,0:T(8,128)S(1)} %copy-done.14, f32[4,128,128]{2,1,0:T(8,128)S(1)} %copy-done, f32[2,128,128]{2,1,0:T(8,128)S(1)} %collective-permute-done.refs_5_.near), custom_call_target="tpu_custom_call" | custom-call | flops 1000000 | bytes 1000000 | tf_op jit(solution)/shard_map/pallas_call | solution.py:282
  13.0 0.7 %copy-done.16 = f32[4,128,128]{2,1,0:T(8,128)} copy-done((f32[4,128,128]{2,1,0:T(8,128)}, f32[4,128,128]{2,1,0:T(8,128)S(1)}, u32[]{:S(2)}) %copy-start.16) | copy-done | bytes 262168
  13.7 1.4 %collective-permute-start.3 = (f32[4,128,128]{2,1,0:T(8,128)}, f32[4,128,128]{2,1,0:T(8,128)}, u32[]{:S(2)}, u32[]{:S(2)}) collective-permute-start(f32[4,128,128]{2,1,0:T(8,128)} %get-tuple-element.42), channel_id=1, source_target_pairs={{1,2},{3,4},{5,6},{7,8},{9,10},{11,12},{13,14},{2,1},{4,3},{6,5},{... | collective-permute-start | bytes 786440 | tf_op jit(solution)/shard_map/ppermute | solution.py:344
  15.0 2.1 %shard_map.103 = (f32[3,4,128,128]{3,2,1,0:T(8,128)S(1)}, f32[3,4,128,128]{3,2,1,0:T(8,128)S(1)}, f32[6,4,128,128]{3,2,1,0:T(8,128)S(1)}, f32[2,128,128]{2,1,0:T...) custom-call(s32[3]{0:T(128)S(1)} %pad_add_fusion.role.refs_0_, ...), custom_call_target="tpu_custom_call" | custom-call | flops 1000000 | bytes 1000000 | tf_op jit(solution)/shard_map/pallas_call | solution.py:282
  17.1 0.8 %copy-done.2 = f32[3,3,128,128]{3,2,1,0:T(8,128)} copy-done((f32[3,3,128,128]{3,2,1,0:T(8,128)}, f32[3,3,128,128]{3,2,1,0:T(8,128)S(1)}, u32[]{:S(2)}) %copy-start.2) | copy-done | bytes 589848
  17.9 0.8 %copy-done.6 = f32[3,3,128,128]{3,2,1,0:T(8,128)} copy-done((f32[3,3,128,128]{3,2,1,0:T(8,128)}, f32[3,3,128,128]{3,2,1,0:T(8,128)S(1)}, u32[]{:S(2)}) %copy-start.6) | copy-done | bytes 589848
  18.7 0.7 %copy-done.10 = f32[4,128,128]{2,1,0:T(8,128)} copy-done((f32[4,128,128]{2,1,0:T(8,128)}, f32[4,128,128]{2,1,0:T(8,128)S(1)}, u32[]{:S(2)}) %copy-start.10) | copy-done | bytes 262168
  19.5 2.1 %collective-permute-start.2 = (f32[2,128,128]{2,1,0:T(8,128)}, f32[2,128,128]{2,1,0:T(8,128)S(1)}, u32[]{:S(2)}, u32[]{:S(2)}) collective-permute-start(f32[2,128,128]{2,1,0:T(8,128)} %get-tuple-element.41), channel_id=1, source_target_pairs={{0,1},{1,0},{2,3},{3,2},{4,5},{5,4},{6,7},{7,6},{8,9},{9,8},{10,11... | collective-permute-start | bytes 393224 | tf_op jit(solution)/shard_map/ppermute | solution.py:358
  21.6 2.6 %copy.56 = f32[6,32,4,128]{1,3,2,0:T(8,128)} copy(f32[6,32,4,128]{3,2,1,0:T(4,128)} %param.11) | data formatting | bytes 786432 | tf_op args[4]
  24.2 1.4 %collective-permute-start.6 = (f32[4,128,128]{2,1,0:T(8,128)}, f32[4,128,128]{2,1,0:T(8,128)}, u32[]{:S(2)}, u32[]{:S(2)}) collective-permute-start(f32[4,128,128]{2,1,0:T(8,128)} %copy-done.16), channel_id=1, source_target_pairs={{1,2},{3,4},{5,6},{7,8},{9,10},{11,12},{13,14},{2,1},{4,3},{6,5},{... | collective-permute-start | bytes 786440 | tf_op jit(solution)/shard_map/ppermute | solution.py:344
  25.6 0.0 collective-permute-done.2.refs_5_
  25.6 0.0 collective-permute-done.3.refs_6_
  25.6 0.0 copy-start.3
  25.6 1.1 %copy-done.3 = f32[3,3,128,128]{3,2,1,0:T(8,128)S(1)} copy-done((f32[3,3,128,128]{3,2,1,0:T(8,128)S(1)}, f32[3,3,128,128]{3,2,1,0:T(8,128)}, u32[]{:S(2)}) %copy-start.3) | copy-done | bytes 589848
  26.6 1.1 %copy-done.7 = f32[3,3,128,128]{3,2,1,0:T(8,128)S(1)} copy-done((f32[3,3,128,128]{3,2,1,0:T(8,128)S(1)}, f32[3,3,128,128]{3,2,1,0:T(8,128)}, u32[]{:S(2)}) %copy-start.7) | copy-done | bytes 589848
  27.7 0.9 %copy-done.11 = f32[4,128,128]{2,1,0:T(8,128)S(1)} copy-done((f32[4,128,128]{2,1,0:T(8,128)S(1)}, f32[4,128,128]{2,1,0:T(8,128)}, u32[]{:S(2)}) %copy-start.11) | copy-done | bytes 262168
  28.7 3.2 %shard_map.105 = (f32[3,4,128,128]{3,2,1,0:T(8,128)S(1)}, f32[3,4,128,128]{3,2,1,0:T(8,128)S(1)}, f32[6,4,128,128]{3,2,1,0:T(8,128)S(1)}, f32[2,128,128]{2,1,0:T...) custom-call(s32[3]{0:T(128)S(1)} %pad_add_fusion.role.refs_0_, ...), custom_call_target="tpu_custom_call", output_to_operand_aliasing={{0}: (1, {}), {1}: (2, {}), {2}: (4, {}), {4}: (8, {}), {5}... | custom-call | flops 1000000 | bytes 1000000 | tf_op jit(solution)/shard_map/pallas_call | solution.py:282
  31.8 0.8 %copy-done.4 = f32[3,3,128,128]{3,2,1,0:T(8,128)} copy-done((f32[3,3,128,128]{3,2,1,0:T(8,128)}, f32[3,3,128,128]{3,2,1,0:T(8,128)S(1)}, u32[]{:S(2)}) %copy-start.4) | copy-done | bytes 589848
  32.6 0.8 %copy-done.8 = f32[3,3,128,128]{3,2,1,0:T(8,128)} copy-done((f32[3,3,128,128]{3,2,1,0:T(8,128)}, f32[3,3,128,128]{3,2,1,0:T(8,128)S(1)}, u32[]{:S(2)}) %copy-start.8) | copy-done | bytes 589848
  33.5 2.1 %collective-permute-start.4 = (f32[2,128,128]{2,1,0:T(8,128)}, f32[2,128,128]{2,1,0:T(8,128)S(1)}, u32[]{:S(2)}, u32[]{:S(2)}) collective-permute-start(f32[2,128,128]{2,1,0:T(8,128)} %get-tuple-element.48), channel_id=1, source_target_pairs={{0,1},{1,0},{2,3},{3,2},{4,5},{5,4},{6,7},{7,6},{8,9},{9,8},{10,11... | collective-permute-start | bytes 393224 | tf_op jit(solution)/shard_map/ppermute | solution.py:358
  35.5 1.4 %multiply_bitcast_fusion = f32[6,4,128,32]{3,2,1,0:T(8,128)} fusion(f32[6,32,4,128]{1,3,2,0:T(8,128)S(1)} %copy-done.17, f32[6]{0:T(128)S(1)} %copy-done.19), kind=kLoop, calls=%fused_computation | loop fusion | flops 98304 | bytes 786456 | tf_op jit(solution)/shard_map/mul | solution.py:325
  36.9 2.0 %pad.4.refs_10_ = f32[6,4,128,128]{3,2,1,0:T(8,128)S(1)} pad(f32[6,4,128,32]{3,2,1,0:T(8,128)} %multiply_bitcast_fusion, f32[]{:T(128)} %constant.49.clone.1), padding=0_0x0_0x0_0x48_48 | pad | bytes 1966084 | tf_op jit(solution)/shard_map/jit(_pad)/pad | solution.py:324
  39.0 0.0 copy-start.18
  39.0 2.5 %shard_map.106 = (f32[3,4,128,128]{3,2,1,0:T(8,128)S(1)}, f32[3,4,128,128]{3,2,1,0:T(8,128)S(1)}, f32[6,4,128,128]{3,2,1,0:T(8,128)S(1)}, f32[2,128,128]{2,1,0:T...) custom-call(s32[3]{0:T(128)S(1)} %pad_add_fusion.role.refs_0_, ...), custom_call_target="tpu_custom_call", output_to_operand_aliasing={{0}: (1, {}), {1}: (2, {}), {2}: (4, {}), {4}: (8, {}), {5}... | custom-call | flops 1000000 | bytes 1000000 | tf_op jit(solution)/shard_map/pallas_call | solution.py:282
  41.5 0.1 collective-permute-start.5
  41.6 1.3 %collective-permute-done.5.refs_5_ = f32[2,128,128]{2,1,0:T(8,128)S(1)} collective-permute-done((f32[2,128,128]{2,1,0:T(8,128)S(1)}, f32[2,128,128]{2,1,0:T(8,128)S(1)}, u32[]{:S(2)}, u32[]{:S(2)}) %collective-permute-start.5) | collective-permute-done | bytes 131104 | tf_op jit(solution)/shard_map/ppermute | solution.py:358
  42.9 2.5 %shard_map.107 = (f32[3,4,128,128]{3,2,1,0:T(8,128)S(1)}, f32[3,4,128,128]{3,2,1,0:T(8,128)S(1)}, f32[6,4,128,128]{3,2,1,0:T(8,128)S(1)}, f32[2,128,128]{2,1,0:T...) custom-call(s32[3]{0:T(128)S(1)} %pad_add_fusion.role.refs_0_, ...), custom_call_target="tpu_custom_call", output_to_operand_aliasing={{0}: (1, {}), {1}: (2, {}), {2}: (4, {}), {4}: (8, {}), {5}... | custom-call | flops 1000000 | bytes 1000000 | tf_op jit(solution)/shard_map/pallas_call | solution.py:282
  45.4 0.1 collective-permute-start.7
  45.5 0.1 fusion.refs_12_
  45.6 1.2 %collective-permute-done.7.refs_5_ = f32[2,128,128]{2,1,0:T(8,128)S(1)} collective-permute-done((f32[2,128,128]{2,1,0:T(8,128)S(1)}, f32[2,128,128]{2,1,0:T(8,128)S(1)}, u32[]{:S(2)}, u32[]{:S(2)}) %collective-permute-start.7) | collective-permute-done | bytes 131104 | tf_op jit(solution)/shard_map/ppermute | solution.py:358
  46.8 4.2 %shard_map.108 = (f32[3,4,128,128]{3,2,1,0:T(8,128)}, f32[3,4,128,128]{3,2,1,0:T(8,128)}, f32[6,4,128,128]{3,2,1,0:T(8,128)}, f32[16,128]{1,0:T(8,128)S(1)}) custom-call(s32[3]{0:T(128)S(1)} %pad_add_fusion.role.refs_0_, f32[3,4,128,128]{3,2,1,0:T(8,128)S(1)} %get-tuple-element.58.refs_1_, f32[3,4,128,128]{3,2,1,0:T(8,128)S(1)} %get-tuple-element.59.refs_2_, ...), custom_call_target="tpu_custom_call" | custom-call | flops 1000000 | bytes 1000000 | tf_op jit(solution)/shard_map/pallas_call | solution.py:282
  51.0 0.2 collective-permute-start.8
  51.2 1.0 %collective-permute-done.8 = f32[8,128]{1,0:T(8,128)S(1)} collective-permute-done((f32[8,128]{1,0:T(8,128)S(1)}, f32[8,128]{1,0:T(8,128)S(1)}, u32[]{:S(2)}, u32[]{:S(2)}) %collective-permute-start.8) | collective-permute-done | bytes 4128 | tf_op jit(solution)/shard_map/ppermute | solution.py:308
  52.3 1.7 %collective-permute-start.9 = (f32[4,128]{1,0:T(4,128)S(1)}, f32[4,128]{1,0:T(4,128)S(1)}, u32[]{:S(2)}, u32[]{:S(2)}) collective-permute-start(f32[4,128]{1,0:T(4,128)S(1)} %bitcast.53), channel_id=1, source_target_pairs={{0,2},{1,3},{2,0},{3,1},{4,6},{5,7},{6,4},{7,5},{8,10},{9,11},{10,... | collective-permute-start | bytes 6152 | tf_op jit(solution)/shard_map/ppermute | solution.py:308
  54.0 2.0 %collective-permute-done.9 = f32[4,128]{1,0:T(4,128)S(1)} collective-permute-done((f32[4,128]{1,0:T(4,128)S(1)}, f32[4,128]{1,0:T(4,128)S(1)}, u32[]{:S(2)}, u32[]{:S(2)}) %collective-permute-start.9) | collective-permute-done | bytes 2080 | tf_op jit(solution)/shard_map/ppermute | solution.py:308
  55.9 1.6 %collective-permute-start.10 = (f32[2,128]{1,0:T(2,128)S(1)}, f32[2,128]{1,0:T(2,128)S(1)}, u32[]{:S(2)}, u32[]{:S(2)}) collective-permute-start(f32[2,128]{1,0:T(2,128)S(1)} %bitcast.54), channel_id=1, source_target_pairs={{0,4},{1,5},{2,6},{3,7},{4,0},{5,1},{6,2},{7,3},{8,12},{9,13},{10,... | collective-permute-start | bytes 3080 | tf_op jit(solution)/shard_map/ppermute | solution.py:308
  57.6 2.0 %collective-permute-done.10 = f32[2,128]{1,0:T(2,128)S(1)} collective-permute-done((f32[2,128]{1,0:T(2,128)S(1)}, f32[2,128]{1,0:T(2,128)S(1)}, u32[]{:S(2)}, u32[]{:S(2)}) %collective-permute-start.10) | collective-permute-done | bytes 1056 | tf_op jit(solution)/shard_map/ppermute | solution.py:308
  59.6 2.7 %collective-permute-start.11 = (f32[1,128]{1,0:T(1,128)S(1)}, f32[1,128]{1,0:T(1,128)S(1)}, u32[]{:S(2)}, u32[]{:S(2)}) collective-permute-start(f32[1,128]{1,0:T(1,128)S(1)} %fusion.6), channel_id=1, source_target_pairs={{0,8},{1,9},{2,10},{3,11},{4,12},{5,13},{6,14},{7,15},{8,0},{9,1},... | collective-permute-start | bytes 1544 | tf_op jit(solution)/shard_map/ppermute | solution.py:308
  62.2 1.9 %collective-permute-done.11 = f32[1,128]{1,0:T(1,128)S(1)} collective-permute-done((f32[1,128]{1,0:T(1,128)S(1)}, f32[1,128]{1,0:T(1,128)S(1)}, u32[]{:S(2)}, u32[]{:S(2)}) %collective-permute-start.11) | collective-permute-done | bytes 544 | tf_op jit(solution)/shard_map/ppermute | solution.py:308
  64.1 0.5 fusion.5
  (38 shorter events, 0.1 us)
Async XLA Ops:
  0.7 1.0 %copy-start = (f32[4,128,128]{2,1,0:T(8,128)S(1)}, f32[4,128,128]{2,1,0:T(8,128)}, u32[]{:S(2)}) copy-start(f32[4,128,128]{2,1,0:T(8,128)} %refs_3_.9) | copy-start | bytes 786436
  1.7 1.1 %copy-start.13 = (f32[3,4,128,128]{3,2,1,0:T(8,128)S(1)}, f32[3,4,128,128]{3,2,1,0:T(8,128)}, u32[]{:S(2)}) copy-start(f32[3,4,128,128]{3,2,1,0:T(8,128)} %elec_in.1) | copy-start | bytes 2359300
  2.8 1.1 %copy-start.14 = (f32[3,4,128,128]{3,2,1,0:T(8,128)S(1)}, f32[3,4,128,128]{3,2,1,0:T(8,128)}, u32[]{:S(2)}) copy-start(f32[3,4,128,128]{3,2,1,0:T(8,128)} %mag_in.1) | copy-start | bytes 2359300
  3.9 11.1 %copy-start.15 = (f32[6,4,128,128]{3,2,1,0:T(8,128)S(1)}, f32[6,4,128,128]{3,2,1,0:T(8,128)}, u32[]{:S(2)}) copy-start(f32[6,4,128,128]{3,2,1,0:T(8,128)} %refs_4_.1) | copy-start | bytes 4718596
  4.6 10.4 %collective-permute-start.1 = (f32[4,128,128]{2,1,0:T(8,128)S(1)}, f32[4,128,128]{2,1,0:T(8,128)S(1)}, u32[]{:S(2)}, u32[]{:S(2)}) collective-permute-start(f32[4,128,128]{2,1,0:T(8,128)S(1)} %get-tuple-element.37), channel_id=1, source_target_pairs={{1,2},{3,4},{5,6},{7,8},{9,10},{11,12},{13,14},{2,1},{4,3},{6,5},{... | collective-permute-start | bytes 786440 | tf_op jit(solution)/shard_map/ppermute | solution.py:336
  5.3 5.4 %collective-permute-start = (f32[2,128,128]{2,1,0:T(8,128)S(1)}, f32[2,128,128]{2,1,0:T(8,128)S(1)}, u32[]{:S(2)}, u32[]{:S(2)}) collective-permute-start(f32[2,128,128]{2,1,0:T(8,128)S(1)} %get-tuple-element.36), channel_id=1, source_target_pairs={{0,1},{1,0},{2,3},{3,2},{4,5},{5,4},{6,7},{7,6},{8,9},{9,8},{10,11... | collective-permute-start | bytes 393224 | tf_op jit(solution)/shard_map/ppermute | solution.py:337
  13.0 0.7 %copy-start.16 = (f32[4,128,128]{2,1,0:T(8,128)}, f32[4,128,128]{2,1,0:T(8,128)S(1)}, u32[]{:S(2)}) copy-start(f32[4,128,128]{2,1,0:T(8,128)S(1)} %get-tuple-element.55) | copy-start | bytes 786436
  13.7 11.9 %collective-permute-start.3 = (f32[4,128,128]{2,1,0:T(8,128)}, f32[4,128,128]{2,1,0:T(8,128)}, u32[]{:S(2)}, u32[]{:S(2)}) collective-permute-start(f32[4,128,128]{2,1,0:T(8,128)} %get-tuple-element.42), channel_id=1, source_target_pairs={{1,2},{3,4},{5,6},{7,8},{9,10},{11,12},{13,14},{2,1},{4,3},{6,5},{... | collective-permute-start | bytes 786440 | tf_op jit(solution)/shard_map/ppermute | solution.py:344
  17.1 0.8 %copy-start.2 = (f32[3,3,128,128]{3,2,1,0:T(8,128)}, f32[3,3,128,128]{3,2,1,0:T(8,128)S(1)}, u32[]{:S(2)}) copy-start(f32[3,3,128,128]{3,2,1,0:T(8,128)S(1)} %get-tuple-element.43.refs_8_) | copy-start | bytes 1769476
  17.9 0.8 %copy-start.6 = (f32[3,3,128,128]{3,2,1,0:T(8,128)}, f32[3,3,128,128]{3,2,1,0:T(8,128)S(1)}, u32[]{:S(2)}) copy-start(f32[3,3,128,128]{3,2,1,0:T(8,128)S(1)} %get-tuple-element.44.refs_9_) | copy-start | bytes 1769476
  18.7 0.7 %copy-start.10 = (f32[4,128,128]{2,1,0:T(8,128)}, f32[4,128,128]{2,1,0:T(8,128)S(1)}, u32[]{:S(2)}) copy-start(f32[4,128,128]{2,1,0:T(8,128)S(1)} %collective-permute-done.1.refs_6_.refs_7_) | copy-start | bytes 786436
  19.5 6.1 %copy-start.1 = (f32[4,128,128]{2,1,0:T(8,128)S(1)}, f32[4,128,128]{2,1,0:T(8,128)}, u32[]{:S(2)}) copy-start(f32[4,128,128]{2,1,0:T(8,128)} %refs_3_.9) | copy-start | bytes 786436
  19.5 6.1 %collective-permute-start.2 = (f32[2,128,128]{2,1,0:T(8,128)}, f32[2,128,128]{2,1,0:T(8,128)S(1)}, u32[]{:S(2)}, u32[]{:S(2)}) collective-permute-start(f32[2,128,128]{2,1,0:T(8,128)} %get-tuple-element.41), channel_id=1, source_target_pairs={{0,1},{1,0},{2,3},{3,2},{4,5},{5,4},{6,7},{7,6},{8,9},{9,8},{10,11... | collective-permute-start | bytes 393224 | tf_op jit(solution)/shard_map/ppermute | solution.py:358
  24.2 17.4 %collective-permute-start.6 = (f32[4,128,128]{2,1,0:T(8,128)}, f32[4,128,128]{2,1,0:T(8,128)}, u32[]{:S(2)}, u32[]{:S(2)}) collective-permute-start(f32[4,128,128]{2,1,0:T(8,128)} %copy-done.16), channel_id=1, source_target_pairs={{1,2},{3,4},{5,6},{7,8},{9,10},{11,12},{13,14},{2,1},{4,3},{6,5},{... | collective-permute-start | bytes 786440 | tf_op jit(solution)/shard_map/ppermute | solution.py:344
  25.6 1.1 %copy-start.3 = (f32[3,3,128,128]{3,2,1,0:T(8,128)S(1)}, f32[3,3,128,128]{3,2,1,0:T(8,128)}, u32[]{:S(2)}) copy-start(f32[3,3,128,128]{3,2,1,0:T(8,128)} %copy-done.2) | copy-start | bytes 1769476
  26.6 1.1 %copy-start.7 = (f32[3,3,128,128]{3,2,1,0:T(8,128)S(1)}, f32[3,3,128,128]{3,2,1,0:T(8,128)}, u32[]{:S(2)}) copy-start(f32[3,3,128,128]{3,2,1,0:T(8,128)} %copy-done.6) | copy-start | bytes 1769476
  27.7 0.9 %copy-start.11 = (f32[4,128,128]{2,1,0:T(8,128)S(1)}, f32[4,128,128]{2,1,0:T(8,128)}, u32[]{:S(2)}) copy-start(f32[4,128,128]{2,1,0:T(8,128)} %copy-done.10) | copy-start | bytes 786436
  28.7 6.9 %copy-start.17 = (f32[6,32,4,128]{1,3,2,0:T(8,128)S(1)}, f32[6,32,4,128]{1,3,2,0:T(8,128)}, u32[]{:S(2)}) copy-start(f32[6,32,4,128]{1,3,2,0:T(8,128)} %copy.56) | copy-start | bytes 1179652
  28.7 6.9 %copy-start.19 = (f32[6]{0:T(128)S(1)}, f32[6]{0:T(128)}, u32[]{:S(2)}) copy-start(f32[6]{0:T(128)} %constant.64) | copy-start | bytes 76
  31.8 0.8 %copy-start.4 = (f32[3,3,128,128]{3,2,1,0:T(8,128)}, f32[3,3,128,128]{3,2,1,0:T(8,128)S(1)}, u32[]{:S(2)}) copy-start(f32[3,3,128,128]{3,2,1,0:T(8,128)S(1)} %get-tuple-element.49.refs_8_) | copy-start | bytes 1769476
  32.6 0.8 %copy-start.8 = (f32[3,3,128,128]{3,2,1,0:T(8,128)}, f32[3,3,128,128]{3,2,1,0:T(8,128)S(1)}, u32[]{:S(2)}) copy-start(f32[3,3,128,128]{3,2,1,0:T(8,128)S(1)} %get-tuple-element.50.refs_9_) | copy-start | bytes 1769476
  33.5 5.5 %collective-permute-start.4 = (f32[2,128,128]{2,1,0:T(8,128)}, f32[2,128,128]{2,1,0:T(8,128)S(1)}, u32[]{:S(2)}, u32[]{:S(2)}) collective-permute-start(f32[2,128,128]{2,1,0:T(8,128)} %get-tuple-element.48), channel_id=1, source_target_pairs={{0,1},{1,0},{2,3},{3,2},{4,5},{5,4},{6,7},{7,6},{8,9},{9,8},{10,11... | collective-permute-start | bytes 393224 | tf_op jit(solution)/shard_map/ppermute | solution.py:358
  36.9 2.0 %copy-start.5 = (f32[3,3,128,128]{3,2,1,0:T(8,128)S(1)}, f32[3,3,128,128]{3,2,1,0:T(8,128)}, u32[]{:S(2)}) copy-start(f32[3,3,128,128]{3,2,1,0:T(8,128)} %copy-done.4) | copy-start | bytes 1769476
  36.9 2.0 %copy-start.9 = (f32[3,3,128,128]{3,2,1,0:T(8,128)S(1)}, f32[3,3,128,128]{3,2,1,0:T(8,128)}, u32[]{:S(2)}) copy-start(f32[3,3,128,128]{3,2,1,0:T(8,128)} %copy-done.8) | copy-start | bytes 1769476
  36.9 2.0 %copy-start.12 = (f32[4,128,128]{2,1,0:T(8,128)S(1)}, f32[4,128,128]{2,1,0:T(8,128)}, u32[]{:S(2)}) copy-start(f32[4,128,128]{2,1,0:T(8,128)} %copy-done.10) | copy-start | bytes 786436
  39.0 2.6 %copy-start.18 = (s32[4,128]{1,0:T(4,128)S(1)}, s32[4,128]{1,0:T(4,128)}, u32[]{:S(2)}) copy-start(s32[4,128]{1,0:T(4,128)} %param.12) | copy-start | bytes 6148
  41.5 1.4 %collective-permute-start.5 = (f32[2,128,128]{2,1,0:T(8,128)S(1)}, f32[2,128,128]{2,1,0:T(8,128)S(1)}, u32[]{:S(2)}, u32[]{:S(2)}) collective-permute-start(f32[2,128,128]{2,1,0:T(8,128)S(1)} %get-tuple-element.54), channel_id=1, source_target_pairs={{0,1},{1,0},{2,3},{3,2},{4,5},{5,4},{6,7},{7,6},{8,9},{9,8},{10,11... | collective-permute-start | bytes 393224 | tf_op jit(solution)/shard_map/ppermute | solution.py:358
  45.4 1.4 %collective-permute-start.7 = (f32[2,128,128]{2,1,0:T(8,128)S(1)}, f32[2,128,128]{2,1,0:T(8,128)S(1)}, u32[]{:S(2)}, u32[]{:S(2)}) collective-permute-start(f32[2,128,128]{2,1,0:T(8,128)S(1)} %get-tuple-element.61), channel_id=1, source_target_pairs={{0,1},{1,0},{2,3},{3,2},{4,5},{5,4},{6,7},{7,6},{8,9},{9,8},{10,11... | collective-permute-start | bytes 393224 | tf_op jit(solution)/shard_map/ppermute | solution.py:358
  51.0 1.2 %collective-permute-start.8 = (f32[8,128]{1,0:T(8,128)S(1)}, f32[8,128]{1,0:T(8,128)S(1)}, u32[]{:S(2)}, u32[]{:S(2)}) collective-permute-start(f32[8,128]{1,0:T(8,128)S(1)} %select_bitcast_fusion), channel_id=1, source_target_pairs={{0,1},{1,0},{2,3},{3,2},{4,5},{5,4},{6,7},{7,6},{8,9},{9,8},{10,11... | collective-permute-start | bytes 12296 | tf_op jit(solution)/shard_map/ppermute | solution.py:308
  52.3 3.6 %collective-permute-start.9 = (f32[4,128]{1,0:T(4,128)S(1)}, f32[4,128]{1,0:T(4,128)S(1)}, u32[]{:S(2)}, u32[]{:S(2)}) collective-permute-start(f32[4,128]{1,0:T(4,128)S(1)} %bitcast.53), channel_id=1, source_target_pairs={{0,2},{1,3},{2,0},{3,1},{4,6},{5,7},{6,4},{7,5},{8,10},{9,11},{10,... | collective-permute-start | bytes 6152 | tf_op jit(solution)/shard_map/ppermute | solution.py:308
  55.9 3.6 %collective-permute-start.10 = (f32[2,128]{1,0:T(2,128)S(1)}, f32[2,128]{1,0:T(2,128)S(1)}, u32[]{:S(2)}, u32[]{:S(2)}) collective-permute-start(f32[2,128]{1,0:T(2,128)S(1)} %bitcast.54), channel_id=1, source_target_pairs={{0,4},{1,5},{2,6},{3,7},{4,0},{5,1},{6,2},{7,3},{8,12},{9,13},{10,... | collective-permute-start | bytes 3080 | tf_op jit(solution)/shard_map/ppermute | solution.py:308
  59.6 4.5 %collective-permute-start.11 = (f32[1,128]{1,0:T(1,128)S(1)}, f32[1,128]{1,0:T(1,128)S(1)}, u32[]{:S(2)}, u32[]{:S(2)}) collective-permute-start(f32[1,128]{1,0:T(1,128)S(1)} %fusion.6), channel_id=1, source_target_pairs={{0,8},{1,9},{2,10},{3,11},{4,12},{5,13},{6,14},{7,15},{8,0},{9,1},... | collective-permute-start | bytes 1544 | tf_op jit(solution)/shard_map/ppermute | solution.py:308

commit v2 on v0

v2 whole, which is shorter than its diff:
```python
import functools
import math

import jax
import jax.numpy as jnp
from jax import lax
from jax.experimental import pallas as pl
from jax.experimental.pallas import tpu as pltpu
from jax.sharding import PartitionSpec as P

STEPS = 5
COURANT = 0.5
ANGULAR = 0.3
SENS_SCALE = 0.05
X, Y, Z = 0, 1, 2
VMEM = pl.BlockSpec(memory_space=pltpu.VMEM)
SMEM = pl.BlockSpec(memory_space=pltpu.SMEM)


def shifted(field, axis, ahead):
    size = field.shape[axis]
    where = lax.broadcasted_iota(jnp.int32, field.shape, axis)
    if ahead:
        return jnp.where(where == size - 1, 0.0, pltpu.roll(field, size - 1, axis))
    return jnp.where(where == 0, 0.0, pltpu.roll(field, 1, axis))


def magnetic_plane(elec, beyond, mag):
    ex, ey, ez = elec
    curl_x = shifted(ez, 0, True) - ez - (shifted(ey, 1, True) - ey)
    far_y, far_z = beyond if beyond is not None else (0.0, 0.0)
    curl_y = shifted(ex, 1, True) - ex - (far_z - ez)
    curl_z = far_y - ey - (shifted(ex, 0, True) - ex)
    return [
        None if m is None else m - COURANT * c
        for m, c in zip(mag, (curl_x, curl_y, curl_z))
    ]


def electric_plane(mag, before, elec, eps):
    hx, hy, hz = mag
    past_y, past_z = before if before is not None else (0.0, 0.0)
    rot_x = hz - shifted(hz, 0, False) - (hy - shifted(hy, 1, False))
    rot_y = hx - shifted(hx, 1, False) - (hz - past_z)
    rot_z = hy - past_y - (hx - shifted(hx, 0, False))
    half = COURANT * eps
    return [e + half * r for e, r in zip(elec, (rot_x, rot_y, rot_z))]


def planes(ref, p):
    return [ref[c, p] for c in range(3)]


def store(ref, p, values):
    for c, v in enumerate(values):
        ref[c, p] = v


def magnetic_all(elec, mag, count, beyond):
    for p in range(count):
        far = (elec[Y, p + 1], elec[Z, p + 1]) if p + 1 < count else beyond
        store(mag, p, magnetic_plane(planes(elec, p), far, planes(mag, p)))


def electric_all(elec, mag, eps, count, before):
    for p in range(count):
        past = (mag[Y, p - 1], mag[Z, p - 1]) if p else before
        store(elec, p, electric_plane(planes(mag, p), past, planes(elec, p), eps[p]))


WINDOW = 42
LOW = 43


def turned(plane, by):
    return pltpu.roll(plane, by % plane.shape[1], 1)


def packed(a, b, c):
    lane = lax.broadcasted_iota(jnp.int32, a.shape, 1)
    last = jnp.where(lane < LOW + 2 * WINDOW, turned(b, WINDOW), turned(c, WINDOW))
    core = jnp.where(
        lane < LOW, turned(c, -WINDOW), jnp.where(lane < LOW + WINDOW, a, last)
    )
    inside = jnp.logical_and(lane >= LOW, lane < LOW + WINDOW)
    rest_a = jnp.where(inside, turned(c, LOW), a)
    rest_b = jnp.where(inside, turned(c, -LOW), b)
    return core, rest_a, rest_b


def unpacked(core, rests):
    b = turned(core, -WINDOW)
    c = turned(core, WINDOW)
    if rests is None:
        return core, b, c
    rest_a, rest_b = rests
    lane = lax.broadcasted_iota(jnp.int32, core.shape, 1)
    inside = jnp.logical_and(lane >= LOW, lane < LOW + WINDOW)
    end = LOW + WINDOW
    outer = jnp.where(lane == end, b, turned(rest_b, LOW))
    c = jnp.where(lane < LOW - 1, turned(rest_a, -LOW), jnp.where(lane < end, c, outer))
    return jnp.where(inside, core, rest_a), jnp.where(inside, b, rest_b), c


def opening_kernel(role, first_y, first_z, last_e, last_hy, last_hz, eps, msg):
    even = role[0] == 0

    @pl.when(even)
    def _():
        for k, v in enumerate(packed(first_y[0, 0], first_z[0, 0], eps[0])):
            msg[k] = v

    @pl.when(jnp.logical_not(even))
    def _():
        mid = magnetic_plane(planes(last_e, 0), None, (None, last_hy[0, 0], last_hz[0, 0]))[1:]
        for k, v in enumerate(packed(*mid, eps[0])):
            msg[k] = v


def needed(wanted_mag, wanted_elec, count):
    mag, elec = dict(wanted_mag), dict(wanted_elec)
    for step in range(STEPS, 0, -1):
        elec[step] = set(elec.get(step, ()))
        mag[step] = set(mag.get(step, ()))
        mag[step] |= elec[step] | {p - 1 for p in elec[step] if p}
        elec[step - 1] = set(elec.get(step - 1, ())) | elec[step] | mag[step]
        elec[step - 1] |= {p + 1 for p in mag[step] if p + 1 < count}
        mag[step - 1] = set(mag.get(step - 1, ())) | mag[step]
    return mag, elec


def closed_kernel(role, own_e, own_m, own_eps, mate_e, mate_m, mate_eps, core_msg, rest_msg, nears, elec, mag, raw):
    half = own_e.shape[1]
    count = 2 * half
    even = role[0] == 0
    spot = {2: (0, 1), 3: (3, 4), 4: (5, 6), 5: (7, 8)}

    def run(is_even):
        steps = range(1, STEPS + 1)
        if is_even:
            raw[2] = own_eps[1]
            want_m, want_e = {}, {s: {0, half} for s in steps if s < STEPS}
        else:
            raw[2] = own_eps[half - 2]
            want_m, want_e = {s: {half - 1, count - 1} for s in steps}, {}
        need_m, need_e = needed(want_m, want_e, count)

        def first(own, mate, p):
            ref = own if (p < half) == is_even else mate
            return ref, p % half

        def all_of(step, pair, ref, p):
            if step > 1:
                return planes(ref, p)
            return planes(*first(*pair, p))

        def two_of(step, pair, ref, p):
            return tuple(all_of(step, pair, ref, p)[1:])

        pair_e, pair_m = (own_e, mate_e), (own_m, mate_m)
        if is_even:
            for k in range(2):
                nears[k] = mate_e[1 + k, 0]
        for step in steps:
            for p in sorted(need_m[step]):
                far = two_of(step, pair_e, elec, p + 1) if p + 1 < count else None
                here = all_of(step, pair_e, elec, p)
                new = magnetic_plane(here, far, all_of(step, pair_m, mag, p))
                store(mag, p, new)
                if not is_even and p == count - 1 and step > 1:
                    for k in range(2):
                        raw[spot[step][k]] = new[1 + k]
                if not is_even and p == half - 1:
                    nears[2 * (step - 1)] = new[Y] - COURANT * far[1]
                    nears[2 * (step - 1) + 1] = new[Z] + COURANT * far[0]
            for p in sorted(need_e[step]):
                past = (mag[Y, p - 1], mag[Z, p - 1]) if p else None
                ref, at = first(own_eps, mate_eps, p)
                new = electric_plane(planes(mag, p), past, all_of(step, pair_e, elec, p), ref[at])
                store(elec, p, new)
                if is_even and p == 0:
                    for k in range(2):
                        raw[spot[step + 1][k]] = new[1 + k]
                if is_even and p == half:
                    for k in range(2):
                        nears[2 * step + k] = new[1 + k]

    pl.when(even)(functools.partial(run, True))
    pl.when(jnp.logical_not(even))(functools.partial(run, False))
    for g in range(3):
        core, rest_a, rest_b = packed(raw[3 * g], raw[3 * g + 1], raw[3 * g + 2])
        core_msg[g] = core
        rest_msg[2 * g] = rest_a
        rest_msg[2 * g + 1] = rest_b


def past_near(near, elec):
    return (near[0] + COURANT * elec[Z, 0], near[1] - COURANT * elec[Y, 0])


def late_kernel(role, first_y, first_z, eps, opening, msg):
    even = role[0] == 0
    far = unpacked(opening[0], (opening[1], opening[2]))[:2]
    scale = jnp.where(even, role[1], role[2]).astype(jnp.float32)
    for p in range(eps.shape[0]):
        scale = scale * (COURANT * COURANT * eps[p])
    mine = jnp.where(even, COURANT, 0.0)
    msg[0] = scale * (far[0] + mine * first_z[0, 0])
    msg[1] = scale * (far[1] - mine * first_y[0, 0])


def weights_kernel(forward, accum, weights, base):
    depth, count, ny = forward.shape[1:]
    nz = weights.shape[3]
    blank = jnp.zeros(((nz - depth) // 2, ny), jnp.float32)
    for p in range(count):
        total = None
        for c in range(6):
            slab = forward[c, :, p, :] * (SENS_SCALE if c < 3 else -SENS_SCALE)
            w = jnp.transpose(jnp.concatenate([blank, slab, blank], 0))
            weights[c, p] = w
            term = w * accum[c, p]
            total = term if total is None else total + term
        base[p] = total


LEFT_MAG = {1: 1, 2: 2, 3: 3, 4: 2, 5: 1}
LEFT_ELEC = {1: 1, 2: 2, 3: 2, 4: 1, 5: 0}
RIGHT_MAG = {1: 0, 2: 1, 3: 2, 4: 1, 5: 0}
RIGHT_ELEC = {1: 1, 2: 2, 3: 2, 4: 1, 5: 0}


def beyond_left(step, elec, side_e, side_m):
    for j in range(LEFT_MAG[step]):
        if j == 0:
            far = (elec[Y, 0], elec[Z, 0])
        else:
            far = (side_e[Y, j - 1], side_e[Z, j - 1])
        store(side_m, j, magnetic_plane(planes(side_e, j), far, planes(side_m, j)))


def beyond_left_electric(step, side_e, side_m, side_eps):
    for j in range(LEFT_ELEC[step]):
        past = (side_m[Y, j + 1], side_m[Z, j + 1])
        store(side_e, j, electric_plane(planes(side_m, j), past, planes(side_e, j), side_eps[j]))


def beyond_right(step, mag, side_e, side_m, side_eps, last):
    for j in range(RIGHT_MAG[step]):
        far = (side_e[Y, j + 1], side_e[Z, j + 1])
        store(side_m, j, magnetic_plane(planes(side_e, j), far, planes(side_m, j)))
    for j in range(RIGHT_ELEC[step]):
        if j == 0:
            past = (mag[Y, last], mag[Z, last])
        else:
            past = (side_m[Y, j - 1], side_m[Z, j - 1])
        store(side_e, j, electric_plane(planes(side_m, j), past, planes(side_e, j), side_eps[j]))


def open_kernel(slab, role, elec_0, mag_0, eps, nears, late, *refs):
    if slab:
        opening, cores, weights, base, high, low, pillars, elec, mag, side_e, side_m, far = refs
    else:
        opening, cores, others, accum_0, elec, mag, accum, side_e, side_m, far = refs
    count = eps.shape[0]
    last = count - 1
    even = role[0] == 0
    side_e[...] = jnp.zeros_like(side_e)
    side_m[...] = jnp.zeros_like(side_m)
    spots = ((0, 1, 10), (2, 3, 11), (4, 5, 6), (7, 8, 9))
    for g, spot in enumerate(spots):
        if g == 0:
            core, rests = opening[0], (opening[1], opening[2])
        else:
            core = cores[g - 1]
            rests = None if slab else (others[2 * g - 2], others[2 * g - 1])
        for k, v in zip(spot, unpacked(core, rests)):
            far[k] = v
    side_eps = far.at[10:12]

    def run(is_even):
        totals = [base[p] for p in range(count)] if slab else None
        scale = role[1 if is_even else 2].astype(jnp.float32)
        for step in range(1, STEPS + 1):
            src_e, src_m = (elec_0, mag_0) if step == 1 else (elec, mag)
            at = 2 * (step - 1)
            near = (nears[at], nears[at + 1])
            if step == STEPS:
                near = (near[0] + late[0], near[1] + late[1])
            if is_even:
                beyond = near
                beyond_left(step, src_e, side_e, side_m)
                past0 = ((far[at] + side_m[Y, 0]) * scale, (far[at + 1] + side_m[Z, 0]) * scale)
            else:
                beyond = ((far[at] + side_e[Y, 0]) * scale, (far[at + 1] + side_e[Z, 0]) * scale)
                past0 = past_near(near, src_e)
            for p in range(count):
                nxt = (src_e[Y, p + 1], src_e[Z, p + 1]) if p < last else beyond
                store(mag, p, magnetic_plane(planes(src_e, p), nxt, planes(src_m, p)))
            if is_even:
                beyond_left_electric(step, side_e, side_m, side_eps)
            else:
                beyond_right(step, mag, side_e, side_m, side_eps, last)
            waves = (math.cos(ANGULAR * step), math.sin(ANGULAR * step))
            for p in range(count):
                past = (mag[Y, p - 1], mag[Z, p - 1]) if p else past0
                new = electric_plane(planes(mag, p), past, planes(src_e, p), eps[p])
                if not slab or step < STEPS:
                    store(elec, p, new)
                if slab:
                    for c in range(3):
                        mix = waves[0] * weights[c, p] + waves[1] * weights[3 + c, p]
                        totals[p] = totals[p] + mix * new[c]
                    continue
                src_a = accum_0 if step == 1 else accum
                for c in range(6):
                    accum[c, p] = src_a[c, p] + waves[c // 3] * new[c % 3]
        if not slab:
            return
        owners = pillars.shape[0]
        sums = None
        for p, total in enumerate(totals):
            row = lax.dot_general(
                jnp.ones((8, total.shape[1]), jnp.float32), total, (((1,), (1,)), ((), ())),
                precision=lax.Precision.HIGHEST, preferred_element_type=jnp.float32,
            )[0:1]
            label = lax.broadcasted_iota(jnp.int32, (owners, total.shape[0]), 0)
            spread = jnp.where(label == high[p : p + 1], row, 0.0)
            term = lax.dot_general(
                spread, low[p], (((1,), (0,)), ((), ())),
                precision=lax.Precision.HIGHEST, preferred_element_type=jnp.float32,
            )
            sums = term if sums is None else sums + term
        pillars[...] = sums

    pl.when(even)(functools.partial(run, True))
    pl.when(jnp.logical_not(even))(functools.partial(run, False))


def call(kernel, args, outs, scratch=(), smem=1):
    return pl.pallas_call(
        kernel,
        out_shape=[shape_of(*o) for o in outs],
        in_specs=[SMEM] * smem + [VMEM] * (len(args) - smem),
        out_specs=[VMEM] * len(outs),
        scratch_shapes=[pltpu.VMEM(d, jnp.float32) for d in scratch],
        compiler_params=pltpu.CompilerParams(vmem_limit_bytes=24 * 2**20),
        cost_estimate=pl.CostEstimate(flops=1, bytes_accessed=1, transcendentals=0),
    )(*args)


def opening_call(role, elec, mag, eps):
    _, count, ny, nz = elec.shape

    def plane(c, p):
        return pl.BlockSpec((1, 1, ny, nz), lambda i, role: (c, p, 0, 0))

    return pl.pallas_call(
        opening_kernel,
        out_shape=shape_of(3, ny, nz),
        grid_spec=pltpu.PrefetchScalarGridSpec(
            num_scalar_prefetch=1,
            grid=(1,),
            in_specs=[
                plane(Y, 0),
                plane(Z, 0),
                pl.BlockSpec((3, 1, ny, nz), lambda i, role: (0, count - 1, 0, 0)),
                plane(Y, count - 1),
                plane(Z, count - 1),
                pl.BlockSpec((1, ny, nz), lambda i, role: (role[0] * (count - 1), 0, 0)),
            ],
            out_specs=pl.BlockSpec((3, ny, nz), lambda i, role: (0, 0, 0)),
        ),
        compiler_params=pltpu.CompilerParams(vmem_limit_bytes=8 * 2**20),
        cost_estimate=pl.CostEstimate(flops=1, bytes_accessed=1, transcendentals=0),
    )(role, *(pltpu.with_memory_space_constraint(a, pltpu.HBM) for a in (elec, elec, elec, mag, mag, eps)))


def late_call(role, elec, eps, opening):
    _, count, ny, nz = elec.shape

    def plane(c):
        return pl.BlockSpec((1, 1, ny, nz), lambda i, role: (c, 0, 0, 0))

    return pl.pallas_call(
        late_kernel,
        out_shape=shape_of(2, ny, nz),
        grid_spec=pltpu.PrefetchScalarGridSpec(
            num_scalar_prefetch=1,
            grid=(1,),
            in_specs=[
                plane(Y),
                plane(Z),
                pl.BlockSpec((count, ny, nz), lambda i, role: (0, 0, 0)),
                pl.BlockSpec((3, ny, nz), lambda i, role: (0, 0, 0)),
            ],
            out_specs=pl.BlockSpec((2, ny, nz), lambda i, role: (0, 0, 0)),
        ),
        compiler_params=pltpu.CompilerParams(vmem_limit_bytes=8 * 2**20),
        cost_estimate=pl.CostEstimate(flops=1, bytes_accessed=1, transcendentals=0),
    )(role, elec, elec, eps, opening)


def shape_of(*dims):
    return jax.ShapeDtypeStruct(dims, jnp.float32)


def halved(sums, axis):
    size = lax.axis_size(axis)
    me = lax.axis_index(axis)
    bits = size.bit_length() - 1
    block = sums
    for bit in range(bits):
        pair = block.reshape(-1, 2, block.shape[-1])
        mine = (me >> bit) & 1
        keep = jnp.where(mine == 0, pair[:, 0], pair[:, 1])
        give = jnp.where(mine == 0, pair[:, 1], pair[:, 0])
        block = keep + lax.ppermute(give, axis, [(i, i ^ (1 << bit)) for i in range(size)])
    return block.reshape(-1)


def per_device(electric, magnetic, inv_eps, accum, forward, pillar_ids):
    size = lax.axis_size("gx")
    me = lax.axis_index("gx")
    role = jnp.stack([me % 2, jnp.where(me == 0, 0, 1), jnp.where(me == size - 1, 0, 1)]).astype(jnp.int32)
    count, ny, nz = inv_eps.shape
    same_chip = [(i, i ^ 1) for i in range(size)]
    inner = range(1, size - 1, 2)
    next_chip = [(i, i + 1) for i in inner] + [(i + 1, i) for i in inner]

    per_owner = ny
    high = pillar_ids // per_owner
    low = (pillar_ids % per_owner)[:, :, None] == jnp.arange(per_owner, dtype=jnp.int32)
    low = low.astype(jnp.float32)
    field, side = electric.shape, (3, 3, ny, nz)

    def to_mate(block):
        return lax.ppermute(block, "gx", same_chip)

    def to_chip(block):
        return lax.ppermute(block, "gx", next_chip)

    opening = to_chip(opening_call(role, electric, magnetic, inv_eps))
    fixed = [role, electric, magnetic, inv_eps]
    mate = [to_mate(electric), to_mate(magnetic), to_mate(inv_eps)]
    cores, others, nears = call(
        closed_kernel,
        fixed + mate,
        [(3, ny, nz), (6, ny, nz), (2 * STEPS, ny, nz)],
        scratch=[(3, 2 * count, ny, nz)] * 2 + [(9, ny, nz)],
    )
    cores = to_chip(cores)
    opening, nears = lax.optimization_barrier((opening, nears))
    late = to_mate(late_call(role, electric, inv_eps, opening))
    cores, others = lax.optimization_barrier((cores, others))
    others = to_chip(others)
    weights, base = call(weights_kernel, [forward, accum], [accum.shape, inv_eps.shape], smem=0)
    scratch = [side, side, (12, ny, nz)]
    def pillar_sums(args):
        (sums,) = call(
            functools.partial(open_kernel, True),
            args,
            [(size, per_owner)],
            scratch=[field, field] + scratch,
        )
        return halved(sums, "gx")

    grads = lax.cond(
        role[1] < 2,
        pillar_sums,
        lambda args: jnp.zeros((per_owner,), jnp.float32),
        fixed + [nears, late, opening, cores, weights, base, high, low],
    )
    electric, magnetic, accum = call(
        functools.partial(open_kernel, False),
        fixed + [nears, late, opening, cores, others, accum],
        [field, field, accum.shape],
        scratch=scratch,
    )
    return electric, magnetic, accum, grads


def solution(mesh):
    return jax.shard_map(
        per_device,
        mesh=mesh,
        in_specs=(
            P(None, ("design", "gx"), None, None),
            P(None, ("design", "gx"), None, None),
            P(("design", "gx"), None, None),
            P(None, ("design", "gx"), None, None),
            P(None, None, ("design", "gx"), None),
            P("gx", None),
        ),
        out_specs=(
            P(None, ("design", "gx"), None, None),
            P(None, ("design", "gx"), None, None),
            P(None, ("design", "gx"), None, None),
            P(("design", "gx")),
        ),
        check_vma=False,
    )
```

time: 107 us -> 63.3 us (0.59)
  blocking collectives: 31.8 us -> 0 us
  Pallas kernels: 0 us -> 24.3 us
  starting transfers between devices: 36.8 us -> 23.9 us
  local copies, waits for them, and re-layouts: 11 us -> 1.28 us
  waiting for transfers between devices: 15.8 us -> 6.21 us
  matrix products: 1.92 us -> 0 us
  between operations: 2.04 us -> 0.68 us
    unnamed x1 -> x0, blocking collectives: 31.8 us -> none
    pallas_call x0 -> x6, Pallas kernels: none -> 24.3 us  [the longest x4 20.1 us: call(): pl.pallas_call(kernel, out_shape=[shape_of(*o) for o in outs], in_specs=[...]
    ppermute x10 -> x11, starting transfers between devices: 36.8 us -> 23.9 us  [the longest x4 11.8 us: to_mate(): return lax.ppermute(block, 'gx', same_chip)]
    ppermute x10 -> x11, waiting for transfers between devices: 15.8 us -> 6.21 us  [the longest x4 5.79 us: halved(): lax.ppermute(give, axis, [(i, i ^ 1 << bit) for i in range(size)])]
    unnamed x25 -> x12, local copies, waits for them, and re-layouts: 5.02 us -> 0.69 us
    slice x40 -> x1, local copies, waits for them, and re-layouts: 4.27 us -> 0.01 us  [halved(): keep = jnp.where(mine == 0, pair[:, 0], pair[:, 1])]
    another operation x10 -> x1, other arithmetic: 3.72 us -> 0.08 us  [per_device(): jnp.stack([me % 2, jnp.where(me == 0, 0, 1), jnp.where(me == size - 1, 0,...]
    dot_general x1 -> x0, matrix products: 1.92 us -> none  [owner_terms(): jnp.dot(onehot, flat_sens, precision=lax.Precision.HIGHEST, preferred_ele...]
  transfers between devices with their start and end apart: 10 -> 11, of which waited for: 9 -> 5; matrix products, arithmetic and copies ran while one was open for 4% -> 10% of each run, Pallas kernels for 0% -> 28%
where the time goes in v2:
time: 63.3 us; the launch traced here: 62.9 us
  Pallas kernels  24.3 us (38%)
  starting transfers between devices  23.9 us (38%)
  other arithmetic  6.44 us (10%)
  waiting for transfers between devices  6.21 us (10%)
  local copies, waits for them, and re-layouts  1.28 us (2%)
  between operations  0.68 us (1%)
    pallas_call x4, Pallas kernels, call(): pl.pallas_call(kernel, out_shape=[shape_of(*o) for o in outs], in_specs=[...  20.1 us
    ppermute x4, starting transfers between devices, to_mate(): return lax.ppermute(block, 'gx', same_chip)  11.8 us
    ppermute x4, starting transfers between devices, halved(): lax.ppermute(give, axis, [(i, i ^ 1 << bit) for i in range(size)])  9.31 us
    ppermute x4, waiting for transfers between devices, halved(): lax.ppermute(give, axis, [(i, i ^ 1 << bit) for i in range(size)])  5.79 us
    ppermute x3, starting transfers between devices, to_chip(): return lax.ppermute(block, 'gx', next_chip)  2.8 us
    pallas_call x1, Pallas kernels, opening_call(): pl.pallas_call(opening_kernel, out_shape=shape_of(3, ny, nz), grid_spec=p...  2.49 us
    pallas_call x1, Pallas kernels, late_call(): pl.pallas_call(late_kernel, out_shape=shape_of(2, ny, nz), grid_spec=pltp...  1.7 us
    add x2, other arithmetic, halved(): keep + lax.ppermute(give, axis, [(i, i ^ 1 << bit) for i in range(size)])  1.37 us
  transfers between devices with their start and end apart: 11, of which 5 were waited for; matrix products, arithmetic and copies ran while one was open for 10% of the time, Pallas kernels for 28%

profile of v2, /device:TPU:0, one launch (start us, length us, event | category | flops | bytes accessed | tf_op | source)
XLA Modules:
  0.0 62.9 jit_solution(9061909387030746439)
XLA Ops:
  0.6 0.5 collective-permute-start.6
  1.1 0.1 collective-permute-start.5
  1.2 0.4 collective-permute-start.7
  1.7 0.1 pad_add_fusion.role
  1.7 0.0 copy-start.1
  1.7 2.5 %shard_map.93 = f32[3,128,128]{2,1,0:T(8,128)} custom-call(s32[3]{0:T(128)S(1)} %pad_add_fusion.role, f32[3,4,128,128]{3,2,1,0:T(8,128)} %elec_0.1, f32[3,4,128,128]{3,2,1,0:T(8,128)} %elec_0.1, f32[3,4,128,128]{3,2,1,0:T(8,128)} %elec_0.1, f32[3,4,128,128]{3,2,1,0:T(8,128)} %mag_0.1, f32[3,4,128,128]{3,2,1,0:T(8,128)} %mag_0.1, f32[4,128,128]{2,1,0:T(8,128)} %eps.5), custom_call_target="tpu_custom_call" | custom-call | flops 1 | bytes 1 | tf_op jit(solution)/shard_map/pallas_call | solution.py:358
  4.2 1.3 %collective-permute-start.4 = (f32[3,128,128]{2,1,0:T(8,128)}, f32[3,128,128]{2,1,0:T(8,128)}, u32[]{:S(2)}, u32[]{:S(2)}) collective-permute-start(f32[3,128,128]{2,1,0:T(8,128)} %shard_map.93), channel_id=1, source_target_pairs={{1,2},{3,4},{5,6},{7,8},{9,10},{11,12},{13,14},{2,1},{4,3},{6,5},{... | collective-permute-start | bytes 589832 | tf_op jit(solution)/shard_map/ppermute | solution.py:441
  5.6 0.0 copy-done
  5.6 0.0 copy-done.1
  5.6 1.7 %shard_map.97 = (f32[6,4,128,128]{3,2,1,0:T(8,128)}, f32[4,128,128]{2,1,0:T(8,128)}) custom-call(f32[6,32,4,128]{3,2,1,0:T(4,128)S(1)} %copy-done.1, f32[6,4,128,128]{3,2,1,0:T(8,128)S(1)} %copy-done), custom_call_target="tpu_custom_call" | custom-call | flops 1 | bytes 1 | tf_op jit(solution)/shard_map/pallas_call | solution.py:341
  7.3 0.0 collective-permute-done.7.mate_eps
  7.3 0.0 collective-permute-done.6.mate_m
  7.3 0.0 collective-permute-done.5.mate_e
  7.3 5.1 %shard_map.94 = (f32[3,128,128]{2,1,0:T(8,128)S(1)}, f32[6,128,128]{2,1,0:T(8,128)}, f32[10,128,128]{2,1,0:T(8,128)}) custom-call(s32[3]{0:T(128)S(1)} %pad_add_fusion.role, f32[3,4,128,128]{3,2,1,0:T(8,128)} %elec_0.1, f32[3,4,128,128]{3,2,1,0:T(8,128)} %mag_0.1, f32[4,128,128]{2,1,0:T(8,128)} %eps.5, f32[3,4,128,128]{3,2,1,0:T(8,128)S(1)} %collective-permute-done.5.mate_e, ...), custom_call_target="tpu_custom_call" | custom-call | flops 1 | bytes 1 | tf_op jit(solution)/shard_map/pallas_call | solution.py:341
  12.4 0.8 %collective-permute-start.9 = (f32[3,128,128]{2,1,0:T(8,128)S(1)}, f32[3,128,128]{2,1,0:T(8,128)S(1)}, u32[]{:S(2)}, u32[]{:S(2)}) collective-permute-start(f32[3,128,128]{2,1,0:T(8,128)S(1)} %get-tuple-element.91), channel_id=1, source_target_pairs={{1,2},{3,4},{5,6},{7,8},{9,10},{11,12},{13,14},{2,1},{4,3},{6,5},{... | collective-permute-start | bytes 589832 | tf_op jit(solution)/shard_map/ppermute | solution.py:441
  13.2 0.0 copy-done.5
  13.2 0.5 add_select_fusion.1
  13.7 0.0 collective-permute-done.9.refs_1_
  13.7 0.7 %copy-done.4 = f32[3,128,128]{2,1,0:T(8,128)} copy-done((f32[3,128,128]{2,1,0:T(8,128)}, f32[3,128,128]{2,1,0:T(8,128)S(1)}, u32[]{:S(2)}) %copy-start.4) | copy-done | bytes 196632
  14.4 0.7 %collective-permute-start.10 = (f32[6,128,128]{2,1,0:T(8,128)}, f32[6,128,128]{2,1,0:T(8,128)S(1)}, u32[]{:S(2)}, u32[]{:S(2)}) collective-permute-start(f32[6,128,128]{2,1,0:T(8,128)} %get-tuple-element.94), channel_id=1, source_target_pairs={{1,2},{3,4},{5,6},{7,8},{9,10},{11,12},{13,14},{2,1},{4,3},{6,5},{... | collective-permute-start | bytes 1179656 | tf_op jit(solution)/shard_map/ppermute | solution.py:441
  15.1 0.8 %fusion.7 = f32[4,128,128]{2,1,0:T(8,128)} fusion(s32[4,128]{1,0:T(4,128)S(1)} %get-tuple-element.100), kind=kLoop, calls=%fused_computation.20 | loop fusion | flops 131072 | bytes 264192 | tf_op jit(solution)/shard_map/convert_element_type | solution.py:434
  15.9 0.0 collective-permute-done.4.opening.refs_0_
  15.9 1.7 %shard_map.95 = f32[2,128,128]{2,1,0:T(8,128)S(1)} custom-call(s32[3]{0:T(128)S(1)} %pad_add_fusion.role, f32[3,4,128,128]{3,2,1,0:T(8,128)} %elec_0.1, f32[3,4,128,128]{3,2,1,0:T(8,128)} %elec_0.1, f32[4,128,128]{2,1,0:T(8,128)} %eps.5, f32[3,128,128]{2,1,0:T(8,128)} %collective-permute-done.4.opening.refs_0_), custom_call_target="tpu_custom_call" | custom-call | flops 1 | bytes 1 | tf_op jit(solution)/shard_map/pallas_call | solution.py:385
  17.6 10.8 %collective-permute-start.8 = (f32[2,128,128]{2,1,0:T(8,128)S(1)}, f32[2,128,128]{2,1,0:T(8,128)S(1)}, u32[]{:S(2)}, u32[]{:S(2)}) collective-permute-start(f32[2,128,128]{2,1,0:T(8,128)S(1)} %shard_map.95), channel_id=1, source_target_pairs={{0,1},{1,0},{2,3},{3,2},{4,5},{5,4},{6,7},{7,6},{8,9},{9,8},{10,11... | collective-permute-start | bytes 393224 | tf_op jit(solution)/shard_map/ppermute | solution.py:438
  28.4 0.6 broadcast_and_fusion
  29.0 0.4 collective-permute-done.8.late
  29.4 0.0 copy-done.2
  29.4 0.0 copy-done.3
  29.4 26.6 %conditional.1 = (f32[128]{0:T(128)}) conditional(s32[]{:T(128)} %convert_element_type.6, () %tuple.21, (s32[4,128]{1,0:T(4,128)S(1)}, s32[4,128]{1,0:T(4,128)}, pred[4,128]{1,0:T(4,128)(4,1)}, s32[4,128]{1,0:T(4,128)S(1)}, s32[4,128]{1,0:T(4,128)S(1)}, /*index=5*/s32[3]{0:T(128)S(1)}, f32[3,4,128,128]{3,2,1,0:T(8,128)}, ...), branch_computations={%region_0.1_spmd, %region_1.2_spmd} | conditional | flops 11407 | bytes 126309 | solution.py:468
  29.4 0.7 %add_select_fusion.refs_4_ = s32[4,128]{1,0:T(4,128)S(1)} fusion(pred[4,128]{1,0:T(4,128)(4,1)} %get-tuple-element.67, s32[4,128]{1,0:T(4,128)S(1)} %get-tuple-element.70, s32[4,128]{1,0:T(4,128)S(1)} %get-tuple-element.66, s32[4,128]{1,0:T(4,128)S(1)} %get-tuple-element.69, s32[4,128]{1,0:T(4,128)} %get-tuple-element.68), kind=kLoop, calls=%fused_computation.3 | loop fusion | flops 5632 | bytes 10752 | tf_op jit(solution)/shard_map/jit(floor_divide)/jit(_where)/select_n | solution.py:432
  30.1 6.5 %branch_1_fun.1 = f32[16,128]{1,0:T(8,128)S(1)} custom-call(s32[3]{0:T(128)S(1)} %get-tuple-element.56.role, f32[3,4,128,128]{3,2,1,0:T(8,128)} %get-tuple-element.57.elec_0, f32[3,4,128,128]{3,2,1,0:T(8,128)S(1)} %get-tuple-element.58.mag_0, f32[4,128,128]{2,1,0:T(8,128)} %get-tuple-element.59.eps, f32[10,128,128]{2,1,0:T(8,128)S(1)} %get-tuple-element.60.nears, ...), custom_call_target="tpu_custom_call" | custom-call | flops 1 | bytes 1 | tf_op jit(solution)/shard_map/cond/branch_1_fun/pallas_call | solution.py:341
  36.6 0.4 collective-permute-start
  37.0 1.0 %collective-permute-done = f32[8,128]{1,0:T(8,128)} collective-permute-done((f32[8,128]{1,0:T(8,128)S(1)}, f32[8,128]{1,0:T(8,128)}, u32[]{:S(2)}, u32[]{:S(2)}) %collective-permute-start) | collective-permute-done | bytes 4128 | tf_op jit(solution)/shard_map/cond/branch_1_fun/ppermute | solution.py:418
  38.0 0.7 %bitcast_add_fusion = f32[8,128]{1,0:T(8,128)S(1)} fusion(f32[8,128]{1,0:T(8,128)} %collective-permute-done, f32[8,1,128]{2,0,1:T(8,128)S(1)} %bitcast.42, f32[8,1,128]{2,0,1:T(8,128)S(1)} %bitcast.44, pred[]{:T(512)S(6)} %eq.7), kind=kLoop, calls=%fused_computation | loop fusion | flops 2048 | bytes 16385 | tf_op jit(solution)/shard_map/cond/branch_1_fun/add | solution.py:418
  38.7 0.6 fusion.9
  39.3 3.5 %collective-permute-start.1 = (f32[4,128]{1,0:T(4,128)}, f32[4,128]{1,0:T(4,128)S(1)}, u32[]{:S(2)}, u32[]{:S(2)}) collective-permute-start(f32[4,128]{1,0:T(4,128)} %bitcast.7), channel_id=1, source_target_pairs={{0,2},{1,3},{2,0},{3,1},{4,6},{5,7},{6,4},{7,5},{8,10},{9,11},{10,... | collective-permute-start | bytes 6152 | tf_op jit(solution)/shard_map/cond/branch_1_fun/ppermute | solution.py:418
  42.8 1.8 %collective-permute-done.1 = f32[4,128]{1,0:T(4,128)S(1)} collective-permute-done((f32[4,128]{1,0:T(4,128)}, f32[4,128]{1,0:T(4,128)S(1)}, u32[]{:S(2)}, u32[]{:S(2)}) %collective-permute-start.1) | collective-permute-done | bytes 2080 | tf_op jit(solution)/shard_map/cond/branch_1_fun/ppermute | solution.py:418
  44.6 0.6 copy-done.6
  45.1 0.7 %bitcast_add_fusion.1 = f32[4,128]{1,0:T(4,128)S(1)} fusion(f32[4,128]{1,0:T(4,128)} %copy-done.6, f32[4,1,128]{2,0,1:T(4,128)S(1)} %bitcast.47, f32[4,1,128]{2,0,1:T(4,128)S(1)} %bitcast.46, pred[]{:T(512)S(6)} %eq.6), kind=kLoop, calls=%fused_computation.7 | loop fusion | flops 1024 | bytes 8193 | tf_op jit(solution)/shard_map/cond/branch_1_fun/add | solution.py:418
  45.8 0.6 fusion.10
  46.4 2.3 %collective-permute-start.2 = (f32[2,128]{1,0:T(2,128)S(1)}, f32[2,128]{1,0:T(2,128)S(1)}, u32[]{:S(2)}, u32[]{:S(2)}) collective-permute-start(f32[2,128]{1,0:T(2,128)S(1)} %bitcast.51), channel_id=1, source_target_pairs={{0,4},{1,5},{2,6},{3,7},{4,0},{5,1},{6,2},{7,3},{8,12},{9,13},{10,... | collective-permute-start | bytes 3080 | tf_op jit(solution)/shard_map/cond/branch_1_fun/ppermute | solution.py:418
  48.7 1.5 %collective-permute-done.2 = f32[2,128]{1,0:T(2,128)S(1)} collective-permute-done((f32[2,128]{1,0:T(2,128)S(1)}, f32[2,128]{1,0:T(2,128)S(1)}, u32[]{:S(2)}, u32[]{:S(2)}) %collective-permute-start.2) | collective-permute-done | bytes 1056 | tf_op jit(solution)/shard_map/cond/branch_1_fun/ppermute | solution.py:418
  50.3 0.7 %fusion.2 = f32[1,2,128]{2,1,0:T(2,128)S(1)} fusion(f32[2,128]{1,0:T(2,128)S(1)} %collective-permute-done.2, f32[2,1,128]{2,0,1:T(2,128)} %bitcast.50, f32[2,1,128]{2,0,1:T(2,128)S(1)} %bitcast.49, pred[]{:T(512)S(6)} %eq.4), kind=kLoop, calls=%fused_computation.12 | loop fusion | flops 512 | bytes 4097 | tf_op jit(solution)/shard_map/cond/branch_1_fun/reshape | solution.py:414
  51.0 3.0 %collective-permute-start.3 = (f32[1,128]{1,0:T(1,128)S(1)}, f32[1,128]{1,0:T(1,128)S(1)}, u32[]{:S(2)}, u32[]{:S(2)}) collective-permute-start(f32[1,128]{1,0:T(1,128)S(1)} %fusion.6), channel_id=1, source_target_pairs={{0,8},{1,9},{2,10},{3,11},{4,12},{5,13},{6,14},{7,15},{8,0},{9,1},... | collective-permute-start | bytes 1544 | tf_op jit(solution)/shard_map/cond/branch_1_fun/ppermute | solution.py:418
  54.0 1.5 %collective-permute-done.3 = f32[1,128]{1,0:T(1,128)S(1)} collective-permute-done((f32[1,128]{1,0:T(1,128)S(1)}, f32[1,128]{1,0:T(1,128)S(1)}, u32[]{:S(2)}, u32[]{:S(2)}) %collective-permute-start.3) | collective-permute-done | bytes 544 | tf_op jit(solution)/shard_map/cond/branch_1_fun/ppermute | solution.py:418
  55.5 0.5 fusion.5
  56.0 0.0 collective-permute-done.10.refs_2_
  56.1 6.8 %shard_map.96 = (f32[3,4,128,128]{3,2,1,0:T(8,128)}, f32[3,4,128,128]{3,2,1,0:T(8,128)}, f32[6,4,128,128]{3,2,1,0:T(8,128)}) custom-call(s32[3]{0:T(128)S(1)} %pad_add_fusion.role, f32[3,4,128,128]{3,2,1,0:T(8,128)} %elec_0.1, f32[3,4,128,128]{3,2,1,0:T(8,128)S(1)} %copy-done.2, f32[4,128,128]{2,1,0:T(8,128)} %eps.5, f32[10,128,128]{2,1,0:T(8,128)S(1)} %copy-done.3, ...), custom_call_target="tpu_custom_call" | custom-call | flops 1 | bytes 1 | tf_op jit(solution)/shard_map/pallas_call | solution.py:341
  (10 shorter events, 0.0 us)
Async XLA Ops:
  0.6 6.7 %collective-permute-start.6 = (f32[3,4,128,128]{3,2,1,0:T(8,128)}, f32[3,4,128,128]{3,2,1,0:T(8,128)S(1)}, u32[]{:S(2)}, u32[]{:S(2)}) collective-permute-start(f32[3,4,128,128]{3,2,1,0:T(8,128)} %mag_0.1), channel_id=1, source_target_pairs={{0,1},{1,0},{2,3},{3,2},{4,5},{5,4},{6,7},{7,6},{8,9},{9,8},{10,11... | collective-permute-start | bytes 2359304 | tf_op jit(solution)/shard_map/ppermute | solution.py:438
  1.1 6.1 %collective-permute-start.5 = (f32[3,4,128,128]{3,2,1,0:T(8,128)}, f32[3,4,128,128]{3,2,1,0:T(8,128)S(1)}, u32[]{:S(2)}, u32[]{:S(2)}) collective-permute-start(f32[3,4,128,128]{3,2,1,0:T(8,128)} %elec_0.1), channel_id=1, source_target_pairs={{0,1},{1,0},{2,3},{3,2},{4,5},{5,4},{6,7},{7,6},{8,9},{9,8},{10,11... | collective-permute-start | bytes 2359304 | tf_op jit(solution)/shard_map/ppermute | solution.py:438
  1.2 6.1 %collective-permute-start.7 = (f32[4,128,128]{2,1,0:T(8,128)}, f32[4,128,128]{2,1,0:T(8,128)S(1)}, u32[]{:S(2)}, u32[]{:S(2)}) collective-permute-start(f32[4,128,128]{2,1,0:T(8,128)} %eps.5), channel_id=1, source_target_pairs={{0,1},{1,0},{2,3},{3,2},{4,5},{5,4},{6,7},{7,6},{8,9},{9,8},{10,11... | collective-permute-start | bytes 786440 | tf_op jit(solution)/shard_map/ppermute | solution.py:438
  1.7 3.8 %copy-start = (f32[6,4,128,128]{3,2,1,0:T(8,128)S(1)}, f32[6,4,128,128]{3,2,1,0:T(8,128)}, u32[]{:S(2)}) copy-start(f32[6,4,128,128]{3,2,1,0:T(8,128)} %accum.1) | copy-start | bytes 4718596
  1.7 3.8 %copy-start.1 = (f32[6,32,4,128]{3,2,1,0:T(4,128)S(1)}, f32[6,32,4,128]{3,2,1,0:T(4,128)}, u32[]{:S(2)}) copy-start(f32[6,32,4,128]{3,2,1,0:T(4,128)} %forward.1) | copy-start | bytes 1179652
  4.2 11.7 %collective-permute-start.4 = (f32[3,128,128]{2,1,0:T(8,128)}, f32[3,128,128]{2,1,0:T(8,128)}, u32[]{:S(2)}, u32[]{:S(2)}) collective-permute-start(f32[3,128,128]{2,1,0:T(8,128)} %shard_map.93), channel_id=1, source_target_pairs={{1,2},{3,4},{5,6},{7,8},{9,10},{11,12},{13,14},{2,1},{4,3},{6,5},{... | collective-permute-start | bytes 589832 | tf_op jit(solution)/shard_map/ppermute | solution.py:441
  7.3 5.9 %copy-start.5 = (s32[4,128]{1,0:T(4,128)S(1)}, s32[4,128]{1,0:T(4,128)}, u32[]{:S(2)}) copy-start(s32[4,128]{1,0:T(4,128)} %param.13) | copy-start | bytes 6148
  12.4 17.0 %copy-start.2 = (f32[3,4,128,128]{3,2,1,0:T(8,128)S(1)}, f32[3,4,128,128]{3,2,1,0:T(8,128)}, u32[]{:S(2)}) copy-start(f32[3,4,128,128]{3,2,1,0:T(8,128)} %mag_0.1) | copy-start | bytes 2359300
  12.4 17.0 %copy-start.3 = (f32[10,128,128]{2,1,0:T(8,128)S(1)}, f32[10,128,128]{2,1,0:T(8,128)}, u32[]{:S(2)}) copy-start(f32[10,128,128]{2,1,0:T(8,128)} %get-tuple-element.89.nears) | copy-start | bytes 1966084
  12.4 1.4 %collective-permute-start.9 = (f32[3,128,128]{2,1,0:T(8,128)S(1)}, f32[3,128,128]{2,1,0:T(8,128)S(1)}, u32[]{:S(2)}, u32[]{:S(2)}) collective-permute-start(f32[3,128,128]{2,1,0:T(8,128)S(1)} %get-tuple-element.91), channel_id=1, source_target_pairs={{1,2},{3,4},{5,6},{7,8},{9,10},{11,12},{13,14},{2,1},{4,3},{6,5},{... | collective-permute-start | bytes 589832 | tf_op jit(solution)/shard_map/ppermute | solution.py:441
  13.7 0.7 %copy-start.4 = (f32[3,128,128]{2,1,0:T(8,128)}, f32[3,128,128]{2,1,0:T(8,128)S(1)}, u32[]{:S(2)}) copy-start(f32[3,128,128]{2,1,0:T(8,128)S(1)} %collective-permute-done.9.refs_1_) | copy-start | bytes 589828
  14.4 41.6 %collective-permute-start.10 = (f32[6,128,128]{2,1,0:T(8,128)}, f32[6,128,128]{2,1,0:T(8,128)S(1)}, u32[]{:S(2)}, u32[]{:S(2)}) collective-permute-start(f32[6,128,128]{2,1,0:T(8,128)} %get-tuple-element.94), channel_id=1, source_target_pairs={{1,2},{3,4},{5,6},{7,8},{9,10},{11,12},{13,14},{2,1},{4,3},{6,5},{... | collective-permute-start | bytes 1179656 | tf_op jit(solution)/shard_map/ppermute | solution.py:441
  17.6 11.8 %collective-permute-start.8 = (f32[2,128,128]{2,1,0:T(8,128)S(1)}, f32[2,128,128]{2,1,0:T(8,128)S(1)}, u32[]{:S(2)}, u32[]{:S(2)}) collective-permute-start(f32[2,128,128]{2,1,0:T(8,128)S(1)} %shard_map.95), channel_id=1, source_target_pairs={{0,1},{1,0},{2,3},{3,2},{4,5},{5,4},{6,7},{7,6},{8,9},{9,8},{10,11... | collective-permute-start | bytes 393224 | tf_op jit(solution)/shard_map/ppermute | solution.py:438
  36.6 1.4 %collective-permute-start = (f32[8,128]{1,0:T(8,128)S(1)}, f32[8,128]{1,0:T(8,128)}, u32[]{:S(2)}, u32[]{:S(2)}) collective-permute-start(f32[8,128]{1,0:T(8,128)S(1)} %select_bitcast_fusion), channel_id=1, source_target_pairs={{0,1},{1,0},{2,3},{3,2},{4,5},{5,4},{6,7},{7,6},{8,9},{9,8},{10,11... | collective-permute-start | bytes 12296 | tf_op jit(solution)/shard_map/cond/branch_1_fun/ppermute | solution.py:418
  39.3 5.3 %collective-permute-start.1 = (f32[4,128]{1,0:T(4,128)}, f32[4,128]{1,0:T(4,128)S(1)}, u32[]{:S(2)}, u32[]{:S(2)}) collective-permute-start(f32[4,128]{1,0:T(4,128)} %bitcast.7), channel_id=1, source_target_pairs={{0,2},{1,3},{2,0},{3,1},{4,6},{5,7},{6,4},{7,5},{8,10},{9,11},{10,... | collective-permute-start | bytes 6152 | tf_op jit(solution)/shard_map/cond/branch_1_fun/ppermute | solution.py:418
  44.6 0.6 copy-start.6
  46.4 3.9 %collective-permute-start.2 = (f32[2,128]{1,0:T(2,128)S(1)}, f32[2,128]{1,0:T(2,128)S(1)}, u32[]{:S(2)}, u32[]{:S(2)}) collective-permute-start(f32[2,128]{1,0:T(2,128)S(1)} %bitcast.51), channel_id=1, source_target_pairs={{0,4},{1,5},{2,6},{3,7},{4,0},{5,1},{6,2},{7,3},{8,12},{9,13},{10,... | collective-permute-start | bytes 3080 | tf_op jit(solution)/shard_map/cond/branch_1_fun/ppermute | solution.py:418
  51.0 4.6 %collective-permute-start.3 = (f32[1,128]{1,0:T(1,128)S(1)}, f32[1,128]{1,0:T(1,128)S(1)}, u32[]{:S(2)}, u32[]{:S(2)}) collective-permute-start(f32[1,128]{1,0:T(1,128)S(1)} %fusion.6), channel_id=1, source_target_pairs={{0,8},{1,9},{2,10},{3,11},{4,12},{5,13},{6,14},{7,15},{8,0},{9,1},... | collective-permute-start | bytes 1544 | tf_op jit(solution)/shard_map/cond/branch_1_fun/ppermute | solution.py:418

commit v3 on v2

v3 whole, which is shorter than its diff:
```python
import functools
import math

import jax
import jax.numpy as jnp
from jax import lax
from jax.experimental import pallas as pl
from jax.experimental.pallas import tpu as pltpu
from jax.sharding import PartitionSpec as P

STEPS = 5
COURANT = 0.5
ANGULAR = 0.3
SENS_SCALE = 0.05
X, Y, Z = 0, 1, 2
VMEM = pl.BlockSpec(memory_space=pltpu.VMEM)
SMEM = pl.BlockSpec(memory_space=pltpu.SMEM)
HBM = pl.BlockSpec(memory_space=pltpu.HBM)


def shifted(field, axis, ahead):
    size = field.shape[axis]
    where = lax.broadcasted_iota(jnp.int32, field.shape, axis)
    if ahead:
        return jnp.where(where == size - 1, 0.0, pltpu.roll(field, size - 1, axis))
    return jnp.where(where == 0, 0.0, pltpu.roll(field, 1, axis))


def magnetic_plane(elec, beyond, mag):
    ex, ey, ez = elec
    curl_x = shifted(ez, 0, True) - ez - (shifted(ey, 1, True) - ey)
    far_y, far_z = beyond if beyond is not None else (0.0, 0.0)
    curl_y = shifted(ex, 1, True) - ex - (far_z - ez)
    curl_z = far_y - ey - (shifted(ex, 0, True) - ex)
    return [
        None if m is None else m - COURANT * c
        for m, c in zip(mag, (curl_x, curl_y, curl_z))
    ]


def electric_plane(mag, before, elec, eps):
    hx, hy, hz = mag
    past_y, past_z = before if before is not None else (0.0, 0.0)
    rot_x = hz - shifted(hz, 0, False) - (hy - shifted(hy, 1, False))
    rot_y = hx - shifted(hx, 1, False) - (hz - past_z)
    rot_z = hy - past_y - (hx - shifted(hx, 0, False))
    half = COURANT * eps
    return [e + half * r for e, r in zip(elec, (rot_x, rot_y, rot_z))]


def planes(ref, p):
    return [ref[c, p] for c in range(3)]


def store(ref, p, values):
    for c, v in enumerate(values):
        ref[c, p] = v


def magnetic_all(elec, mag, count, beyond):
    for p in range(count):
        far = (elec[Y, p + 1], elec[Z, p + 1]) if p + 1 < count else beyond
        store(mag, p, magnetic_plane(planes(elec, p), far, planes(mag, p)))


def electric_all(elec, mag, eps, count, before):
    for p in range(count):
        past = (mag[Y, p - 1], mag[Z, p - 1]) if p else before
        store(elec, p, electric_plane(planes(mag, p), past, planes(elec, p), eps[p]))


def needed(wanted_mag, wanted_elec, count):
    mag, elec = dict(wanted_mag), dict(wanted_elec)
    for step in range(STEPS, 0, -1):
        elec[step] = set(elec.get(step, ()))
        mag[step] = set(mag.get(step, ()))
        mag[step] |= elec[step] | {p - 1 for p in elec[step] if p}
        elec[step - 1] = set(elec.get(step - 1, ())) | elec[step] | mag[step]
        elec[step - 1] |= {p + 1 for p in mag[step] if p + 1 < count}
        mag[step - 1] = set(mag.get(step - 1, ())) | mag[step]
    return mag, elec


def early_kernel(role, own_e, own_m, own_eps, msg, elec, mag):
    count = own_e.shape[1]
    last = count - 1
    even = role[0] == 0

    def run(is_even):
        if is_even:
            want_m, want_e = {}, {1: {0}, 2: {0}}
        else:
            want_m, want_e = {s: {last} for s in range(1, 4)}, {}
        need_m, need_e = needed(want_m, want_e, count)
        for k in range(2):
            msg[6 + k] = own_eps[k if is_even else last - k]
            if is_even:
                msg[k] = own_e[1 + k, 0]
        for step in range(1, 4):
            src_e, src_m = (own_e, own_m) if step == 1 else (elec, mag)
            for p in sorted(need_m[step]):
                far = (src_e[Y, p + 1], src_e[Z, p + 1]) if p < last else None
                new = magnetic_plane(planes(src_e, p), far, planes(src_m, p))
                store(mag, p, new)
                if not is_even and p == last:
                    for k in range(2):
                        msg[2 * step - 2 + k] = new[1 + k]
            for p in sorted(need_e[step]):
                past = (mag[Y, p - 1], mag[Z, p - 1]) if p else None
                new = electric_plane(planes(mag, p), past, planes(src_e, p), own_eps[p])
                store(elec, p, new)
                if is_even and p == 0:
                    for k in range(2):
                        msg[2 * step + k] = new[1 + k]

    pl.when(even)(functools.partial(run, True))
    pl.when(jnp.logical_not(even))(functools.partial(run, False))


def closed_kernel(role, own_e, own_m, own_eps, mate_e, mate_m, mate_eps, msg, nears, elec, mag):
    half = own_e.shape[1]
    count = 2 * half
    even = role[0] == 0

    def send(step, value):
        for k in range(2):
            msg[2 * (step - 4) + k] = value[1 + k]

    def run(is_even):
        steps = range(1, STEPS + 1)
        if is_even:
            want_m, want_e = {}, {s: {0, half} if s > 2 else {half} for s in steps if s < STEPS}
        else:
            want_m, want_e = {s: {half - 1, count - 1} if s > 3 else {half - 1} for s in steps}, {}
        need_m, need_e = needed(want_m, want_e, count)

        def first(own, mate, p):
            ref = own if (p < half) == is_even else mate
            return ref, p % half

        def all_of(step, pair, ref, p):
            if step > 1:
                return planes(ref, p)
            return planes(*first(*pair, p))

        def two_of(step, pair, ref, p):
            return tuple(all_of(step, pair, ref, p)[1:])

        pair_e, pair_m = (own_e, mate_e), (own_m, mate_m)
        if is_even:
            for k in range(2):
                nears[k] = mate_e[1 + k, 0]
        for step in steps:
            for p in sorted(need_m[step]):
                far = two_of(step, pair_e, elec, p + 1) if p + 1 < count else None
                here = all_of(step, pair_e, elec, p)
                new = magnetic_plane(here, far, all_of(step, pair_m, mag, p))
                store(mag, p, new)
                if not is_even and p == count - 1 and step > 3:
                    send(step, new)
                if not is_even and p == half - 1:
                    nears[2 * (step - 1)] = new[Y] - COURANT * far[1]
                    nears[2 * (step - 1) + 1] = new[Z] + COURANT * far[0]
            for p in sorted(need_e[step]):
                past = (mag[Y, p - 1], mag[Z, p - 1]) if p else None
                ref, at = first(own_eps, mate_eps, p)
                new = electric_plane(planes(mag, p), past, all_of(step, pair_e, elec, p), ref[at])
                store(elec, p, new)
                if is_even and p == 0 and step > 2:
                    send(step + 1, new)
                if is_even and p == half:
                    for k in range(2):
                        nears[2 * step + k] = new[1 + k]

    pl.when(even)(functools.partial(run, True))
    pl.when(jnp.logical_not(even))(functools.partial(run, False))


def past_near(near, elec):
    return (near[0] + COURANT * elec[Z, 0], near[1] - COURANT * elec[Y, 0])


def weights_kernel(forward, weights):
    depth, count, ny = forward.shape[1:]
    nz = weights.shape[3]
    blank = jnp.zeros(((nz - depth) // 2, ny), jnp.float32)
    for p in range(count):
        for c in range(6):
            slab = forward[c, :, p, :] * (SENS_SCALE if c < 3 else -SENS_SCALE)
            weights[c, p] = jnp.transpose(jnp.concatenate([blank, slab, blank], 0))


LEFT_MAG = {1: 1, 2: 2, 3: 3, 4: 2, 5: 1}
LEFT_ELEC = {1: 1, 2: 2, 3: 2, 4: 1, 5: 0}
RIGHT_MAG = {1: 0, 2: 1, 3: 2, 4: 1, 5: 0}
RIGHT_ELEC = {1: 1, 2: 2, 3: 2, 4: 1, 5: 0}


def beyond_left(step, elec, side_e, side_m):
    for j in range(LEFT_MAG[step]):
        if j == 0:
            far = (elec[Y, 0], elec[Z, 0])
        else:
            far = (side_e[Y, j - 1], side_e[Z, j - 1])
        store(side_m, j, magnetic_plane(planes(side_e, j), far, planes(side_m, j)))


def beyond_left_electric(step, side_e, side_m, side_eps):
    for j in range(LEFT_ELEC[step]):
        past = (side_m[Y, j + 1], side_m[Z, j + 1])
        store(side_e, j, electric_plane(planes(side_m, j), past, planes(side_e, j), side_eps[j]))


def beyond_right(step, mag, side_e, side_m, side_eps, last):
    for j in range(RIGHT_MAG[step]):
        far = (side_e[Y, j + 1], side_e[Z, j + 1])
        store(side_m, j, magnetic_plane(planes(side_e, j), far, planes(side_m, j)))
    for j in range(RIGHT_ELEC[step]):
        if j == 0:
            past = (mag[Y, last], mag[Z, last])
        else:
            past = (side_m[Y, j - 1], side_m[Z, j - 1])
        store(side_e, j, electric_plane(planes(side_m, j), past, planes(side_e, j), side_eps[j]))


def open_kernel(steps, role, elec_in, mag_in, eps, nears, opening, *refs):
    ending = steps[-1] == STEPS
    if ending:
        msgs, accum_in, late_in, side_e_in, side_m_in, weights, high, low = refs[:8]
        elec_out, mag_out, accum_out, pillars, elec, mag, accum, side_e, side_m, sems = refs[8:]
    else:
        accum_in, elec, mag, accum, side_e, side_m, late = refs
    count = eps.shape[0]
    last = count - 1
    even = role[0] == 0
    side_eps = opening.at[6:8]
    for ref, from_ref in zip((side_e, side_m), (side_e_in, side_m_in) if ending else (None, None)):
        for j in range(2):
            for c in range(3):
                ref[c, j] = jnp.zeros(eps.shape[1:], jnp.float32) if from_ref is None else from_ref[c, j]
    if not ending:
        for c in range(3):
            side_e[c, 2] = jnp.zeros(eps.shape[1:], jnp.float32)
            side_m[c, 2] = jnp.zeros(eps.shape[1:], jnp.float32)

    pending = []

    def put(src, dst):
        copy = pltpu.make_async_copy(src, dst, sems.at[len(pending)])
        copy.start()
        pending.append(copy)

    def run(is_even):
        pending.clear()
        sums = None
        scale = role[1 if is_even else 2].astype(jnp.float32)
        if not ending:
            far = (opening[0], opening[1])
            if is_even:
                far = past_near(far, elec_in)
            factor = scale
            for p in range(count):
                factor = factor * (COURANT * COURANT * eps[p])
            for k in range(2):
                late[k] = factor * far[k]
        for step in steps:
            src_e, src_m = (elec_in, mag_in) if step == steps[0] else (elec, mag)
            near = (nears[2 * step - 2], nears[2 * step - 1])
            if step == STEPS:
                near = (near[0] + late_in[0], near[1] + late_in[1])
            ref, at = (opening, 2 * step - 2) if step < 4 else (msgs, 2 * step - 8)
            far = (ref[at], ref[at + 1])
            if is_even:
                beyond = near
                beyond_left(step, src_e, side_e, side_m)
                past0 = ((far[0] + side_m[Y, 0]) * scale, (far[1] + side_m[Z, 0]) * scale)
            else:
                beyond = ((far[0] + side_e[Y, 0]) * scale, (far[1] + side_e[Z, 0]) * scale)
                past0 = past_near(near, src_e)
            for p in range(count):
                nxt = (src_e[Y, p + 1], src_e[Z, p + 1]) if p < last else beyond
                store(mag, p, magnetic_plane(planes(src_e, p), nxt, planes(src_m, p)))
            if step == STEPS:
                put(mag, mag_out)
            if is_even:
                beyond_left_electric(step, side_e, side_m, side_eps)
            else:
                beyond_right(step, mag, side_e, side_m, side_eps, last)
            waves = (math.cos(ANGULAR * step), math.sin(ANGULAR * step))
            src_a = accum_in if step == steps[0] else accum
            for p in range(count):
                past = (mag[Y, p - 1], mag[Z, p - 1]) if p else past0
                new = electric_plane(planes(mag, p), past, planes(src_e, p), eps[p])
                store(elec, p, new)
                total = None
                for c in range(6):
                    value = src_a[c, p] + waves[c // 3] * new[c % 3]
                    accum[c, p] = value
                    if step == STEPS:
                        term = value * weights[c, p]
                        total = term if total is None else total + term
                if step == STEPS:
                    put(elec.at[:, p], elec_out.at[:, p])
                    put(accum.at[:, p], accum_out.at[:, p])
                    term = pillar_terms(total, high[p : p + 1], low[p], pillars.shape[0])
                    sums = term if sums is None else sums + term
        if ending:
            pillars[...] = sums
        for copy in pending:
            copy.wait()

    pl.when(even)(functools.partial(run, True))
    pl.when(jnp.logical_not(even))(functools.partial(run, False))


def pillar_terms(total, high, low, owners):
    row = lax.dot_general(
        jnp.ones((8, total.shape[1]), jnp.float32), total, (((1,), (1,)), ((), ())),
        precision=lax.Precision.HIGHEST, preferred_element_type=jnp.float32,
    )[0:1]
    label = lax.broadcasted_iota(jnp.int32, (owners, total.shape[0]), 0)
    return lax.dot_general(
        jnp.where(label == high, row, 0.0), low, (((1,), (0,)), ((), ())),
        precision=lax.Precision.HIGHEST, preferred_element_type=jnp.float32,
    )


def call(kernel, args, outs, scratch=(), smem=1, fast=(), slow_outs=0, copies=0):
    args = [
        pltpu.with_memory_space_constraint(a, pltpu.VMEM if i in fast else pltpu.HBM) if i >= smem else a
        for i, a in enumerate(args)
    ]
    return pl.pallas_call(
        kernel,
        out_shape=[
            shape_of(*o) if i < slow_outs else pltpu.VMEM(o, jnp.float32) for i, o in enumerate(outs)
        ],
        in_specs=[SMEM] * smem + [VMEM] * (len(args) - smem),
        out_specs=[HBM] * slow_outs + [VMEM] * (len(outs) - slow_outs),
        scratch_shapes=[pltpu.VMEM(d, jnp.float32) for d in scratch]
        + [pltpu.SemaphoreType.DMA((copies,))] * (copies > 0),
        compiler_params=pltpu.CompilerParams(vmem_limit_bytes=12 * 2**20),
        cost_estimate=pl.CostEstimate(flops=1, bytes_accessed=1, transcendentals=0),
    )(*args)


def shape_of(*dims):
    return jax.ShapeDtypeStruct(dims, jnp.float32)


def halved(sums, axis):
    size = lax.axis_size(axis)
    me = lax.axis_index(axis)
    bits = size.bit_length() - 1
    block = sums
    for bit in range(bits):
        pair = block.reshape(-1, 2, block.shape[-1])
        mine = (me >> bit) & 1
        keep = jnp.where(mine == 0, pair[:, 0], pair[:, 1])
        give = jnp.where(mine == 0, pair[:, 1], pair[:, 0])
        block = keep + lax.ppermute(give, axis, [(i, i ^ (1 << bit)) for i in range(size)])
    return block.reshape(-1)


def per_device(electric, magnetic, inv_eps, accum, forward, pillar_ids):
    size = lax.axis_size("gx")
    me = lax.axis_index("gx")
    role = jnp.stack([me % 2, jnp.where(me == 0, 0, 1), jnp.where(me == size - 1, 0, 1)]).astype(jnp.int32)
    count, ny, nz = inv_eps.shape
    same_chip = [(i, i ^ 1) for i in range(size)]
    inner = range(1, size - 1, 2)
    next_chip = [(i, i + 1) for i in inner] + [(i + 1, i) for i in inner]

    per_owner = ny
    high = pillar_ids // per_owner
    low = (pillar_ids % per_owner)[:, :, None] == jnp.arange(per_owner, dtype=jnp.int32)
    low = low.astype(jnp.float32)
    field, side = electric.shape, (3, 3, ny, nz)

    def to_mate(block):
        return lax.ppermute(block, "gx", same_chip)

    def to_chip(block):
        return lax.ppermute(block, "gx", next_chip)

    own = [role, electric, magnetic, inv_eps]
    (opening,) = call(early_kernel, own, [(8, ny, nz)], scratch=[field, field])
    opening = to_chip(opening)
    mate = [to_mate(electric), to_mate(magnetic), to_mate(inv_eps)]
    later, nears = call(
        closed_kernel,
        own + mate,
        [(4, ny, nz), (2 * STEPS, ny, nz)],
        scratch=[(3, 2 * count, ny, nz)] * 2,
        fast=(4, 5, 6),
    )
    later = to_chip(later)
    (weights,) = call(weights_kernel, [forward], [accum.shape], smem=0)
    elec, mag, total, side_e, side_m, late = call(
        functools.partial(open_kernel, (1, 2, 3)),
        own + [nears, opening, accum],
        [field, field, accum.shape, side, side, (2, ny, nz)],
        fast=(4, 5),
    )
    late = to_mate(late)
    electric, magnetic, accum, sums = call(
        functools.partial(open_kernel, (4, 5)),
        [role, elec, mag, inv_eps, nears, opening, later, total, late, side_e, side_m, weights, high, low],
        [field, field, accum.shape, (size, per_owner)],
        scratch=[field, field, accum.shape, side, side],
        fast=(1, 2, *range(4, 12)),
        slow_outs=3,
        copies=1 + 2 * count,
    )
    return electric, magnetic, accum, halved(sums, "gx")


def solution(mesh):
    return jax.shard_map(
        per_device,
        mesh=mesh,
        in_specs=(
            P(None, ("design", "gx"), None, None),
            P(None, ("design", "gx"), None, None),
            P(("design", "gx"), None, None),
            P(None, ("design", "gx"), None, None),
            P(None, None, ("design", "gx"), None),
            P("gx", None),
        ),
        out_specs=(
            P(None, ("design", "gx"), None, None),
            P(None, ("design", "gx"), None, None),
            P(None, ("design", "gx"), None, None),
            P(("design", "gx")),
        ),
        check_vma=False,
    )
```

time: 63.3 us -> 47.5 us (0.75)
  Pallas kernels: 24.3 us -> 17.2 us
  other arithmetic: 6.44 us -> 2.06 us
  starting transfers between devices: 23.9 us -> 20.5 us
  local copies, waits for them, and re-layouts: 1.28 us -> 0.02 us
    pallas_call x6 -> x5, Pallas kernels: 24.3 us -> 17.2 us  [call(): pl.pallas_call(kernel, out_shape=[shape_of(*o) if i < slow_outs else pltp...]
    ppermute x4, starting transfers between devices: 11.8 us -> 7.97 us  [to_mate(): return lax.ppermute(block, 'gx', same_chip)]
    ppermute x4, starting transfers between devices: 9.31 us -> 11.2 us  [halved(): lax.ppermute(give, axis, [(i, i ^ 1 << bit) for i in range(size)])]
    ppermute x3 -> x2, starting transfers between devices: 2.8 us -> 1.36 us  [to_chip(): return lax.ppermute(block, 'gx', next_chip)]
    add x2, other arithmetic: 1.37 us -> 0.01 us  [halved(): keep + lax.ppermute(give, axis, [(i, i ^ 1 << bit) for i in range(size)])]
    slice x2, other arithmetic: 1.15 us -> 0.02 us  [halved(): keep = jnp.where(mine == 0, pair[:, 0], pair[:, 1])]
    ppermute x4, waiting for transfers between devices: 0.42 us -> 1.31 us  [to_mate(): return lax.ppermute(block, 'gx', same_chip)]
    unnamed x12 -> x4, local copies, waits for them, and re-layouts: 0.69 us -> 0.01 us
  transfers between devices with their start and end apart: 11 -> 10, of which waited for: 5 -> 6; matrix products, arithmetic and copies ran while one was open for 10% -> 3% of each run, Pallas kernels for 28% -> 27%
where the time goes in v3:
time: 47.5 us; the launch traced here: 47.3 us
  starting transfers between devices  20.5 us (43%)
  Pallas kernels  17.2 us (36%)
  waiting for transfers between devices  6.77 us (14%)
  other arithmetic  2.06 us (4%)
  between operations  0.75 us (2%)
    pallas_call x5, Pallas kernels, call(): pl.pallas_call(kernel, out_shape=[shape_of(*o) if i < slow_outs else pltp...  17.2 us
    ppermute x4, starting transfers between devices, halved(): lax.ppermute(give, axis, [(i, i ^ 1 << bit) for i in range(size)])  11.2 us
    ppermute x4, starting transfers between devices, to_mate(): return lax.ppermute(block, 'gx', same_chip)  7.97 us
    ppermute x4, waiting for transfers between devices, halved(): lax.ppermute(give, axis, [(i, i ^ 1 << bit) for i in range(size)])  5.46 us
    ppermute x2, starting transfers between devices, to_chip(): return lax.ppermute(block, 'gx', next_chip)  1.36 us
    ppermute x4, waiting for transfers between devices, to_mate(): return lax.ppermute(block, 'gx', same_chip)  1.31 us
  transfers between devices with their start and end apart: 10, of which 6 were waited for; matrix products, arithmetic and copies ran while one was open for 3% of the time, Pallas kernels for 27%

profile of v3, /device:TPU:0, one launch (start us, length us, event | category | flops | bytes accessed | tf_op | source)
XLA Modules:
  0.0 47.3 jit_solution(3582673110678726532)
XLA Ops:
  0.6 0.0 copy-start
  0.6 0.5 %collective-permute-start = (f32[3,4,128,128]{3,2,1,0:T(8,128)}, f32[3,4,128,128]{3,2,1,0:T(8,128)S(1)}, u32[]{:S(2)}, u32[]{:S(2)}) collective-permute-start(f32[3,4,128,128]{3,2,1,0:T(8,128)} %elec_in.1), channel_id=1, source_target_pairs={{0,1},{1,0},{2,3},{3,2},{4,5},{5,4},{6,7},{7,6},{8,9},{9,8},{10,11... | collective-permute-start | bytes 2359304 | tf_op jit(solution)/shard_map/ppermute | solution.py:381
  1.2 0.1 collective-permute-start.1
  1.2 0.1 pad_add_fusion.role
  1.3 1.8 %shard_map.94 = f32[8,128,128]{2,1,0:T(8,128)S(1)} custom-call(s32[3]{0:T(128)S(1)} %pad_add_fusion.role, f32[3,4,128,128]{3,2,1,0:T(8,128)} %elec_in.1, f32[3,4,128,128]{3,2,1,0:T(8,128)} %mag_in.1, f32[4,128,128]{2,1,0:T(8,128)} %eps.3), custom_call_target="tpu_custom_call" | custom-call | flops 1 | bytes 1 | tf_op jit(solution)/shard_map/pallas_call | solution.py:333
  3.2 0.0 copy-start.1
  3.2 0.7 %collective-permute-start.3 = (f32[8,128,128]{2,1,0:T(8,128)S(1)}, f32[8,128,128]{2,1,0:T(8,128)S(1)}, u32[]{:S(2)}, u32[]{:S(2)}) collective-permute-start(f32[8,128,128]{2,1,0:T(8,128)S(1)} %shard_map.94), channel_id=1, source_target_pairs={{1,2},{3,4},{5,6},{7,8},{9,10},{11,12},{13,14},{2,1},{4,3},{6,5},{... | collective-permute-start | bytes 1572872 | tf_op jit(solution)/shard_map/ppermute | solution.py:384
  3.9 0.0 copy-done
  3.9 4.3 %collective-permute-start.2 = (f32[4,128,128]{2,1,0:T(8,128)S(1)}, f32[4,128,128]{2,1,0:T(8,128)S(1)}, u32[]{:S(2)}, u32[]{:S(2)}) collective-permute-start(f32[4,128,128]{2,1,0:T(8,128)S(1)} %copy-done), channel_id=1, source_target_pairs={{0,1},{1,0},{2,3},{3,2},{4,5},{5,4},{6,7},{7,6},{8,9},{9,8},{10,11... | collective-permute-start | bytes 786440 | tf_op jit(solution)/shard_map/ppermute | solution.py:381
  8.2 1.2 %collective-permute-done.2.mate_eps = f32[4,128,128]{2,1,0:T(8,128)S(1)} collective-permute-done((f32[4,128,128]{2,1,0:T(8,128)S(1)}, f32[4,128,128]{2,1,0:T(8,128)S(1)}, u32[]{:S(2)}, u32[]{:S(2)}) %collective-permute-start.2) | collective-permute-done | bytes 262176 | tf_op jit(solution)/shard_map/ppermute | solution.py:381
  9.4 0.0 collective-permute-done.mate_e
  9.4 0.0 collective-permute-done.1.mate_m
  9.4 4.6 %shard_map.93 = (f32[4,128,128]{2,1,0:T(8,128)}, f32[10,128,128]{2,1,0:T(8,128)S(1)}) custom-call(s32[3]{0:T(128)S(1)} %pad_add_fusion.role, f32[3,4,128,128]{3,2,1,0:T(8,128)} %elec_in.1, f32[3,4,128,128]{3,2,1,0:T(8,128)} %mag_in.1, f32[4,128,128]{2,1,0:T(8,128)} %eps.3, f32[3,4,128,128]{3,2,1,0:T(8,128)S(1)} %collective-permute-done.mate_e, ...), custom_call_target="tpu_custom_call" | custom-call | flops 1 | bytes 1 | tf_op jit(solution)/shard_map/pallas_call | solution.py:333
  14.0 0.7 %collective-permute-start.4 = (f32[4,128,128]{2,1,0:T(8,128)}, f32[4,128,128]{2,1,0:T(8,128)S(1)}, u32[]{:S(2)}, u32[]{:S(2)}) collective-permute-start(f32[4,128,128]{2,1,0:T(8,128)} %get-tuple-element.19), channel_id=1, source_target_pairs={{1,2},{3,4},{5,6},{7,8},{9,10},{11,12},{13,14},{2,1},{4,3},{6,5},{... | collective-permute-start | bytes 786440 | tf_op jit(solution)/shard_map/ppermute | solution.py:384
  14.7 0.0 copy-done.1
  14.7 0.6 %add_select_fusion = (s32[4,128]{1,0:T(4,128)S(1)}, s32[4,128]{1,0:T(4,128)}) fusion(s32[4,128]{1,0:T(4,128)S(1)} %copy-done.1), kind=kLoop, calls=%fused_computation.5 | loop fusion | flops 9728 | bytes 6144 | tf_op jit(solution)/shard_map/jit(remainder)/select_n | solution.py:376
  15.3 1.5 %shard_map.96.refs_5_ = f32[6,4,128,128]{3,2,1,0:T(8,128)S(1)} custom-call(f32[6,32,4,128]{3,2,1,0:T(4,128)} %forward.1), custom_call_target="tpu_custom_call" | custom-call | flops 1 | bytes 1 | tf_op jit(solution)/shard_map/pallas_call | solution.py:333
  16.8 0.0 collective-permute-done.3.opening
  16.8 4.9 %shard_map.95 = (f32[3,4,128,128]{3,2,1,0:T(8,128)S(1)}, f32[3,4,128,128]{3,2,1,0:T(8,128)S(1)}, f32[6,4,128,128]{3,2,1,0:T(8,128)S(1)}, f32[3,3,128,128]{3,2,1,...) custom-call(s32[3]{0:T(128)S(1)} %pad_add_fusion.role, f32[3,4,128,128]{3,2,1,0:T(8,128)} %elec_in.1, ...), custom_call_target="tpu_custom_call" | custom-call | flops 1 | bytes 1 | tf_op jit(solution)/shard_map/pallas_call | solution.py:333
  21.7 3.0 %collective-permute-start.5 = (f32[2,128,128]{2,1,0:T(8,128)S(1)}, f32[2,128,128]{2,1,0:T(8,128)S(1)}, u32[]{:S(2)}, u32[]{:S(2)}) collective-permute-start(f32[2,128,128]{2,1,0:T(8,128)S(1)} %get-tuple-element.21), channel_id=1, source_target_pairs={{0,1},{1,0},{2,3},{3,2},{4,5},{5,4},{6,7},{7,6},{8,9},{9,8},{10,11... | collective-permute-start | bytes 393224 | tf_op jit(solution)/shard_map/ppermute | solution.py:381
  24.7 0.8 %fusion.refs_7_ = f32[4,128,128]{2,1,0:T(8,128)} fusion(s32[4,128]{1,0:T(4,128)S(1)} %get-tuple-element.36), kind=kLoop, calls=%fused_computation.1 | loop fusion | flops 131072 | bytes 264192 | tf_op jit(solution)/shard_map/convert_element_type | solution.py:377
  25.5 0.1 collective-permute-done.5.refs_2_
  25.7 0.0 collective-permute-done.4.refs_0_
  25.7 4.4 %shard_map.97 = (f32[3,4,128,128]{3,2,1,0:T(8,128)}, f32[3,4,128,128]{3,2,1,0:T(8,128)}, f32[6,4,128,128]{3,2,1,0:T(8,128)}, f32[16,128]{1,0:T(8,128)S(1)}) custom-call(s32[3]{0:T(128)S(1)} %pad_add_fusion.role, f32[3,4,128,128]{3,2,1,0:T(8,128)S(1)} %get-tuple-element.17.elec_in, f32[3,4,128,128]{3,2,1,0:T(8,128)S(1)} %get-tuple-element.18.mag_in, ...), custom_call_target="tpu_custom_call" | custom-call | flops 1 | bytes 1 | tf_op jit(solution)/shard_map/pallas_call | solution.py:333
  30.1 0.4 collective-permute-start.6
  30.5 0.8 %collective-permute-done.6 = f32[8,128]{1,0:T(8,128)S(1)} collective-permute-done((f32[8,128]{1,0:T(8,128)S(1)}, f32[8,128]{1,0:T(8,128)S(1)}, u32[]{:S(2)}, u32[]{:S(2)}) %collective-permute-start.6) | collective-permute-done | bytes 4128 | tf_op jit(solution)/shard_map/ppermute | solution.py:361
  31.4 2.9 %collective-permute-start.7 = (f32[4,128]{1,0:T(4,128)S(1)}, f32[4,128]{1,0:T(4,128)S(1)}, u32[]{:S(2)}, u32[]{:S(2)}) collective-permute-start(f32[4,128]{1,0:T(4,128)S(1)} %bitcast.51), channel_id=1, source_target_pairs={{0,2},{1,3},{2,0},{3,1},{4,6},{5,7},{6,4},{7,5},{8,10},{9,11},{10,... | collective-permute-start | bytes 6152 | tf_op jit(solution)/shard_map/ppermute | solution.py:361
  34.3 1.6 %collective-permute-done.7 = f32[4,128]{1,0:T(4,128)S(1)} collective-permute-done((f32[4,128]{1,0:T(4,128)S(1)}, f32[4,128]{1,0:T(4,128)S(1)}, u32[]{:S(2)}, u32[]{:S(2)}) %collective-permute-start.7) | collective-permute-done | bytes 2080 | tf_op jit(solution)/shard_map/ppermute | solution.py:361
  35.8 4.7 %collective-permute-start.8 = (f32[2,128]{1,0:T(2,128)S(1)}, f32[2,128]{1,0:T(2,128)S(1)}, u32[]{:S(2)}, u32[]{:S(2)}) collective-permute-start(f32[2,128]{1,0:T(2,128)S(1)} %bitcast.52), channel_id=1, source_target_pairs={{0,4},{1,5},{2,6},{3,7},{4,0},{5,1},{6,2},{7,3},{8,12},{9,13},{10,... | collective-permute-start | bytes 3080 | tf_op jit(solution)/shard_map/ppermute | solution.py:361
  40.6 1.5 %collective-permute-done.8 = f32[2,128]{1,0:T(2,128)S(1)} collective-permute-done((f32[2,128]{1,0:T(2,128)S(1)}, f32[2,128]{1,0:T(2,128)S(1)}, u32[]{:S(2)}, u32[]{:S(2)}) %collective-permute-start.8) | collective-permute-done | bytes 1056 | tf_op jit(solution)/shard_map/ppermute | solution.py:361
  42.1 3.1 %collective-permute-start.9 = (f32[1,128]{1,0:T(1,128)S(1)}, f32[1,128]{1,0:T(1,128)S(1)}, u32[]{:S(2)}, u32[]{:S(2)}) collective-permute-start(f32[1,128]{1,0:T(1,128)S(1)} %fusion.6), channel_id=1, source_target_pairs={{0,8},{1,9},{2,10},{3,11},{4,12},{5,13},{6,14},{7,15},{8,0},{9,1},... | collective-permute-start | bytes 1544 | tf_op jit(solution)/shard_map/ppermute | solution.py:361
  45.2 1.5 %collective-permute-done.9 = f32[1,128]{1,0:T(1,128)S(1)} collective-permute-done((f32[1,128]{1,0:T(1,128)S(1)}, f32[1,128]{1,0:T(1,128)S(1)}, u32[]{:S(2)}, u32[]{:S(2)}) %collective-permute-start.9) | collective-permute-done | bytes 544 | tf_op jit(solution)/shard_map/ppermute | solution.py:361
  46.7 0.5 %fusion.5 = f32[128]{0:T(128)} fusion(f32[1,128]{1,0:T(1,128)S(1)} %collective-permute-done.9, pred[]{:T(512)S(6)} %eq.44, f32[1,2,128]{2,1,0:T(2,128)S(1)} %fusion.2), kind=kLoop, calls=%fused_computation.21 | loop fusion | flops 256 | bytes 2049 | tf_op jit(solution)/shard_map/reshape | solution.py:362
  (8 shorter events, 0.1 us)
Async XLA Ops:
  0.6 3.2 %copy-start = (f32[4,128,128]{2,1,0:T(8,128)S(1)}, f32[4,128,128]{2,1,0:T(8,128)}, u32[]{:S(2)}) copy-start(f32[4,128,128]{2,1,0:T(8,128)} %eps.3) | copy-start | bytes 786436
  0.6 8.7 %collective-permute-start = (f32[3,4,128,128]{3,2,1,0:T(8,128)}, f32[3,4,128,128]{3,2,1,0:T(8,128)S(1)}, u32[]{:S(2)}, u32[]{:S(2)}) collective-permute-start(f32[3,4,128,128]{3,2,1,0:T(8,128)} %elec_in.1), channel_id=1, source_target_pairs={{0,1},{1,0},{2,3},{3,2},{4,5},{5,4},{6,7},{7,6},{8,9},{9,8},{10,11... | collective-permute-start | bytes 2359304 | tf_op jit(solution)/shard_map/ppermute | solution.py:381
  1.2 8.2 %collective-permute-start.1 = (f32[3,4,128,128]{3,2,1,0:T(8,128)}, f32[3,4,128,128]{3,2,1,0:T(8,128)S(1)}, u32[]{:S(2)}, u32[]{:S(2)}) collective-permute-start(f32[3,4,128,128]{3,2,1,0:T(8,128)} %mag_in.1), channel_id=1, source_target_pairs={{0,1},{1,0},{2,3},{3,2},{4,5},{5,4},{6,7},{7,6},{8,9},{9,8},{10,11... | collective-permute-start | bytes 2359304 | tf_op jit(solution)/shard_map/ppermute | solution.py:381
  3.2 11.5 %copy-start.1 = (s32[4,128]{1,0:T(4,128)S(1)}, s32[4,128]{1,0:T(4,128)}, u32[]{:S(2)}) copy-start(s32[4,128]{1,0:T(4,128)} %param.11) | copy-start | bytes 6148
  3.2 13.6 %collective-permute-start.3 = (f32[8,128,128]{2,1,0:T(8,128)S(1)}, f32[8,128,128]{2,1,0:T(8,128)S(1)}, u32[]{:S(2)}, u32[]{:S(2)}) collective-permute-start(f32[8,128,128]{2,1,0:T(8,128)S(1)} %shard_map.94), channel_id=1, source_target_pairs={{1,2},{3,4},{5,6},{7,8},{9,10},{11,12},{13,14},{2,1},{4,3},{6,5},{... | collective-permute-start | bytes 1572872 | tf_op jit(solution)/shard_map/ppermute | solution.py:384
  3.9 5.5 %collective-permute-start.2 = (f32[4,128,128]{2,1,0:T(8,128)S(1)}, f32[4,128,128]{2,1,0:T(8,128)S(1)}, u32[]{:S(2)}, u32[]{:S(2)}) collective-permute-start(f32[4,128,128]{2,1,0:T(8,128)S(1)} %copy-done), channel_id=1, source_target_pairs={{0,1},{1,0},{2,3},{3,2},{4,5},{5,4},{6,7},{7,6},{8,9},{9,8},{10,11... | collective-permute-start | bytes 786440 | tf_op jit(solution)/shard_map/ppermute | solution.py:381
  14.0 11.7 %collective-permute-start.4 = (f32[4,128,128]{2,1,0:T(8,128)}, f32[4,128,128]{2,1,0:T(8,128)S(1)}, u32[]{:S(2)}, u32[]{:S(2)}) collective-permute-start(f32[4,128,128]{2,1,0:T(8,128)} %get-tuple-element.19), channel_id=1, source_target_pairs={{1,2},{3,4},{5,6},{7,8},{9,10},{11,12},{13,14},{2,1},{4,3},{6,5},{... | collective-permute-start | bytes 786440 | tf_op jit(solution)/shard_map/ppermute | solution.py:384
  21.7 4.0 %collective-permute-start.5 = (f32[2,128,128]{2,1,0:T(8,128)S(1)}, f32[2,128,128]{2,1,0:T(8,128)S(1)}, u32[]{:S(2)}, u32[]{:S(2)}) collective-permute-start(f32[2,128,128]{2,1,0:T(8,128)S(1)} %get-tuple-element.21), channel_id=1, source_target_pairs={{0,1},{1,0},{2,3},{3,2},{4,5},{5,4},{6,7},{7,6},{8,9},{9,8},{10,11... | collective-permute-start | bytes 393224 | tf_op jit(solution)/shard_map/ppermute | solution.py:381
  30.1 1.3 %collective-permute-start.6 = (f32[8,128]{1,0:T(8,128)S(1)}, f32[8,128]{1,0:T(8,128)S(1)}, u32[]{:S(2)}, u32[]{:S(2)}) collective-permute-start(f32[8,128]{1,0:T(8,128)S(1)} %select_bitcast_fusion), channel_id=1, source_target_pairs={{0,1},{1,0},{2,3},{3,2},{4,5},{5,4},{6,7},{7,6},{8,9},{9,8},{10,11... | collective-permute-start | bytes 12296 | tf_op jit(solution)/shard_map/ppermute | solution.py:361
  31.4 4.5 %collective-permute-start.7 = (f32[4,128]{1,0:T(4,128)S(1)}, f32[4,128]{1,0:T(4,128)S(1)}, u32[]{:S(2)}, u32[]{:S(2)}) collective-permute-start(f32[4,128]{1,0:T(4,128)S(1)} %bitcast.51), channel_id=1, source_target_pairs={{0,2},{1,3},{2,0},{3,1},{4,6},{5,7},{6,4},{7,5},{8,10},{9,11},{10,... | collective-permute-start | bytes 6152 | tf_op jit(solution)/shard_map/ppermute | solution.py:361
  35.8 6.3 %collective-permute-start.8 = (f32[2,128]{1,0:T(2,128)S(1)}, f32[2,128]{1,0:T(2,128)S(1)}, u32[]{:S(2)}, u32[]{:S(2)}) collective-permute-start(f32[2,128]{1,0:T(2,128)S(1)} %bitcast.52), channel_id=1, source_target_pairs={{0,4},{1,5},{2,6},{3,7},{4,0},{5,1},{6,2},{7,3},{8,12},{9,13},{10,... | collective-permute-start | bytes 3080 | tf_op jit(solution)/shard_map/ppermute | solution.py:361
  42.1 4.6 %collective-permute-start.9 = (f32[1,128]{1,0:T(1,128)S(1)}, f32[1,128]{1,0:T(1,128)S(1)}, u32[]{:S(2)}, u32[]{:S(2)}) collective-permute-start(f32[1,128]{1,0:T(1,128)S(1)} %fusion.6), channel_id=1, source_target_pairs={{0,8},{1,9},{2,10},{3,11},{4,12},{5,13},{6,14},{7,15},{8,0},{9,1},... | collective-permute-start | bytes 1544 | tf_op jit(solution)/shard_map/ppermute | solution.py:361

commit v4 on v3

--- a/solution.py
+++ b/solution.py
@@ -81,37 +81,40 @@
     return mag, elec
 
 
-def early_kernel(role, own_e, own_m, own_eps, msg, elec, mag):
+def early_kernel(role, own_e, own_m, own_eps, msg_a, msg_b, elec, mag):
     count = own_e.shape[1]
     last = count - 1
     even = role[0] == 0
 
+    def send(step, value):
+        ref = msg_a if step < 3 else msg_b
+        for k in range(2):
+            ref[2 * ((step - 1) % 2) + k] = value[1 + k]
+
     def run(is_even):
         if is_even:
-            want_m, want_e = {}, {1: {0}, 2: {0}}
+            want_m, want_e = {}, {s: {0} for s in range(1, 4)}
         else:
-            want_m, want_e = {s: {last} for s in range(1, 4)}, {}
+            want_m, want_e = {s: {last} for s in range(1, 5)}, {}
         need_m, need_e = needed(want_m, want_e, count)
         for k in range(2):
-            msg[6 + k] = own_eps[k if is_even else last - k]
-            if is_even:
-                msg[k] = own_e[1 + k, 0]
-        for step in range(1, 4):
+            msg_a[4 + k] = own_eps[k if is_even else last - k]
+        if is_even:
+            send(1, planes(own_e, 0))
+        for step in range(1, 5):
             src_e, src_m = (own_e, own_m) if step == 1 else (elec, mag)
             for p in sorted(need_m[step]):
                 far = (src_e[Y, p + 1], src_e[Z, p + 1]) if p < last else None
                 new = magnetic_plane(planes(src_e, p), far, planes(src_m, p))
                 store(mag, p, new)
                 if not is_even and p == last:
-                    for k in range(2):
-                        msg[2 * step - 2 + k] = new[1 + k]
+                    send(step, new)
             for p in sorted(need_e[step]):
                 past = (mag[Y, p - 1], mag[Z, p - 1]) if p else None
                 new = electric_plane(planes(mag, p), past, planes(src_e, p), own_eps[p])
                 store(elec, p, new)
                 if is_even and p == 0:
-                    for k in range(2):
-                        msg[2 * step + k] = new[1 + k]
+                    send(step + 1, new)
 
     pl.when(even)(functools.partial(run, True))
     pl.when(jnp.logical_not(even))(functools.partial(run, False))
@@ -122,16 +125,16 @@
     count = 2 * half
     even = role[0] == 0
 
-    def send(step, value):
+    def send(value):
         for k in range(2):
-            msg[2 * (step - 4) + k] = value[1 + k]
+            msg[k] = value[1 + k]
 
     def run(is_even):
         steps = range(1, STEPS + 1)
         if is_even:
-            want_m, want_e = {}, {s: {0, half} if s > 2 else {half} for s in steps if s < STEPS}
+            want_m, want_e = {}, {s: {0, half} if s > 3 else {half} for s in steps if s < STEPS}
         else:
-            want_m, want_e = {s: {half - 1, count - 1} if s > 3 else {half - 1} for s in steps}, {}
+            want_m, want_e = {s: {half - 1, count - 1} if s > 4 else {half - 1} for s in steps}, {}
         need_m, need_e = needed(want_m, want_e, count)
 
         def first(own, mate, p):
@@ -156,8 +159,8 @@
                 here = all_of(step, pair_e, elec, p)
                 new = magnetic_plane(here, far, all_of(step, pair_m, mag, p))
                 store(mag, p, new)
-                if not is_even and p == count - 1 and step > 3:
-                    send(step, new)
+                if not is_even and p == count - 1 and step == STEPS:
+                    send(new)
                 if not is_even and p == half - 1:
                     nears[2 * (step - 1)] = new[Y] - COURANT * far[1]
                     nears[2 * (step - 1) + 1] = new[Z] + COURANT * far[0]
@@ -166,8 +169,8 @@
                 ref, at = first(own_eps, mate_eps, p)
                 new = electric_plane(planes(mag, p), past, all_of(step, pair_e, elec, p), ref[at])
                 store(elec, p, new)
-                if is_even and p == 0 and step > 2:
-                    send(step + 1, new)
+                if is_even and p == 0 and step == STEPS - 1:
+                    send(new)
                 if is_even and p == half:
                     for k in range(2):
                         nears[2 * step + k] = new[1 + k]
@@ -180,7 +183,14 @@
     return (near[0] + COURANT * elec[Z, 0], near[1] - COURANT * elec[Y, 0])
 
 
-def weights_kernel(forward, weights):
+def staging_kernel(forward, *refs):
+    half = (len(refs) - 2) // 2
+    sems, weights = refs[-1], refs[half]
+    copies = [
+        pltpu.make_async_copy(refs[i], refs[half + 1 + i], sems.at[i]) for i in range(half)
+    ]
+    for copy in copies:
+        copy.start()
     depth, count, ny = forward.shape[1:]
     nz = weights.shape[3]
     blank = jnp.zeros(((nz - depth) // 2, ny), jnp.float32)
@@ -188,6 +198,8 @@
         for c in range(6):
             slab = forward[c, :, p, :] * (SENS_SCALE if c < 3 else -SENS_SCALE)
             weights[c, p] = jnp.transpose(jnp.concatenate([blank, slab, blank], 0))
+    for copy in copies:
+        copy.wait()
 
 
 LEFT_MAG = {1: 1, 2: 2, 3: 3, 4: 2, 5: 1}
@@ -223,30 +235,35 @@
         store(side_e, j, electric_plane(planes(side_m, j), past, planes(side_e, j), side_eps[j]))
 
 
-def open_kernel(steps, role, elec_in, mag_in, eps, nears, opening, *refs):
-    ending = steps[-1] == STEPS
-    if ending:
-        msgs, accum_in, late_in, side_e_in, side_m_in, weights, high, low = refs[:8]
-        elec_out, mag_out, accum_out, pillars, elec, mag, accum, side_e, side_m, sems = refs[8:]
-    else:
-        accum_in, elec, mag, accum, side_e, side_m, late = refs
+def open_kernel(steps, *refs):
+    first, ending = steps[0], steps[-1] == STEPS
+    names = ["role", "elec_in", "mag_in", "eps", "nears", "opening", "accum_in"]
+    names += ["msgs", "side_e_in", "side_m_in"] * (first > 1)
+    names += ["late_in", "weights", "ids"] * ending
+    names += ["elec_out", "mag_out", "accum_out", "pillars"] * ending
+    names += ["elec", "mag", "accum", "side_e", "side_m"]
+    names += ["late"] * (first == 1) + ["sems"] * ending
+    r = dict(zip(names, refs, strict=True))
+    role, elec_in, mag_in, eps, nears, opening, accum_in = refs[:7]
+    elec, mag, accum, side_e, side_m = (r[n] for n in ("elec", "mag", "accum", "side_e", "side_m"))
     count = eps.shape[0]
     last = count - 1
     even = role[0] == 0
-    side_eps = opening.at[6:8]
-    for ref, from_ref in zip((side_e, side_m), (side_e_in, side_m_in) if ending else (None, None)):
-        for j in range(2):
-            for c in range(3):
-                ref[c, j] = jnp.zeros(eps.shape[1:], jnp.float32) if from_ref is None else from_ref[c, j]
-    if not ending:
+    side_eps = opening.at[4:6]
+    reached = min(first - 1, STEPS + 1 - first)
+    for j in range(3):
         for c in range(3):
-            side_e[c, 2] = jnp.zeros(eps.shape[1:], jnp.float32)
-            side_m[c, 2] = jnp.zeros(eps.shape[1:], jnp.float32)
+            if j < reached:
+                side_e[c, j] = r["side_e_in"][c, j]
+                side_m[c, j] = r["side_m_in"][c, j]
+            elif first < STEPS:
+                side_e[c, j] = jnp.zeros(eps.shape[1:], jnp.float32)
+                side_m[c, j] = jnp.zeros(eps.shape[1:], jnp.float32)
 
     pending = []
 
     def put(src, dst):
-        copy = pltpu.make_async_copy(src, dst, sems.at[len(pending)])
+        copy = pltpu.make_async_copy(src, dst, r["sems"].at[len(pending)])
         copy.start()
         pending.append(copy)
 
@@ -254,7 +271,7 @@
         pending.clear()
         sums = None
         scale = role[1 if is_even else 2].astype(jnp.float32)
-        if not ending:
+        if first == 1:
             far = (opening[0], opening[1])
             if is_even:
                 far = past_near(far, elec_in)
@@ -262,13 +279,13 @@
             for p in range(count):
                 factor = factor * (COURANT * COURANT * eps[p])
             for k in range(2):
-                late[k] = factor * far[k]
+                r["late"][k] = factor * far[k]
         for step in steps:
             src_e, src_m = (elec_in, mag_in) if step == steps[0] else (elec, mag)
             near = (nears[2 * step - 2], nears[2 * step - 1])
             if step == STEPS:
-                near = (near[0] + late_in[0], near[1] + late_in[1])
-            ref, at = (opening, 2 * step - 2) if step < 4 else (msgs, 2 * step - 8)
+                near = (near[0] + r["late_in"][0], near[1] + r["late_in"][1])
+            ref, at = (opening if step < 3 else r["msgs"]), 2 * ((step - 1) % 2)
             far = (ref[at], ref[at + 1])
             if is_even:
                 beyond = near
@@ -281,7 +298,7 @@
                 nxt = (src_e[Y, p + 1], src_e[Z, p + 1]) if p < last else beyond
                 store(mag, p, magnetic_plane(planes(src_e, p), nxt, planes(src_m, p)))
             if step == STEPS:
-                put(mag, mag_out)
+                put(mag, r["mag_out"])
             if is_even:
                 beyond_left_electric(step, side_e, side_m, side_eps)
             else:
@@ -297,15 +314,15 @@
                     value = src_a[c, p] + waves[c // 3] * new[c % 3]
                     accum[c, p] = value
                     if step == STEPS:
-                        term = value * weights[c, p]
+                        term = value * r["weights"][c, p]
                         total = term if total is None else total + term
                 if step == STEPS:
-                    put(elec.at[:, p], elec_out.at[:, p])
-                    put(accum.at[:, p], accum_out.at[:, p])
-                    term = pillar_terms(total, high[p : p + 1], low[p], pillars.shape[0])
+                    put(elec.at[:, p], r["elec_out"].at[:, p])
+                    put(accum.at[:, p], r["accum_out"].at[:, p])
+                    term = pillar_terms(total, r["ids"][p : p + 1], r["pillars"].shape[0])
                     sums = term if sums is None else sums + term
         if ending:
-            pillars[...] = sums
+            r["pillars"][...] = sums
         for copy in pending:
             copy.wait()
 
@@ -313,19 +330,24 @@
     pl.when(jnp.logical_not(even))(functools.partial(run, False))
 
 
-def pillar_terms(total, high, low, owners):
+def pillar_terms(total, ids, owners):
     row = lax.dot_general(
         jnp.ones((8, total.shape[1]), jnp.float32), total, (((1,), (1,)), ((), ())),
         precision=lax.Precision.HIGHEST, preferred_element_type=jnp.float32,
     )[0:1]
-    label = lax.broadcasted_iota(jnp.int32, (owners, total.shape[0]), 0)
+    each = total.shape[0]
+    owner = lax.broadcasted_iota(jnp.int32, (owners, each), 0)
+    label = lax.broadcasted_iota(jnp.int32, (each, each), 0)
+    high = lax.div(ids, jnp.int32(each))
     return lax.dot_general(
-        jnp.where(label == high, row, 0.0), low, (((1,), (0,)), ((), ())),
+        jnp.where(owner == high, row, 0.0),
+        jnp.where(label == ids - each * high, 1.0, 0.0),
+        (((1,), (1,)), ((), ())),
         precision=lax.Precision.HIGHEST, preferred_element_type=jnp.float32,
     )
 
 
-def call(kernel, args, outs, scratch=(), smem=1, fast=(), slow_outs=0, copies=0):
+def call(kernel, args, outs, scratch=(), smem=1, fast=(), slow_outs=0, copies=0, slow=()):
     args = [
         pltpu.with_memory_space_constraint(a, pltpu.VMEM if i in fast else pltpu.HBM) if i >= smem else a
         for i, a in enumerate(args)
@@ -335,7 +357,7 @@
         out_shape=[
             shape_of(*o) if i < slow_outs else pltpu.VMEM(o, jnp.float32) for i, o in enumerate(outs)
         ],
-        in_specs=[SMEM] * smem + [VMEM] * (len(args) - smem),
+        in_specs=[SMEM if i < smem else HBM if i in slow else VMEM for i in range(len(args))],
         out_specs=[HBM] * slow_outs + [VMEM] * (len(outs) - slow_outs),
         scratch_shapes=[pltpu.VMEM(d, jnp.float32) for d in scratch]
         + [pltpu.SemaphoreType.DMA((copies,))] * (copies > 0),
@@ -348,18 +370,8 @@
     return jax.ShapeDtypeStruct(dims, jnp.float32)
 
 
-def halved(sums, axis):
-    size = lax.axis_size(axis)
-    me = lax.axis_index(axis)
-    bits = size.bit_length() - 1
-    block = sums
-    for bit in range(bits):
-        pair = block.reshape(-1, 2, block.shape[-1])
-        mine = (me >> bit) & 1
-        keep = jnp.where(mine == 0, pair[:, 0], pair[:, 1])
-        give = jnp.where(mine == 0, pair[:, 1], pair[:, 0])
-        block = keep + lax.ppermute(give, axis, [(i, i ^ (1 << bit)) for i in range(size)])
-    return block.reshape(-1)
+def summed(sums):
+    return jnp.sum(lax.all_to_all(sums, "gx", 0, 0, tiled=True), 0)
 
 
 def per_device(electric, magnetic, inv_eps, accum, forward, pillar_ids):
@@ -371,10 +383,6 @@
     inner = range(1, size - 1, 2)
     next_chip = [(i, i + 1) for i in inner] + [(i + 1, i) for i in inner]
 
-    per_owner = ny
-    high = pillar_ids // per_owner
-    low = (pillar_ids % per_owner)[:, :, None] == jnp.arange(per_owner, dtype=jnp.int32)
-    low = low.astype(jnp.float32)
     field, side = electric.shape, (3, 3, ny, nz)
 
     def to_mate(block):
@@ -384,35 +392,52 @@
         return lax.ppermute(block, "gx", next_chip)
 
     own = [role, electric, magnetic, inv_eps]
-    (opening,) = call(early_kernel, own, [(8, ny, nz)], scratch=[field, field])
+    opening, middle = call(
+        early_kernel, own, [(6, ny, nz), (4, ny, nz)], scratch=[field, field]
+    )
     opening = to_chip(opening)
+    middle = to_chip(middle)
     mate = [to_mate(electric), to_mate(magnetic), to_mate(inv_eps)]
-    later, nears = call(
+    ending, nears = call(
         closed_kernel,
         own + mate,
-        [(4, ny, nz), (2 * STEPS, ny, nz)],
+        [(2, ny, nz), (2 * STEPS, ny, nz)],
         scratch=[(3, 2 * count, ny, nz)] * 2,
         fast=(4, 5, 6),
     )
-    later = to_chip(later)
-    (weights,) = call(weights_kernel, [forward], [accum.shape], smem=0)
-    elec, mag, total, side_e, side_m, late = call(
-        functools.partial(open_kernel, (1, 2, 3)),
-        own + [nears, opening, accum],
-        [field, field, accum.shape, side, side, (2, ny, nz)],
-        fast=(4, 5),
+    ending = to_chip(ending)
+    weights, elec, mag, eps, total = call(
+        staging_kernel,
+        [forward, electric, magnetic, inv_eps, accum],
+        [accum.shape, field, field, inv_eps.shape, accum.shape],
+        smem=0,
+        slow=(1, 2, 3, 4),
+        copies=4,
+    )
+    kept = [field, field, accum.shape, side, side]
+    elec, mag, total, *sides, late = call(
+        functools.partial(open_kernel, (1, 2)),
+        [role, elec, mag, eps, nears, opening, total],
+        kept + [(2, ny, nz)],
+        fast=range(1, 7),
     )
     late = to_mate(late)
+    elec, mag, total, *sides = call(
+        functools.partial(open_kernel, (3, 4)),
+        [role, elec, mag, eps, nears, opening, total, middle, *sides],
+        kept,
+        fast=range(1, 10),
+    )
     electric, magnetic, accum, sums = call(
-        functools.partial(open_kernel, (4, 5)),
-        [role, elec, mag, inv_eps, nears, opening, later, total, late, side_e, side_m, weights, high, low],
-        [field, field, accum.shape, (size, per_owner)],
-        scratch=[field, field, accum.shape, side, side],
-        fast=(1, 2, *range(4, 12)),
+        functools.partial(open_kernel, (5,)),
+        [role, elec, mag, eps, nears, opening, total, ending, *sides, late, weights, pillar_ids],
+        [field, field, accum.shape, (size, ny)],
+        scratch=kept,
+        fast=range(1, 12),
         slow_outs=3,
         copies=1 + 2 * count,
     )
-    return electric, magnetic, accum, halved(sums, "gx")
+    return electric, magnetic, accum, summed(sums)
 
 
 def solution(mesh):

time: 47.5 us -> 42.7 us (0.90)
  blocking collectives: 0 us -> 12.3 us
  starting transfers between devices: 20.5 us -> 11.5 us
  waiting for transfers between devices: 6.77 us -> 0.02 us
  other arithmetic: 2.06 us -> 0.62 us
    all_to_all x0 -> x1, blocking collectives: none -> 12.3 us  [summed(): return jnp.sum(lax.all_to_all(sums, 'gx', 0, 0, tiled=True), 0)]
    ppermute x4 -> x0, starting transfers between devices: 11.2 us -> none  [halved(): lax.ppermute(give, axis, [(i, i ^ 1 << bit) for i in range(size)])]
    ppermute x4 -> x0, waiting for transfers between devices: 5.46 us -> none  [halved(): lax.ppermute(give, axis, [(i, i ^ 1 << bit) for i in range(size)])]
    ppermute x4, starting transfers between devices: 7.97 us -> 9.5 us  [to_mate(): return lax.ppermute(block, 'gx', same_chip)]
    ppermute x4, waiting for transfers between devices: 1.31 us -> 0.01 us  [to_mate(): return lax.ppermute(block, 'gx', same_chip)]
    convert_element_type x1 -> x0, other arithmetic: 0.84 us -> none  [per_device(): low = low.astype(jnp.float32)]
    ppermute x2 -> x3, starting transfers between devices: 1.36 us -> 2.02 us  [to_chip(): return lax.ppermute(block, 'gx', next_chip)]
    select_n x3 -> x0, other arithmetic: 0.6 us -> none  [the longest x1 0.58 us: per_device(): pillar_ids % per_owner]
  transfers between devices with their start and end apart: 10 -> 7, of which waited for: 6 -> 0; matrix products, arithmetic and copies ran while one was open for 3% -> 0% of each run, Pallas kernels for 27% -> 33%
where the time goes in v4:
time: 42.7 us; the launch traced here: 42.4 us
  Pallas kernels  17.2 us (40%)
  blocking collectives  12.3 us (29%)
  starting transfers between devices  11.5 us (27%)
  between operations  0.77 us (2%)
  other arithmetic  0.62 us (1%)
    pallas_call x6, Pallas kernels, call(): pl.pallas_call(kernel, out_shape=[shape_of(*o) if i < slow_outs else pltp...  17.2 us
    all_to_all x1, blocking collectives, summed(): return jnp.sum(lax.all_to_all(sums, 'gx', 0, 0, tiled=True), 0)  12.3 us
    ppermute x4, starting transfers between devices, to_mate(): return lax.ppermute(block, 'gx', same_chip)  9.5 us
    ppermute x3, starting transfers between devices, to_chip(): return lax.ppermute(block, 'gx', next_chip)  2.02 us
  transfers between devices with their start and end apart: 7, of which 0 were waited for; matrix products, arithmetic and copies ran while one was open for 0% of the time, Pallas kernels for 33%

profile of v4, /device:TPU:0, one launch (start us, length us, event | category | flops | bytes accessed | tf_op | source)
XLA Modules:
  0.0 42.4 jit_solution(3448909541346248846)
XLA Ops:
  0.6 0.0 copy-start
  0.6 0.5 %collective-permute-start = (f32[3,4,128,128]{3,2,1,0:T(8,128)}, f32[3,4,128,128]{3,2,1,0:T(8,128)S(1)}, u32[]{:S(2)}, u32[]{:S(2)}) collective-permute-start(f32[3,4,128,128]{3,2,1,0:T(8,128)} %own_e.3), channel_id=1, source_target_pairs={{0,1},{1,0},{2,3},{3,2},{4,5},{5,4},{6,7},{7,6},{8,9},{9,8},{10,11... | collective-permute-start | bytes 2359304 | tf_op jit(solution)/shard_map/ppermute | solution.py:389
  1.2 0.1 collective-permute-start.1
  1.2 0.1 pad_add_fusion.role.refs_0_
  1.3 2.1 %shard_map.95 = (f32[6,128,128]{2,1,0:T(8,128)S(1)}, f32[4,128,128]{2,1,0:T(8,128)S(1)}) custom-call(s32[3]{0:T(128)S(1)} %pad_add_fusion.role.refs_0_, f32[3,4,128,128]{3,2,1,0:T(8,128)} %own_e.3, f32[3,4,128,128]{3,2,1,0:T(8,128)} %own_m.3, f32[4,128,128]{2,1,0:T(8,128)} %own_eps.3), custom_call_target="tpu_custom_call" | custom-call | flops 1 | bytes 1 | tf_op jit(solution)/shard_map/pallas_call | solution.py:355
  3.4 0.7 %collective-permute-start.3 = (f32[6,128,128]{2,1,0:T(8,128)S(1)}, f32[6,128,128]{2,1,0:T(8,128)S(1)}, u32[]{:S(2)}, u32[]{:S(2)}) collective-permute-start(f32[6,128,128]{2,1,0:T(8,128)S(1)} %get-tuple-element.32), channel_id=1, source_target_pairs={{1,2},{3,4},{5,6},{7,8},{9,10},{11,12},{13,14},{2,1},{4,3},{6,5},{... | collective-permute-start | bytes 1179656 | tf_op jit(solution)/shard_map/ppermute | solution.py:392
  4.1 0.0 copy-done
  4.1 4.3 %collective-permute-start.2 = (f32[4,128,128]{2,1,0:T(8,128)S(1)}, f32[4,128,128]{2,1,0:T(8,128)S(1)}, u32[]{:S(2)}, u32[]{:S(2)}) collective-permute-start(f32[4,128,128]{2,1,0:T(8,128)S(1)} %copy-done), channel_id=1, source_target_pairs={{0,1},{1,0},{2,3},{3,2},{4,5},{5,4},{6,7},{7,6},{8,9},{9,8},{10,11... | collective-permute-start | bytes 786440 | tf_op jit(solution)/shard_map/ppermute | solution.py:389
  8.5 0.7 %collective-permute-start.4 = (f32[4,128,128]{2,1,0:T(8,128)S(1)}, f32[4,128,128]{2,1,0:T(8,128)S(1)}, u32[]{:S(2)}, u32[]{:S(2)}) collective-permute-start(f32[4,128,128]{2,1,0:T(8,128)S(1)} %get-tuple-element.37), channel_id=1, source_target_pairs={{1,2},{3,4},{5,6},{7,8},{9,10},{11,12},{13,14},{2,1},{4,3},{6,5},{... | collective-permute-start | bytes 786440 | tf_op jit(solution)/shard_map/ppermute | solution.py:392
  9.2 3.1 %shard_map.93 = (f32[6,4,128,128]{3,2,1,0:T(8,128)S(1)}, f32[3,4,128,128]{3,2,1,0:T(8,128)S(1)}, f32[3,4,128,128]{3,2,1,0:T(8,128)S(1)}, f32[4,128,128]{2,1,0:T(8,128)S(1)}, f32[6,4,128,128]{3,2,1,0:T(8,128)S(1)}) custom-call(f32[6,32,4,128]{3,2,1,0:T(4,128)} %forward.1, f32[3,4,128,128]{3,2,1,0:T(8,128)} %own_e.3, f32[3,4,128,128]{3,2,1,0:T(8,128)} %own_m.3, ...), custom_call_target="tpu_custom_call" | custom-call | flops 1 | bytes 1 | tf_op jit(solution)/shard_map/pallas_call | solution.py:355
  12.3 0.0 collective-permute-done.2.mate_eps
  12.3 0.0 collective-permute-done.mate_e
  12.3 0.0 collective-permute-done.1.mate_m
  12.3 3.9 %shard_map.94 = (f32[2,128,128]{2,1,0:T(8,128)S(1)}, f32[10,128,128]{2,1,0:T(8,128)S(1)}) custom-call(s32[3]{0:T(128)S(1)} %pad_add_fusion.role.refs_0_, f32[3,4,128,128]{3,2,1,0:T(8,128)} %own_e.3, f32[3,4,128,128]{3,2,1,0:T(8,128)} %own_m.3, f32[4,128,128]{2,1,0:T(8,128)} %own_eps.3, f32[3,4,128,128]{3,2,1,0:T(8,128)S(1)} %collective-permute-done.mate_e, ...), custom_call_target="tpu_custom_call" | custom-call | flops 1 | bytes 1 | tf_op jit(solution)/shard_map/pallas_call | solution.py:355
  16.2 0.7 %collective-permute-start.5 = (f32[2,128,128]{2,1,0:T(8,128)S(1)}, f32[2,128,128]{2,1,0:T(8,128)S(1)}, u32[]{:S(2)}, u32[]{:S(2)}) collective-permute-start(f32[2,128,128]{2,1,0:T(8,128)S(1)} %get-tuple-element.43), channel_id=1, source_target_pairs={{1,2},{3,4},{5,6},{7,8},{9,10},{11,12},{13,14},{2,1},{4,3},{6,5},{... | collective-permute-start | bytes 393224 | tf_op jit(solution)/shard_map/ppermute | solution.py:392
  16.9 0.0 collective-permute-done.3.refs_5_
  16.9 2.2 %shard_map.96 = (f32[3,4,128,128]{3,2,1,0:T(8,128)S(1)}, f32[3,4,128,128]{3,2,1,0:T(8,128)S(1)}, f32[6,4,128,128]{3,2,1,0:T(8,128)S(1)}, f32[3,3,128,128]{3,2,1,...) custom-call(s32[3]{0:T(128)S(1)} %pad_add_fusion.role.refs_0_, ...), custom_call_target="tpu_custom_call" | custom-call | flops 1 | bytes 1 | tf_op jit(solution)/shard_map/pallas_call | solution.py:355
  19.2 4.6 %collective-permute-start.6 = (f32[2,128,128]{2,1,0:T(8,128)S(1)}, f32[2,128,128]{2,1,0:T(8,128)S(1)}, u32[]{:S(2)}, u32[]{:S(2)}) collective-permute-start(f32[2,128,128]{2,1,0:T(8,128)S(1)} %get-tuple-element.46), channel_id=1, source_target_pairs={{0,1},{1,0},{2,3},{3,2},{4,5},{5,4},{6,7},{7,6},{8,9},{9,8},{10,11... | collective-permute-start | bytes 393224 | tf_op jit(solution)/shard_map/ppermute | solution.py:389
  23.7 0.0 collective-permute-done.4.refs_7_
  23.7 2.6 %shard_map.97 = (f32[3,4,128,128]{3,2,1,0:T(8,128)S(1)}, f32[3,4,128,128]{3,2,1,0:T(8,128)S(1)}, f32[6,4,128,128]{3,2,1,0:T(8,128)S(1)}, f32[3,3,128,128]{3,2,1,0:T(8,128)S(1)}, f32[3,3,128,128]{3,2,1,0:T(8,128)S(1)}) custom-call(s32[3]{0:T(128)S(1)} %pad_add_fusion.role.refs_0_, f32[3,4,128,128]{3,2,1,0:T(8,128)S(1)} %get-tuple-element.34.refs_1_, ...), custom_call_target="tpu_custom_call" | custom-call | flops 1 | bytes 1 | tf_op jit(solution)/shard_map/pallas_call | solution.py:355
  26.3 0.0 collective-permute-done.5.refs_7_
  26.4 0.0 collective-permute-done.6.refs_10_
  26.4 3.2 %shard_map.98 = (f32[3,4,128,128]{3,2,1,0:T(8,128)}, f32[3,4,128,128]{3,2,1,0:T(8,128)}, f32[6,4,128,128]{3,2,1,0:T(8,128)}, f32[16,128]{1,0:T(8,128)S(1)}) custom-call(s32[3]{0:T(128)S(1)} %pad_add_fusion.role.refs_0_, f32[3,4,128,128]{3,2,1,0:T(8,128)S(1)} %get-tuple-element.40.refs_1_, f32[3,4,128,128]{3,2,1,0:T(8,128)S(1)} %get-tuple-element.41.refs_2_, ...), custom_call_target="tpu_custom_call" | custom-call | flops 1 | bytes 1 | tf_op jit(solution)/shard_map/pallas_call | solution.py:355
  29.5 12.3 %all_to_all.9 = f32[16,1,128]{2,1,0:T(1,128)S(1)} all-to-all(f32[16,1,128]{2,1,0:T(1,128)S(1)} %bitcast.6), channel_id=1, replica_groups=mesh['design'=2,'gx'=16] {'gx'}, dimensions={0} | all-to-all | bytes 16384 | tf_op jit(solution)/shard_map/all_to_all | solution.py:374
  41.9 0.5 %reduce_sum.9 = f32[128]{0:T(128)} reduce(f32[16,1,128]{2,1,0:T(1,128)S(1)} %all_to_all.9, f32[]{:T(128)} %constant.22.clone.1), dimensions={0,1}, to_apply=%region_0.1 | reduce | flops 1920 | bytes 8708 | tf_op jit(solution)/shard_map/reduce_sum | solution.py:374
Async XLA Ops:
  0.6 3.5 %copy-start = (f32[4,128,128]{2,1,0:T(8,128)S(1)}, f32[4,128,128]{2,1,0:T(8,128)}, u32[]{:S(2)}) copy-start(f32[4,128,128]{2,1,0:T(8,128)} %own_eps.3) | copy-start | bytes 786436
  0.6 11.7 %collective-permute-start = (f32[3,4,128,128]{3,2,1,0:T(8,128)}, f32[3,4,128,128]{3,2,1,0:T(8,128)S(1)}, u32[]{:S(2)}, u32[]{:S(2)}) collective-permute-start(f32[3,4,128,128]{3,2,1,0:T(8,128)} %own_e.3), channel_id=1, source_target_pairs={{0,1},{1,0},{2,3},{3,2},{4,5},{5,4},{6,7},{7,6},{8,9},{9,8},{10,11... | collective-permute-start | bytes 2359304 | tf_op jit(solution)/shard_map/ppermute | solution.py:389
  1.2 11.2 %collective-permute-start.1 = (f32[3,4,128,128]{3,2,1,0:T(8,128)}, f32[3,4,128,128]{3,2,1,0:T(8,128)S(1)}, u32[]{:S(2)}, u32[]{:S(2)}) collective-permute-start(f32[3,4,128,128]{3,2,1,0:T(8,128)} %own_m.3), channel_id=1, source_target_pairs={{0,1},{1,0},{2,3},{3,2},{4,5},{5,4},{6,7},{7,6},{8,9},{9,8},{10,11... | collective-permute-start | bytes 2359304 | tf_op jit(solution)/shard_map/ppermute | solution.py:389
  3.4 13.5 %collective-permute-start.3 = (f32[6,128,128]{2,1,0:T(8,128)S(1)}, f32[6,128,128]{2,1,0:T(8,128)S(1)}, u32[]{:S(2)}, u32[]{:S(2)}) collective-permute-start(f32[6,128,128]{2,1,0:T(8,128)S(1)} %get-tuple-element.32), channel_id=1, source_target_pairs={{1,2},{3,4},{5,6},{7,8},{9,10},{11,12},{13,14},{2,1},{4,3},{6,5},{... | collective-permute-start | bytes 1179656 | tf_op jit(solution)/shard_map/ppermute | solution.py:392
  4.1 8.2 %collective-permute-start.2 = (f32[4,128,128]{2,1,0:T(8,128)S(1)}, f32[4,128,128]{2,1,0:T(8,128)S(1)}, u32[]{:S(2)}, u32[]{:S(2)}) collective-permute-start(f32[4,128,128]{2,1,0:T(8,128)S(1)} %copy-done), channel_id=1, source_target_pairs={{0,1},{1,0},{2,3},{3,2},{4,5},{5,4},{6,7},{7,6},{8,9},{9,8},{10,11... | collective-permute-start | bytes 786440 | tf_op jit(solution)/shard_map/ppermute | solution.py:389
  8.5 15.2 %collective-permute-start.4 = (f32[4,128,128]{2,1,0:T(8,128)S(1)}, f32[4,128,128]{2,1,0:T(8,128)S(1)}, u32[]{:S(2)}, u32[]{:S(2)}) collective-permute-start(f32[4,128,128]{2,1,0:T(8,128)S(1)} %get-tuple-element.37), channel_id=1, source_target_pairs={{1,2},{3,4},{5,6},{7,8},{9,10},{11,12},{13,14},{2,1},{4,3},{6,5},{... | collective-permute-start | bytes 786440 | tf_op jit(solution)/shard_map/ppermute | solution.py:392
  16.2 10.1 %collective-permute-start.5 = (f32[2,128,128]{2,1,0:T(8,128)S(1)}, f32[2,128,128]{2,1,0:T(8,128)S(1)}, u32[]{:S(2)}, u32[]{:S(2)}) collective-permute-start(f32[2,128,128]{2,1,0:T(8,128)S(1)} %get-tuple-element.43), channel_id=1, source_target_pairs={{1,2},{3,4},{5,6},{7,8},{9,10},{11,12},{13,14},{2,1},{4,3},{6,5},{... | collective-permute-start | bytes 393224 | tf_op jit(solution)/shard_map/ppermute | solution.py:392
  19.2 7.2 %collective-permute-start.6 = (f32[2,128,128]{2,1,0:T(8,128)S(1)}, f32[2,128,128]{2,1,0:T(8,128)S(1)}, u32[]{:S(2)}, u32[]{:S(2)}) collective-permute-start(f32[2,128,128]{2,1,0:T(8,128)S(1)} %get-tuple-element.46), channel_id=1, source_target_pairs={{0,1},{1,0},{2,3},{3,2},{4,5},{5,4},{6,7},{7,6},{8,9},{9,8},{10,11... | collective-permute-start | bytes 393224 | tf_op jit(solution)/shard_map/ppermute | solution.py:389

commit v5 on v4

--- a/solution.py
+++ b/solution.py
@@ -79,6 +79,10 @@
         elec[step - 1] |= {p + 1 for p in mag[step] if p + 1 < count}
         mag[step - 1] = set(mag.get(step - 1, ())) | mag[step]
     return mag, elec
+
+
+def parts(block):
+    return block.at[0:3], block.at[3:6], block.at[6]
 
 
 def early_kernel(role, own_e, own_m, own_eps, msg_a, msg_b, elec, mag):
@@ -120,7 +124,17 @@
     pl.when(jnp.logical_not(even))(functools.partial(run, False))
 
 
-def closed_kernel(role, own_e, own_m, own_eps, mate_e, mate_m, mate_eps, msg, nears, elec, mag):
+def closed_kernel(role, mate_e, mate_m, mate_eps, *refs):
+    sources, (block, msg, nears, weights, total, elec, mag, forward, sems) = refs[:5], refs[5:]
+    own_e, own_m, own_eps = parts(block)
+    copies = [
+        pltpu.make_async_copy(src, dst, sems.at[i])
+        for i, (src, dst) in enumerate(zip(sources, (own_e, own_m, own_eps, forward, total)))
+    ]
+    for copy in copies:
+        copy.start()
+    for copy in copies[:3]:
+        copy.wait()
     half = own_e.shape[1]
     count = 2 * half
     even = role[0] == 0
@@ -177,20 +191,16 @@
 
     pl.when(even)(functools.partial(run, True))
     pl.when(jnp.logical_not(even))(functools.partial(run, False))
+    copies[3].wait()
+    lay_out(forward, weights)
+    copies[4].wait()
 
 
 def past_near(near, elec):
     return (near[0] + COURANT * elec[Z, 0], near[1] - COURANT * elec[Y, 0])
 
 
-def staging_kernel(forward, *refs):
-    half = (len(refs) - 2) // 2
-    sems, weights = refs[-1], refs[half]
-    copies = [
-        pltpu.make_async_copy(refs[i], refs[half + 1 + i], sems.at[i]) for i in range(half)
-    ]
-    for copy in copies:
-        copy.start()
+def lay_out(forward, weights):
     depth, count, ny = forward.shape[1:]
     nz = weights.shape[3]
     blank = jnp.zeros(((nz - depth) // 2, ny), jnp.float32)
@@ -198,8 +208,6 @@
         for c in range(6):
             slab = forward[c, :, p, :] * (SENS_SCALE if c < 3 else -SENS_SCALE)
             weights[c, p] = jnp.transpose(jnp.concatenate([blank, slab, blank], 0))
-    for copy in copies:
-        copy.wait()
 
 
 LEFT_MAG = {1: 1, 2: 2, 3: 3, 4: 2, 5: 1}
@@ -237,14 +245,17 @@
 
 def open_kernel(steps, *refs):
     first, ending = steps[0], steps[-1] == STEPS
-    names = ["role", "elec_in", "mag_in", "eps", "nears", "opening", "accum_in"]
-    names += ["msgs", "side_e_in", "side_m_in"] * (first > 1)
+    names = ["role", "block", "nears", "opening", "accum_in"]
+    names += ["elec_in", "mag_in", "msgs", "side_e_in", "side_m_in"] * (first > 1)
     names += ["late_in", "weights", "ids"] * ending
     names += ["elec_out", "mag_out", "accum_out", "pillars"] * ending
     names += ["elec", "mag", "accum", "side_e", "side_m"]
     names += ["late"] * (first == 1) + ["sems"] * ending
     r = dict(zip(names, refs, strict=True))
-    role, elec_in, mag_in, eps, nears, opening, accum_in = refs[:7]
+    role, block, nears, opening, accum_in = refs[:5]
+    elec_in, mag_in, eps = parts(block)
+    if first > 1:
+        elec_in, mag_in = r["elec_in"], r["mag_in"]
     elec, mag, accum, side_e, side_m = (r[n] for n in ("elec", "mag", "accum", "side_e", "side_m"))
     count = eps.shape[0]
     last = count - 1
@@ -269,7 +280,7 @@
 
     def run(is_even):
         pending.clear()
-        sums = None
+        totals = []
         scale = role[1 if is_even else 2].astype(jnp.float32)
         if first == 1:
             far = (opening[0], opening[1])
@@ -294,35 +305,43 @@
             else:
                 beyond = ((far[0] + side_e[Y, 0]) * scale, (far[1] + side_e[Z, 0]) * scale)
                 past0 = past_near(near, src_e)
-            for p in range(count):
+            waves = (math.cos(ANGULAR * step), math.sin(ANGULAR * step))
+            src_a = accum_in if step == steps[0] else accum
+
+            def magnetic_at(p):
                 nxt = (src_e[Y, p + 1], src_e[Z, p + 1]) if p < last else beyond
                 store(mag, p, magnetic_plane(planes(src_e, p), nxt, planes(src_m, p)))
-            if step == STEPS:
-                put(mag, r["mag_out"])
-            if is_even:
-                beyond_left_electric(step, side_e, side_m, side_eps)
-            else:
-                beyond_right(step, mag, side_e, side_m, side_eps, last)
-            waves = (math.cos(ANGULAR * step), math.sin(ANGULAR * step))
-            src_a = accum_in if step == steps[0] else accum
-            for p in range(count):
+
+            def electric_at(p):
                 past = (mag[Y, p - 1], mag[Z, p - 1]) if p else past0
                 new = electric_plane(planes(mag, p), past, planes(src_e, p), eps[p])
                 store(elec, p, new)
-                total = None
                 for c in range(6):
-                    value = src_a[c, p] + waves[c // 3] * new[c % 3]
-                    accum[c, p] = value
-                    if step == STEPS:
-                        term = value * r["weights"][c, p]
-                        total = term if total is None else total + term
-                if step == STEPS:
-                    put(elec.at[:, p], r["elec_out"].at[:, p])
-                    put(accum.at[:, p], r["accum_out"].at[:, p])
-                    term = pillar_terms(total, r["ids"][p : p + 1], r["pillars"].shape[0])
-                    sums = term if sums is None else sums + term
+                    accum[c, p] = src_a[c, p] + waves[c // 3] * new[c % 3]
+
+            if step < STEPS:
+                for p in range(count):
+                    magnetic_at(p)
+                if is_even:
+                    beyond_left_electric(step, side_e, side_m, side_eps)
+                else:
+                    beyond_right(step, mag, side_e, side_m, side_eps, last)
+                for p in range(count):
+                    electric_at(p)
+                continue
+            for p in range(count):
+                magnetic_at(p)
+                put(mag.at[:, p], r["mag_out"].at[:, p])
+                electric_at(p)
+                put(elec.at[:, p], r["elec_out"].at[:, p])
+                put(accum.at[:, p], r["accum_out"].at[:, p])
+            for p in range(count):
+                total = accum[0, p] * r["weights"][0, p]
+                for c in range(1, 6):
+                    total = total + accum[c, p] * r["weights"][c, p]
+                totals.append(total)
         if ending:
-            r["pillars"][...] = sums
+            r["pillars"][...] = pillar_terms(totals, r["ids"], r["pillars"].shape[0])
         for copy in pending:
             copy.wait()
 
@@ -330,14 +349,15 @@
     pl.when(jnp.logical_not(even))(functools.partial(run, False))
 
 
-def pillar_terms(total, ids, owners):
+def pillar_terms(totals, ids, owners):
     row = lax.dot_general(
-        jnp.ones((8, total.shape[1]), jnp.float32), total, (((1,), (1,)), ((), ())),
+        jnp.ones((8, totals[0].shape[1]), jnp.float32), jnp.concatenate(totals, 0), (((1,), (1,)), ((), ())),
         precision=lax.Precision.HIGHEST, preferred_element_type=jnp.float32,
     )[0:1]
-    each = total.shape[0]
-    owner = lax.broadcasted_iota(jnp.int32, (owners, each), 0)
-    label = lax.broadcasted_iota(jnp.int32, (each, each), 0)
+    each = totals[0].shape[0]
+    ids = jnp.concatenate([ids[p : p + 1] for p in range(len(totals))], 1)
+    owner = lax.broadcasted_iota(jnp.int32, (owners, ids.shape[1]), 0)
+    label = lax.broadcasted_iota(jnp.int32, (each, ids.shape[1]), 0)
     high = lax.div(ids, jnp.int32(each))
     return lax.dot_general(
         jnp.where(owner == high, row, 0.0),
@@ -391,51 +411,47 @@
     def to_chip(block):
         return lax.ppermute(block, "gx", next_chip)
 
-    own = [role, electric, magnetic, inv_eps]
     opening, middle = call(
-        early_kernel, own, [(6, ny, nz), (4, ny, nz)], scratch=[field, field]
+        early_kernel,
+        [role, electric, magnetic, inv_eps],
+        [(6, ny, nz), (4, ny, nz)],
+        scratch=[field, field],
     )
     opening = to_chip(opening)
     middle = to_chip(middle)
     mate = [to_mate(electric), to_mate(magnetic), to_mate(inv_eps)]
-    ending, nears = call(
+    block, ending, nears, weights, total = call(
         closed_kernel,
-        own + mate,
-        [(2, ny, nz), (2 * STEPS, ny, nz)],
-        scratch=[(3, 2 * count, ny, nz)] * 2,
-        fast=(4, 5, 6),
+        [role, *mate, electric, magnetic, inv_eps, forward, accum],
+        [(7, *inv_eps.shape), (2, ny, nz), (2 * STEPS, ny, nz), accum.shape, accum.shape],
+        scratch=[(3, 2 * count, ny, nz)] * 2 + [forward.shape],
+        fast=(1, 2, 3),
+        slow=range(4, 9),
+        copies=5,
     )
     ending = to_chip(ending)
-    weights, elec, mag, eps, total = call(
-        staging_kernel,
-        [forward, electric, magnetic, inv_eps, accum],
-        [accum.shape, field, field, inv_eps.shape, accum.shape],
-        smem=0,
-        slow=(1, 2, 3, 4),
-        copies=4,
-    )
     kept = [field, field, accum.shape, side, side]
     elec, mag, total, *sides, late = call(
         functools.partial(open_kernel, (1, 2)),
-        [role, elec, mag, eps, nears, opening, total],
+        [role, block, nears, opening, total],
         kept + [(2, ny, nz)],
-        fast=range(1, 7),
+        fast=range(1, 5),
     )
     late = to_mate(late)
     elec, mag, total, *sides = call(
         functools.partial(open_kernel, (3, 4)),
-        [role, elec, mag, eps, nears, opening, total, middle, *sides],
+        [role, block, nears, opening, total, elec, mag, middle, *sides],
         kept,
         fast=range(1, 10),
     )
     electric, magnetic, accum, sums = call(
         functools.partial(open_kernel, (5,)),
-        [role, elec, mag, eps, nears, opening, total, ending, *sides, late, weights, pillar_ids],
+        [role, block, nears, opening, total, elec, mag, ending, *sides, late, weights, pillar_ids],
         [field, field, accum.shape, (size, ny)],
         scratch=kept,
         fast=range(1, 12),
         slow_outs=3,
-        copies=1 + 2 * count,
+        copies=3 * count,
     )
     return electric, magnetic, accum, summed(sums)
 

time: 42.7 us -> 42.4 us (level)
  Pallas kernels: 17.2 us -> 14.7 us
  blocking collectives: 12.3 us -> 14 us
  waiting for transfers between devices: 0.02 us -> 0.5 us
    pallas_call x6 -> x5, Pallas kernels: 17.2 us -> 14.7 us  [call(): pl.pallas_call(kernel, out_shape=[shape_of(*o) if i < slow_outs else pltp...]
    all_to_all x1, blocking collectives: 12.3 us -> 14 us  [summed(): return jnp.sum(lax.all_to_all(sums, 'gx', 0, 0, tiled=True), 0)]
    ppermute x4, waiting for transfers between devices: 0.01 us -> 0.5 us  [to_mate(): return lax.ppermute(block, 'gx', same_chip)]
  transfers between devices with their start and end apart: 7 -> 7, of which waited for: 0 -> 1; matrix products, arithmetic and copies ran while one was open for 0% -> 0% of each run, Pallas kernels for 33% -> 28%
where the time goes in v5:
time: 42.4 us; the launch traced here: 42.2 us
  Pallas kernels  14.7 us (35%)
  blocking collectives  14 us (33%)
  starting transfers between devices  11.6 us (27%)
  between operations  0.74 us (2%)
  other arithmetic  0.62 us (1%)
  waiting for transfers between devices  0.5 us (1%)
    pallas_call x5, Pallas kernels, call(): pl.pallas_call(kernel, out_shape=[shape_of(*o) if i < slow_outs else pltp...  14.7 us
    all_to_all x1, blocking collectives, summed(): return jnp.sum(lax.all_to_all(sums, 'gx', 0, 0, tiled=True), 0)  14 us
    ppermute x4, starting transfers between devices, to_mate(): return lax.ppermute(block, 'gx', same_chip)  9.6 us
    ppermute x3, starting transfers between devices, to_chip(): return lax.ppermute(block, 'gx', next_chip)  2.02 us
  transfers between devices with their start and end apart: 7, of which 1 were waited for; matrix products, arithmetic and copies ran while one was open for 0% of the time, Pallas kernels for 28%

profile of v5, /device:TPU:0, one launch (start us, length us, event | category | flops | bytes accessed | tf_op | source)
XLA Modules:
  0.0 42.2 jit_solution(10515815935997489178)
XLA Ops:
  0.6 0.0 copy-start
  0.6 0.5 %collective-permute-start = (f32[3,4,128,128]{3,2,1,0:T(8,128)}, f32[3,4,128,128]{3,2,1,0:T(8,128)S(1)}, u32[]{:S(2)}, u32[]{:S(2)}) collective-permute-start(f32[3,4,128,128]{3,2,1,0:T(8,128)} %own_e.1), channel_id=1, source_target_pairs={{0,1},{1,0},{2,3},{3,2},{4,5},{5,4},{6,7},{7,6},{8,9},{9,8},{10,11... | collective-permute-start | bytes 2359304 | tf_op jit(solution)/shard_map/ppermute | solution.py:409
  1.2 0.1 collective-permute-start.1
  1.2 0.1 pad_add_fusion.role.refs_0_
  1.3 2.1 %shard_map.94 = (f32[6,128,128]{2,1,0:T(8,128)S(1)}, f32[4,128,128]{2,1,0:T(8,128)S(1)}) custom-call(s32[3]{0:T(128)S(1)} %pad_add_fusion.role.refs_0_, f32[3,4,128,128]{3,2,1,0:T(8,128)} %own_e.1, f32[3,4,128,128]{3,2,1,0:T(8,128)} %own_m.1, f32[4,128,128]{2,1,0:T(8,128)} %own_eps.1), custom_call_target="tpu_custom_call" | custom-call | flops 1 | bytes 1 | tf_op jit(solution)/shard_map/pallas_call | solution.py:375
  3.4 0.7 %collective-permute-start.3 = (f32[6,128,128]{2,1,0:T(8,128)S(1)}, f32[6,128,128]{2,1,0:T(8,128)S(1)}, u32[]{:S(2)}, u32[]{:S(2)}) collective-permute-start(f32[6,128,128]{2,1,0:T(8,128)S(1)} %get-tuple-element.28), channel_id=1, source_target_pairs={{1,2},{3,4},{5,6},{7,8},{9,10},{11,12},{13,14},{2,1},{4,3},{6,5},{... | collective-permute-start | bytes 1179656 | tf_op jit(solution)/shard_map/ppermute | solution.py:412
  4.1 0.0 copy-done
  4.1 4.3 %collective-permute-start.2 = (f32[4,128,128]{2,1,0:T(8,128)S(1)}, f32[4,128,128]{2,1,0:T(8,128)S(1)}, u32[]{:S(2)}, u32[]{:S(2)}) collective-permute-start(f32[4,128,128]{2,1,0:T(8,128)S(1)} %copy-done), channel_id=1, source_target_pairs={{0,1},{1,0},{2,3},{3,2},{4,5},{5,4},{6,7},{7,6},{8,9},{9,8},{10,11... | collective-permute-start | bytes 786440 | tf_op jit(solution)/shard_map/ppermute | solution.py:409
  8.5 0.7 %collective-permute-start.4 = (f32[4,128,128]{2,1,0:T(8,128)S(1)}, f32[4,128,128]{2,1,0:T(8,128)S(1)}, u32[]{:S(2)}, u32[]{:S(2)}) collective-permute-start(f32[4,128,128]{2,1,0:T(8,128)S(1)} %get-tuple-element.33), channel_id=1, source_target_pairs={{1,2},{3,4},{5,6},{7,8},{9,10},{11,12},{13,14},{2,1},{4,3},{6,5},{... | collective-permute-start | bytes 786440 | tf_op jit(solution)/shard_map/ppermute | solution.py:412
  9.2 0.5 %collective-permute-done.2.mate_eps = f32[4,128,128]{2,1,0:T(8,128)S(1)} collective-permute-done((f32[4,128,128]{2,1,0:T(8,128)S(1)}, f32[4,128,128]{2,1,0:T(8,128)S(1)}, u32[]{:S(2)}, u32[]{:S(2)}) %collective-permute-start.2) | collective-permute-done | bytes 262176 | tf_op jit(solution)/shard_map/ppermute | solution.py:409
  9.7 0.0 collective-permute-done.mate_e
  9.7 0.0 collective-permute-done.1.mate_m
  9.7 5.1 %shard_map.93 = (f32[7,4,128,128]{3,2,1,0:T(8,128)S(1)}, f32[2,128,128]{2,1,0:T(8,128)S(1)}, f32[10,128,128]{2,1,0:T(8,128)S(1)}, f32[6,4,128,128]{3,2,1,0:T(8,128)S(1)}, f32[6,4,128,128]{3,2,1,0:T(8,128)S(1)}) custom-call(s32[3]{0:T(128)S(1)} %pad_add_fusion.role.refs_0_, f32[3,4,128,128]{3,2,1,0:T(8,128)S(1)} %collective-permute-done.mate_e, ...), custom_call_target="tpu_custom_call" | custom-call | flops 1 | bytes 1 | tf_op jit(solution)/shard_map/pallas_call | solution.py:375
  14.8 0.7 %collective-permute-start.5 = (f32[2,128,128]{2,1,0:T(8,128)S(1)}, f32[2,128,128]{2,1,0:T(8,128)S(1)}, u32[]{:S(2)}, u32[]{:S(2)}) collective-permute-start(f32[2,128,128]{2,1,0:T(8,128)S(1)} %get-tuple-element.39), channel_id=1, source_target_pairs={{1,2},{3,4},{5,6},{7,8},{9,10},{11,12},{13,14},{2,1},{4,3},{6,5},{... | collective-permute-start | bytes 393224 | tf_op jit(solution)/shard_map/ppermute | solution.py:412
  15.5 0.0 collective-permute-done.3.refs_3_
  15.5 2.2 %shard_map.95 = (f32[3,4,128,128]{3,2,1,0:T(8,128)S(1)}, f32[3,4,128,128]{3,2,1,0:T(8,128)S(1)}, f32[6,4,128,128]{3,2,1,0:T(8,128)S(1)}, f32[3,3,128,128]{3,2,1,...) custom-call(s32[3]{0:T(128)S(1)} %pad_add_fusion.role.refs_0_, ...), custom_call_target="tpu_custom_call" | custom-call | flops 1 | bytes 1 | tf_op jit(solution)/shard_map/pallas_call | solution.py:375
  17.7 4.7 %collective-permute-start.6 = (f32[2,128,128]{2,1,0:T(8,128)S(1)}, f32[2,128,128]{2,1,0:T(8,128)S(1)}, u32[]{:S(2)}, u32[]{:S(2)}) collective-permute-start(f32[2,128,128]{2,1,0:T(8,128)S(1)} %get-tuple-element.42), channel_id=1, source_target_pairs={{0,1},{1,0},{2,3},{3,2},{4,5},{5,4},{6,7},{7,6},{8,9},{9,8},{10,11... | collective-permute-start | bytes 393224 | tf_op jit(solution)/shard_map/ppermute | solution.py:409
  22.4 0.0 collective-permute-done.4.refs_7_
  22.4 2.5 %shard_map.96 = (f32[3,4,128,128]{3,2,1,0:T(8,128)S(1)}, f32[3,4,128,128]{3,2,1,0:T(8,128)S(1)}, f32[6,4,128,128]{3,2,1,0:T(8,128)S(1)}, f32[3,3,128,128]{3,2,1,0:T(8,128)S(1)}, f32[3,3,128,128]{3,2,1,0:T(8,128)S(1)}) custom-call(s32[3]{0:T(128)S(1)} %pad_add_fusion.role.refs_0_, f32[7,4,128,128]{3,2,1,0:T(8,128)S(1)} %get-tuple-element.26.refs_1_, ...), custom_call_target="tpu_custom_call" | custom-call | flops 1 | bytes 1 | tf_op jit(solution)/shard_map/pallas_call | solution.py:375
  24.9 0.0 collective-permute-done.5.refs_7_
  24.9 0.0 collective-permute-done.6.refs_10_
  24.9 2.8 %shard_map.97 = (f32[3,4,128,128]{3,2,1,0:T(8,128)}, f32[3,4,128,128]{3,2,1,0:T(8,128)}, f32[6,4,128,128]{3,2,1,0:T(8,128)}, f32[16,128]{1,0:T(8,128)S(1)}) custom-call(s32[3]{0:T(128)S(1)} %pad_add_fusion.role.refs_0_, f32[7,4,128,128]{3,2,1,0:T(8,128)S(1)} %get-tuple-element.26.refs_1_, f32[10,128,128]{2,1,0:T(8,128)S(1)} %get-tuple-element.27.refs_2_, ...), custom_call_target="tpu_custom_call" | custom-call | flops 1 | bytes 1 | tf_op jit(solution)/shard_map/pallas_call | solution.py:375
  27.7 14.0 %all_to_all.9 = f32[16,1,128]{2,1,0:T(1,128)S(1)} all-to-all(f32[16,1,128]{2,1,0:T(1,128)S(1)} %bitcast.6), channel_id=1, replica_groups=mesh['design'=2,'gx'=16] {'gx'}, dimensions={0} | all-to-all | bytes 16384 | tf_op jit(solution)/shard_map/all_to_all | solution.py:394
  41.6 0.5 %reduce_sum.9 = f32[128]{0:T(128)} reduce(f32[16,1,128]{2,1,0:T(1,128)S(1)} %all_to_all.9, f32[]{:T(128)} %constant.22.clone.1), dimensions={0,1}, to_apply=%region_0.1 | reduce | flops 1920 | bytes 8708 | tf_op jit(solution)/shard_map/reduce_sum | solution.py:394
Async XLA Ops:
  0.6 3.5 %copy-start = (f32[4,128,128]{2,1,0:T(8,128)S(1)}, f32[4,128,128]{2,1,0:T(8,128)}, u32[]{:S(2)}) copy-start(f32[4,128,128]{2,1,0:T(8,128)} %own_eps.1) | copy-start | bytes 786436
  0.6 9.0 %collective-permute-start = (f32[3,4,128,128]{3,2,1,0:T(8,128)}, f32[3,4,128,128]{3,2,1,0:T(8,128)S(1)}, u32[]{:S(2)}, u32[]{:S(2)}) collective-permute-start(f32[3,4,128,128]{3,2,1,0:T(8,128)} %own_e.1), channel_id=1, source_target_pairs={{0,1},{1,0},{2,3},{3,2},{4,5},{5,4},{6,7},{7,6},{8,9},{9,8},{10,11... | collective-permute-start | bytes 2359304 | tf_op jit(solution)/shard_map/ppermute | solution.py:409
  1.2 8.5 %collective-permute-start.1 = (f32[3,4,128,128]{3,2,1,0:T(8,128)}, f32[3,4,128,128]{3,2,1,0:T(8,128)S(1)}, u32[]{:S(2)}, u32[]{:S(2)}) collective-permute-start(f32[3,4,128,128]{3,2,1,0:T(8,128)} %own_m.1), channel_id=1, source_target_pairs={{0,1},{1,0},{2,3},{3,2},{4,5},{5,4},{6,7},{7,6},{8,9},{9,8},{10,11... | collective-permute-start | bytes 2359304 | tf_op jit(solution)/shard_map/ppermute | solution.py:409
  3.4 12.0 %collective-permute-start.3 = (f32[6,128,128]{2,1,0:T(8,128)S(1)}, f32[6,128,128]{2,1,0:T(8,128)S(1)}, u32[]{:S(2)}, u32[]{:S(2)}) collective-permute-start(f32[6,128,128]{2,1,0:T(8,128)S(1)} %get-tuple-element.28), channel_id=1, source_target_pairs={{1,2},{3,4},{5,6},{7,8},{9,10},{11,12},{13,14},{2,1},{4,3},{6,5},{... | collective-permute-start | bytes 1179656 | tf_op jit(solution)/shard_map/ppermute | solution.py:412
  4.1 5.5 %collective-permute-start.2 = (f32[4,128,128]{2,1,0:T(8,128)S(1)}, f32[4,128,128]{2,1,0:T(8,128)S(1)}, u32[]{:S(2)}, u32[]{:S(2)}) collective-permute-start(f32[4,128,128]{2,1,0:T(8,128)S(1)} %copy-done), channel_id=1, source_target_pairs={{0,1},{1,0},{2,3},{3,2},{4,5},{5,4},{6,7},{7,6},{8,9},{9,8},{10,11... | collective-permute-start | bytes 786440 | tf_op jit(solution)/shard_map/ppermute | solution.py:409
  8.5 13.9 %collective-permute-start.4 = (f32[4,128,128]{2,1,0:T(8,128)S(1)}, f32[4,128,128]{2,1,0:T(8,128)S(1)}, u32[]{:S(2)}, u32[]{:S(2)}) collective-permute-start(f32[4,128,128]{2,1,0:T(8,128)S(1)} %get-tuple-element.33), channel_id=1, source_target_pairs={{1,2},{3,4},{5,6},{7,8},{9,10},{11,12},{13,14},{2,1},{4,3},{6,5},{... | collective-permute-start | bytes 786440 | tf_op jit(solution)/shard_map/ppermute | solution.py:412
  14.8 10.1 %collective-permute-start.5 = (f32[2,128,128]{2,1,0:T(8,128)S(1)}, f32[2,128,128]{2,1,0:T(8,128)S(1)}, u32[]{:S(2)}, u32[]{:S(2)}) collective-permute-start(f32[2,128,128]{2,1,0:T(8,128)S(1)} %get-tuple-element.39), channel_id=1, source_target_pairs={{1,2},{3,4},{5,6},{7,8},{9,10},{11,12},{13,14},{2,1},{4,3},{6,5},{... | collective-permute-start | bytes 393224 | tf_op jit(solution)/shard_map/ppermute | solution.py:412
  17.7 7.2 %collective-permute-start.6 = (f32[2,128,128]{2,1,0:T(8,128)S(1)}, f32[2,128,128]{2,1,0:T(8,128)S(1)}, u32[]{:S(2)}, u32[]{:S(2)}) collective-permute-start(f32[2,128,128]{2,1,0:T(8,128)S(1)} %get-tuple-element.42), channel_id=1, source_target_pairs={{0,1},{1,0},{2,3},{3,2},{4,5},{5,4},{6,7},{7,6},{8,9},{9,8},{10,11... | collective-permute-start | bytes 393224 | tf_op jit(solution)/shard_map/ppermute | solution.py:409

commit v6 on v5

--- a/solution.py
+++ b/solution.py
@@ -216,31 +216,48 @@
 RIGHT_ELEC = {1: 1, 2: 2, 3: 2, 4: 1, 5: 0}
 
 
-def beyond_left(step, elec, side_e, side_m):
+def pushed(far):
+    return jnp.zeros_like(far[0]), COURANT * far[1], -COURANT * far[0]
+
+
+def beyond_left(step, elec, side_e, side_m, out_m):
     for j in range(LEFT_MAG[step]):
         if j == 0:
             far = (elec[Y, 0], elec[Z, 0])
         else:
             far = (side_e[Y, j - 1], side_e[Z, j - 1])
-        store(side_m, j, magnetic_plane(planes(side_e, j), far, planes(side_m, j)))
-
-
-def beyond_left_electric(step, side_e, side_m, side_eps):
+        if j == step - 1:
+            store(out_m, j, pushed(far))
+        else:
+            store(out_m, j, magnetic_plane(planes(side_e, j), far, planes(side_m, j)))
+
+
+def beyond_left_electric(step, side_e, side_m, side_eps, out_e):
     for j in range(LEFT_ELEC[step]):
-        past = (side_m[Y, j + 1], side_m[Z, j + 1])
-        store(side_e, j, electric_plane(planes(side_m, j), past, planes(side_e, j), side_eps[j]))
-
-
-def beyond_right(step, mag, side_e, side_m, side_eps, last):
+        past = (side_m[Y, j + 1], side_m[Z, j + 1]) if j + 1 < LEFT_MAG[step] else None
+        here = planes(side_m, j)
+        blank = jnp.zeros_like(here[0])
+        before = [blank] * 3 if j == step - 1 else planes(side_e, j)
+        store(out_e, j, electric_plane(here, past, before, side_eps[j]))
+
+
+def beyond_right(step, mag, side_e, side_m, side_eps, last, out_e, out_m):
     for j in range(RIGHT_MAG[step]):
-        far = (side_e[Y, j + 1], side_e[Z, j + 1])
-        store(side_m, j, magnetic_plane(planes(side_e, j), far, planes(side_m, j)))
+        far = (side_e[Y, j + 1], side_e[Z, j + 1]) if j + 1 < step - 1 else None
+        here = planes(side_e, j)
+        before = [jnp.zeros_like(here[0])] * 3 if j == step - 2 else planes(side_m, j)
+        store(out_m, j, magnetic_plane(here, far, before))
     for j in range(RIGHT_ELEC[step]):
         if j == 0:
             past = (mag[Y, last], mag[Z, last])
         else:
-            past = (side_m[Y, j - 1], side_m[Z, j - 1])
-        store(side_e, j, electric_plane(planes(side_m, j), past, planes(side_e, j), side_eps[j]))
+            past = (out_m[Y, j - 1], out_m[Z, j - 1])
+        if j == step - 1:
+            x, y, z = pushed(past)
+            store(out_e, j, (x, y * side_eps[j], z * side_eps[j]))
+        else:
+            new = electric_plane(planes(out_m, j), past, planes(side_e, j), side_eps[j])
+            store(out_e, j, new)
 
 
 def open_kernel(steps, *refs):
@@ -261,16 +278,6 @@
     last = count - 1
     even = role[0] == 0
     side_eps = opening.at[4:6]
-    reached = min(first - 1, STEPS + 1 - first)
-    for j in range(3):
-        for c in range(3):
-            if j < reached:
-                side_e[c, j] = r["side_e_in"][c, j]
-                side_m[c, j] = r["side_m_in"][c, j]
-            elif first < STEPS:
-                side_e[c, j] = jnp.zeros(eps.shape[1:], jnp.float32)
-                side_m[c, j] = jnp.zeros(eps.shape[1:], jnp.float32)
-
     pending = []
 
     def put(src, dst):
@@ -296,14 +303,20 @@
             near = (nears[2 * step - 2], nears[2 * step - 1])
             if step == STEPS:
                 near = (near[0] + r["late_in"][0], near[1] + r["late_in"][1])
+            from_e, from_m = side_e, side_m
+            if step == first > 1:
+                from_e, from_m = r["side_e_in"], r["side_m_in"]
             ref, at = (opening if step < 3 else r["msgs"]), 2 * ((step - 1) % 2)
             far = (ref[at], ref[at + 1])
             if is_even:
                 beyond = near
-                beyond_left(step, src_e, side_e, side_m)
+                beyond_left(step, src_e, from_e, from_m, side_m)
                 past0 = ((far[0] + side_m[Y, 0]) * scale, (far[1] + side_m[Z, 0]) * scale)
             else:
-                beyond = ((far[0] + side_e[Y, 0]) * scale, (far[1] + side_e[Z, 0]) * scale)
+                beyond = far
+                if step > 1:
+                    beyond = (far[0] + from_e[Y, 0], far[1] + from_e[Z, 0])
+                beyond = (beyond[0] * scale, beyond[1] * scale)
                 past0 = past_near(near, src_e)
             waves = (math.cos(ANGULAR * step), math.sin(ANGULAR * step))
             src_a = accum_in if step == steps[0] else accum
@@ -323,9 +336,9 @@
                 for p in range(count):
                     magnetic_at(p)
                 if is_even:
-                    beyond_left_electric(step, side_e, side_m, side_eps)
+                    beyond_left_electric(step, from_e, side_m, side_eps, side_e)
                 else:
-                    beyond_right(step, mag, side_e, side_m, side_eps, last)
+                    beyond_right(step, mag, from_e, from_m, side_eps, last, side_e, side_m)
                 for p in range(count):
                     electric_at(p)
                 continue

time: 42.4 us -> 42.3 us (level)
  no operation moved by 1% of the time
where the time goes in v6:
time: 42.3 us; the launch traced here: 42 us
  Pallas kernels  14.4 us (34%)
  blocking collectives  14.2 us (34%)
  starting transfers between devices  11.6 us (27%)
  between operations  0.74 us (2%)
  other arithmetic  0.62 us (1%)
  waiting for transfers between devices  0.5 us (1%)
    pallas_call x5, Pallas kernels, call(): pl.pallas_call(kernel, out_shape=[shape_of(*o) if i < slow_outs else pltp...  14.4 us
    all_to_all x1, blocking collectives, summed(): return jnp.sum(lax.all_to_all(sums, 'gx', 0, 0, tiled=True), 0)  14.2 us
    ppermute x4, starting transfers between devices, to_mate(): return lax.ppermute(block, 'gx', same_chip)  9.6 us
    ppermute x3, starting transfers between devices, to_chip(): return lax.ppermute(block, 'gx', next_chip)  2.02 us
  transfers between devices with their start and end apart: 7, of which 1 were waited for; matrix products, arithmetic and copies ran while one was open for 0% of the time, Pallas kernels for 28%

profile of v6, /device:TPU:0, one launch (start us, length us, event | category | flops | bytes accessed | tf_op | source)
XLA Modules:
  0.0 42.0 jit_solution(2821446748990582130)
XLA Ops:
  0.6 0.0 copy-start
  0.6 0.5 %collective-permute-start = (f32[3,4,128,128]{3,2,1,0:T(8,128)}, f32[3,4,128,128]{3,2,1,0:T(8,128)S(1)}, u32[]{:S(2)}, u32[]{:S(2)}) collective-permute-start(f32[3,4,128,128]{3,2,1,0:T(8,128)} %own_e.1), channel_id=1, source_target_pairs={{0,1},{1,0},{2,3},{3,2},{4,5},{5,4},{6,7},{7,6},{8,9},{9,8},{10,11... | collective-permute-start | bytes 2359304 | tf_op jit(solution)/shard_map/ppermute | solution.py:422
  1.2 0.1 collective-permute-start.1
  1.2 0.1 pad_add_fusion.role.refs_0_
  1.3 2.1 %shard_map.94 = (f32[6,128,128]{2,1,0:T(8,128)S(1)}, f32[4,128,128]{2,1,0:T(8,128)S(1)}) custom-call(s32[3]{0:T(128)S(1)} %pad_add_fusion.role.refs_0_, f32[3,4,128,128]{3,2,1,0:T(8,128)} %own_e.1, f32[3,4,128,128]{3,2,1,0:T(8,128)} %own_m.1, f32[4,128,128]{2,1,0:T(8,128)} %own_eps.1), custom_call_target="tpu_custom_call" | custom-call | flops 1 | bytes 1 | tf_op jit(solution)/shard_map/pallas_call | solution.py:388
  3.4 0.7 %collective-permute-start.3 = (f32[6,128,128]{2,1,0:T(8,128)S(1)}, f32[6,128,128]{2,1,0:T(8,128)S(1)}, u32[]{:S(2)}, u32[]{:S(2)}) collective-permute-start(f32[6,128,128]{2,1,0:T(8,128)S(1)} %get-tuple-element.28), channel_id=1, source_target_pairs={{1,2},{3,4},{5,6},{7,8},{9,10},{11,12},{13,14},{2,1},{4,3},{6,5},{... | collective-permute-start | bytes 1179656 | tf_op jit(solution)/shard_map/ppermute | solution.py:425
  4.1 0.0 copy-done
  4.1 4.3 %collective-permute-start.2 = (f32[4,128,128]{2,1,0:T(8,128)S(1)}, f32[4,128,128]{2,1,0:T(8,128)S(1)}, u32[]{:S(2)}, u32[]{:S(2)}) collective-permute-start(f32[4,128,128]{2,1,0:T(8,128)S(1)} %copy-done), channel_id=1, source_target_pairs={{0,1},{1,0},{2,3},{3,2},{4,5},{5,4},{6,7},{7,6},{8,9},{9,8},{10,11... | collective-permute-start | bytes 786440 | tf_op jit(solution)/shard_map/ppermute | solution.py:422
  8.5 0.7 %collective-permute-start.4 = (f32[4,128,128]{2,1,0:T(8,128)S(1)}, f32[4,128,128]{2,1,0:T(8,128)S(1)}, u32[]{:S(2)}, u32[]{:S(2)}) collective-permute-start(f32[4,128,128]{2,1,0:T(8,128)S(1)} %get-tuple-element.33), channel_id=1, source_target_pairs={{1,2},{3,4},{5,6},{7,8},{9,10},{11,12},{13,14},{2,1},{4,3},{6,5},{... | collective-permute-start | bytes 786440 | tf_op jit(solution)/shard_map/ppermute | solution.py:425
  9.2 0.5 %collective-permute-done.2.mate_eps = f32[4,128,128]{2,1,0:T(8,128)S(1)} collective-permute-done((f32[4,128,128]{2,1,0:T(8,128)S(1)}, f32[4,128,128]{2,1,0:T(8,128)S(1)}, u32[]{:S(2)}, u32[]{:S(2)}) %collective-permute-start.2) | collective-permute-done | bytes 262176 | tf_op jit(solution)/shard_map/ppermute | solution.py:422
  9.7 0.0 collective-permute-done.mate_e
  9.7 0.0 collective-permute-done.1.mate_m
  9.7 5.1 %shard_map.93 = (f32[7,4,128,128]{3,2,1,0:T(8,128)S(1)}, f32[2,128,128]{2,1,0:T(8,128)S(1)}, f32[10,128,128]{2,1,0:T(8,128)S(1)}, f32[6,4,128,128]{3,2,1,0:T(8,128)S(1)}, f32[6,4,128,128]{3,2,1,0:T(8,128)S(1)}) custom-call(s32[3]{0:T(128)S(1)} %pad_add_fusion.role.refs_0_, f32[3,4,128,128]{3,2,1,0:T(8,128)S(1)} %collective-permute-done.mate_e, ...), custom_call_target="tpu_custom_call" | custom-call | flops 1 | bytes 1 | tf_op jit(solution)/shard_map/pallas_call | solution.py:388
  14.8 0.7 %collective-permute-start.5 = (f32[2,128,128]{2,1,0:T(8,128)S(1)}, f32[2,128,128]{2,1,0:T(8,128)S(1)}, u32[]{:S(2)}, u32[]{:S(2)}) collective-permute-start(f32[2,128,128]{2,1,0:T(8,128)S(1)} %get-tuple-element.39), channel_id=1, source_target_pairs={{1,2},{3,4},{5,6},{7,8},{9,10},{11,12},{13,14},{2,1},{4,3},{6,5},{... | collective-permute-start | bytes 393224 | tf_op jit(solution)/shard_map/ppermute | solution.py:425
  15.5 0.0 collective-permute-done.3.refs_3_
  15.5 2.0 %shard_map.95 = (f32[3,4,128,128]{3,2,1,0:T(8,128)S(1)}, f32[3,4,128,128]{3,2,1,0:T(8,128)S(1)}, f32[6,4,128,128]{3,2,1,0:T(8,128)S(1)}, f32[3,3,128,128]{3,2,1,...) custom-call(s32[3]{0:T(128)S(1)} %pad_add_fusion.role.refs_0_, ...), custom_call_target="tpu_custom_call" | custom-call | flops 1 | bytes 1 | tf_op jit(solution)/shard_map/pallas_call | solution.py:388
  17.5 4.7 %collective-permute-start.6 = (f32[2,128,128]{2,1,0:T(8,128)S(1)}, f32[2,128,128]{2,1,0:T(8,128)S(1)}, u32[]{:S(2)}, u32[]{:S(2)}) collective-permute-start(f32[2,128,128]{2,1,0:T(8,128)S(1)} %get-tuple-element.42), channel_id=1, source_target_pairs={{0,1},{1,0},{2,3},{3,2},{4,5},{5,4},{6,7},{7,6},{8,9},{9,8},{10,11... | collective-permute-start | bytes 393224 | tf_op jit(solution)/shard_map/ppermute | solution.py:422
  22.2 0.0 collective-permute-done.4.refs_7_
  22.2 2.4 %shard_map.96 = (f32[3,4,128,128]{3,2,1,0:T(8,128)S(1)}, f32[3,4,128,128]{3,2,1,0:T(8,128)S(1)}, f32[6,4,128,128]{3,2,1,0:T(8,128)S(1)}, f32[3,3,128,128]{3,2,1,0:T(8,128)S(1)}, f32[3,3,128,128]{3,2,1,0:T(8,128)S(1)}) custom-call(s32[3]{0:T(128)S(1)} %pad_add_fusion.role.refs_0_, f32[7,4,128,128]{3,2,1,0:T(8,128)S(1)} %get-tuple-element.26.refs_1_, ...), custom_call_target="tpu_custom_call" | custom-call | flops 1 | bytes 1 | tf_op jit(solution)/shard_map/pallas_call | solution.py:388
  24.5 0.0 collective-permute-done.5.refs_7_
  24.5 0.0 collective-permute-done.6.refs_10_
  24.5 2.7 %shard_map.97 = (f32[3,4,128,128]{3,2,1,0:T(8,128)}, f32[3,4,128,128]{3,2,1,0:T(8,128)}, f32[6,4,128,128]{3,2,1,0:T(8,128)}, f32[16,128]{1,0:T(8,128)S(1)}) custom-call(s32[3]{0:T(128)S(1)} %pad_add_fusion.role.refs_0_, f32[7,4,128,128]{3,2,1,0:T(8,128)S(1)} %get-tuple-element.26.refs_1_, f32[10,128,128]{2,1,0:T(8,128)S(1)} %get-tuple-element.27.refs_2_, ...), custom_call_target="tpu_custom_call" | custom-call | flops 1 | bytes 1 | tf_op jit(solution)/shard_map/pallas_call | solution.py:388
  27.3 14.2 %all_to_all.9 = f32[16,1,128]{2,1,0:T(1,128)S(1)} all-to-all(f32[16,1,128]{2,1,0:T(1,128)S(1)} %bitcast.6), channel_id=1, replica_groups=mesh['design'=2,'gx'=16] {'gx'}, dimensions={0} | all-to-all | bytes 16384 | tf_op jit(solution)/shard_map/all_to_all | solution.py:407
  41.5 0.5 %reduce_sum.9 = f32[128]{0:T(128)} reduce(f32[16,1,128]{2,1,0:T(1,128)S(1)} %all_to_all.9, f32[]{:T(128)} %constant.22.clone.1), dimensions={0,1}, to_apply=%region_0.1 | reduce | flops 1920 | bytes 8708 | tf_op jit(solution)/shard_map/reduce_sum | solution.py:407
Async XLA Ops:
  0.6 3.5 %copy-start = (f32[4,128,128]{2,1,0:T(8,128)S(1)}, f32[4,128,128]{2,1,0:T(8,128)}, u32[]{:S(2)}) copy-start(f32[4,128,128]{2,1,0:T(8,128)} %own_eps.1) | copy-start | bytes 786436
  0.6 9.0 %collective-permute-start = (f32[3,4,128,128]{3,2,1,0:T(8,128)}, f32[3,4,128,128]{3,2,1,0:T(8,128)S(1)}, u32[]{:S(2)}, u32[]{:S(2)}) collective-permute-start(f32[3,4,128,128]{3,2,1,0:T(8,128)} %own_e.1), channel_id=1, source_target_pairs={{0,1},{1,0},{2,3},{3,2},{4,5},{5,4},{6,7},{7,6},{8,9},{9,8},{10,11... | collective-permute-start | bytes 2359304 | tf_op jit(solution)/shard_map/ppermute | solution.py:422
  1.2 8.5 %collective-permute-start.1 = (f32[3,4,128,128]{3,2,1,0:T(8,128)}, f32[3,4,128,128]{3,2,1,0:T(8,128)S(1)}, u32[]{:S(2)}, u32[]{:S(2)}) collective-permute-start(f32[3,4,128,128]{3,2,1,0:T(8,128)} %own_m.1), channel_id=1, source_target_pairs={{0,1},{1,0},{2,3},{3,2},{4,5},{5,4},{6,7},{7,6},{8,9},{9,8},{10,11... | collective-permute-start | bytes 2359304 | tf_op jit(solution)/shard_map/ppermute | solution.py:422
  3.4 12.0 %collective-permute-start.3 = (f32[6,128,128]{2,1,0:T(8,128)S(1)}, f32[6,128,128]{2,1,0:T(8,128)S(1)}, u32[]{:S(2)}, u32[]{:S(2)}) collective-permute-start(f32[6,128,128]{2,1,0:T(8,128)S(1)} %get-tuple-element.28), channel_id=1, source_target_pairs={{1,2},{3,4},{5,6},{7,8},{9,10},{11,12},{13,14},{2,1},{4,3},{6,5},{... | collective-permute-start | bytes 1179656 | tf_op jit(solution)/shard_map/ppermute | solution.py:425
  4.1 5.5 %collective-permute-start.2 = (f32[4,128,128]{2,1,0:T(8,128)S(1)}, f32[4,128,128]{2,1,0:T(8,128)S(1)}, u32[]{:S(2)}, u32[]{:S(2)}) collective-permute-start(f32[4,128,128]{2,1,0:T(8,128)S(1)} %copy-done), channel_id=1, source_target_pairs={{0,1},{1,0},{2,3},{3,2},{4,5},{5,4},{6,7},{7,6},{8,9},{9,8},{10,11... | collective-permute-start | bytes 786440 | tf_op jit(solution)/shard_map/ppermute | solution.py:422
  8.5 13.7 %collective-permute-start.4 = (f32[4,128,128]{2,1,0:T(8,128)S(1)}, f32[4,128,128]{2,1,0:T(8,128)S(1)}, u32[]{:S(2)}, u32[]{:S(2)}) collective-permute-start(f32[4,128,128]{2,1,0:T(8,128)S(1)} %get-tuple-element.33), channel_id=1, source_target_pairs={{1,2},{3,4},{5,6},{7,8},{9,10},{11,12},{13,14},{2,1},{4,3},{6,5},{... | collective-permute-start | bytes 786440 | tf_op jit(solution)/shard_map/ppermute | solution.py:425
  14.8 9.7 %collective-permute-start.5 = (f32[2,128,128]{2,1,0:T(8,128)S(1)}, f32[2,128,128]{2,1,0:T(8,128)S(1)}, u32[]{:S(2)}, u32[]{:S(2)}) collective-permute-start(f32[2,128,128]{2,1,0:T(8,128)S(1)} %get-tuple-element.39), channel_id=1, source_target_pairs={{1,2},{3,4},{5,6},{7,8},{9,10},{11,12},{13,14},{2,1},{4,3},{6,5},{... | collective-permute-start | bytes 393224 | tf_op jit(solution)/shard_map/ppermute | solution.py:425
  17.5 7.0 %collective-permute-start.6 = (f32[2,128,128]{2,1,0:T(8,128)S(1)}, f32[2,128,128]{2,1,0:T(8,128)S(1)}, u32[]{:S(2)}, u32[]{:S(2)}) collective-permute-start(f32[2,128,128]{2,1,0:T(8,128)S(1)} %get-tuple-element.42), channel_id=1, source_target_pairs={{0,1},{1,0},{2,3},{3,2},{4,5},{5,4},{6,7},{7,6},{8,9},{9,8},{10,11... | collective-permute-start | bytes 393224 | tf_op jit(solution)/shard_map/ppermute | solution.py:422

commit v7 on v6

--- a/solution.py
+++ b/solution.py
@@ -319,7 +319,7 @@
                 beyond = (beyond[0] * scale, beyond[1] * scale)
                 past0 = past_near(near, src_e)
             waves = (math.cos(ANGULAR * step), math.sin(ANGULAR * step))
-            src_a = accum_in if step == steps[0] else accum
+            before = (math.cos(ANGULAR * (step - 1)), math.sin(ANGULAR * (step - 1)))
 
             def magnetic_at(p):
                 nxt = (src_e[Y, p + 1], src_e[Z, p + 1]) if p < last else beyond
@@ -327,10 +327,16 @@
 
             def electric_at(p):
                 past = (mag[Y, p - 1], mag[Z, p - 1]) if p else past0
-                new = electric_plane(planes(mag, p), past, planes(src_e, p), eps[p])
+                held = planes(src_e, p)
+                new = electric_plane(planes(mag, p), past, held, eps[p])
                 store(elec, p, new)
+                if step < steps[-1]:
+                    return
                 for c in range(6):
-                    accum[c, p] = src_a[c, p] + waves[c // 3] * new[c % 3]
+                    value = accum_in[c, p] + waves[c // 3] * new[c % 3]
+                    if step > first:
+                        value = value + before[c // 3] * held[c % 3]
+                    accum[c, p] = value
 
             if step < STEPS:
                 for p in range(count):

time: 42.3 us -> 42.3 us (level)
  no operation moved by 1% of the time
where the time goes in v7:
time: 42.3 us; the launch traced here: 42 us
  Pallas kernels  14.4 us (34%)
  blocking collectives  14.2 us (34%)
  starting transfers between devices  11.6 us (27%)
  between operations  0.74 us (2%)
  other arithmetic  0.62 us (1%)
  waiting for transfers between devices  0.5 us (1%)
    pallas_call x5, Pallas kernels, call(): pl.pallas_call(kernel, out_shape=[shape_of(*o) if i < slow_outs else pltp...  14.4 us
    all_to_all x1, blocking collectives, summed(): return jnp.sum(lax.all_to_all(sums, 'gx', 0, 0, tiled=True), 0)  14.2 us
    ppermute x4, starting transfers between devices, to_mate(): return lax.ppermute(block, 'gx', same_chip)  9.59 us
    ppermute x3, starting transfers between devices, to_chip(): return lax.ppermute(block, 'gx', next_chip)  2.02 us
  transfers between devices with their start and end apart: 7, of which 1 were waited for; matrix products, arithmetic and copies ran while one was open for 0% of the time, Pallas kernels for 28%

profile of v7, /device:TPU:0, one launch (start us, length us, event | category | flops | bytes accessed | tf_op | source)
XLA Modules:
  0.0 42.0 jit_solution(5136571489175535565)
XLA Ops:
  0.6 0.0 copy-start
  0.6 0.5 %collective-permute-start = (f32[3,4,128,128]{3,2,1,0:T(8,128)}, f32[3,4,128,128]{3,2,1,0:T(8,128)S(1)}, u32[]{:S(2)}, u32[]{:S(2)}) collective-permute-start(f32[3,4,128,128]{3,2,1,0:T(8,128)} %own_e.1), channel_id=1, source_target_pairs={{0,1},{1,0},{2,3},{3,2},{4,5},{5,4},{6,7},{7,6},{8,9},{9,8},{10,11... | collective-permute-start | bytes 2359304 | tf_op jit(solution)/shard_map/ppermute | solution.py:428
  1.2 0.1 collective-permute-start.1
  1.2 0.1 pad_add_fusion.role.refs_0_
  1.3 2.1 %shard_map.94 = (f32[6,128,128]{2,1,0:T(8,128)S(1)}, f32[4,128,128]{2,1,0:T(8,128)S(1)}) custom-call(s32[3]{0:T(128)S(1)} %pad_add_fusion.role.refs_0_, f32[3,4,128,128]{3,2,1,0:T(8,128)} %own_e.1, f32[3,4,128,128]{3,2,1,0:T(8,128)} %own_m.1, f32[4,128,128]{2,1,0:T(8,128)} %own_eps.1), custom_call_target="tpu_custom_call" | custom-call | flops 1 | bytes 1 | tf_op jit(solution)/shard_map/pallas_call | solution.py:394
  3.4 0.7 %collective-permute-start.3 = (f32[6,128,128]{2,1,0:T(8,128)S(1)}, f32[6,128,128]{2,1,0:T(8,128)S(1)}, u32[]{:S(2)}, u32[]{:S(2)}) collective-permute-start(f32[6,128,128]{2,1,0:T(8,128)S(1)} %get-tuple-element.28), channel_id=1, source_target_pairs={{1,2},{3,4},{5,6},{7,8},{9,10},{11,12},{13,14},{2,1},{4,3},{6,5},{... | collective-permute-start | bytes 1179656 | tf_op jit(solution)/shard_map/ppermute | solution.py:431
  4.1 0.0 copy-done
  4.1 4.3 %collective-permute-start.2 = (f32[4,128,128]{2,1,0:T(8,128)S(1)}, f32[4,128,128]{2,1,0:T(8,128)S(1)}, u32[]{:S(2)}, u32[]{:S(2)}) collective-permute-start(f32[4,128,128]{2,1,0:T(8,128)S(1)} %copy-done), channel_id=1, source_target_pairs={{0,1},{1,0},{2,3},{3,2},{4,5},{5,4},{6,7},{7,6},{8,9},{9,8},{10,11... | collective-permute-start | bytes 786440 | tf_op jit(solution)/shard_map/ppermute | solution.py:428
  8.5 0.7 %collective-permute-start.4 = (f32[4,128,128]{2,1,0:T(8,128)S(1)}, f32[4,128,128]{2,1,0:T(8,128)S(1)}, u32[]{:S(2)}, u32[]{:S(2)}) collective-permute-start(f32[4,128,128]{2,1,0:T(8,128)S(1)} %get-tuple-element.33), channel_id=1, source_target_pairs={{1,2},{3,4},{5,6},{7,8},{9,10},{11,12},{13,14},{2,1},{4,3},{6,5},{... | collective-permute-start | bytes 786440 | tf_op jit(solution)/shard_map/ppermute | solution.py:431
  9.2 0.5 %collective-permute-done.2.mate_eps = f32[4,128,128]{2,1,0:T(8,128)S(1)} collective-permute-done((f32[4,128,128]{2,1,0:T(8,128)S(1)}, f32[4,128,128]{2,1,0:T(8,128)S(1)}, u32[]{:S(2)}, u32[]{:S(2)}) %collective-permute-start.2) | collective-permute-done | bytes 262176 | tf_op jit(solution)/shard_map/ppermute | solution.py:428
  9.7 0.0 collective-permute-done.mate_e
  9.7 0.0 collective-permute-done.1.mate_m
  9.7 5.1 %shard_map.93 = (f32[7,4,128,128]{3,2,1,0:T(8,128)S(1)}, f32[2,128,128]{2,1,0:T(8,128)S(1)}, f32[10,128,128]{2,1,0:T(8,128)S(1)}, f32[6,4,128,128]{3,2,1,0:T(8,128)S(1)}, f32[6,4,128,128]{3,2,1,0:T(8,128)S(1)}) custom-call(s32[3]{0:T(128)S(1)} %pad_add_fusion.role.refs_0_, f32[3,4,128,128]{3,2,1,0:T(8,128)S(1)} %collective-permute-done.mate_e, ...), custom_call_target="tpu_custom_call" | custom-call | flops 1 | bytes 1 | tf_op jit(solution)/shard_map/pallas_call | solution.py:394
  14.8 0.7 %collective-permute-start.5 = (f32[2,128,128]{2,1,0:T(8,128)S(1)}, f32[2,128,128]{2,1,0:T(8,128)S(1)}, u32[]{:S(2)}, u32[]{:S(2)}) collective-permute-start(f32[2,128,128]{2,1,0:T(8,128)S(1)} %get-tuple-element.39), channel_id=1, source_target_pairs={{1,2},{3,4},{5,6},{7,8},{9,10},{11,12},{13,14},{2,1},{4,3},{6,5},{... | collective-permute-start | bytes 393224 | tf_op jit(solution)/shard_map/ppermute | solution.py:431
  15.5 0.0 collective-permute-done.3.refs_3_
  15.5 2.0 %shard_map.95 = (f32[3,4,128,128]{3,2,1,0:T(8,128)S(1)}, f32[3,4,128,128]{3,2,1,0:T(8,128)S(1)}, f32[6,4,128,128]{3,2,1,0:T(8,128)S(1)}, f32[3,3,128,128]{3,2,1,...) custom-call(s32[3]{0:T(128)S(1)} %pad_add_fusion.role.refs_0_, ...), custom_call_target="tpu_custom_call" | custom-call | flops 1 | bytes 1 | tf_op jit(solution)/shard_map/pallas_call | solution.py:394
  17.5 4.6 %collective-permute-start.6 = (f32[2,128,128]{2,1,0:T(8,128)S(1)}, f32[2,128,128]{2,1,0:T(8,128)S(1)}, u32[]{:S(2)}, u32[]{:S(2)}) collective-permute-start(f32[2,128,128]{2,1,0:T(8,128)S(1)} %get-tuple-element.42), channel_id=1, source_target_pairs={{0,1},{1,0},{2,3},{3,2},{4,5},{5,4},{6,7},{7,6},{8,9},{9,8},{10,11... | collective-permute-start | bytes 393224 | tf_op jit(solution)/shard_map/ppermute | solution.py:428
  22.2 0.0 collective-permute-done.4.refs_7_
  22.2 2.4 %shard_map.96 = (f32[3,4,128,128]{3,2,1,0:T(8,128)S(1)}, f32[3,4,128,128]{3,2,1,0:T(8,128)S(1)}, f32[6,4,128,128]{3,2,1,0:T(8,128)S(1)}, f32[3,3,128,128]{3,2,1,0:T(8,128)S(1)}, f32[3,3,128,128]{3,2,1,0:T(8,128)S(1)}) custom-call(s32[3]{0:T(128)S(1)} %pad_add_fusion.role.refs_0_, f32[7,4,128,128]{3,2,1,0:T(8,128)S(1)} %get-tuple-element.26.refs_1_, ...), custom_call_target="tpu_custom_call" | custom-call | flops 1 | bytes 1 | tf_op jit(solution)/shard_map/pallas_call | solution.py:394
  24.5 0.0 collective-permute-done.5.refs_7_
  24.5 0.0 collective-permute-done.6.refs_10_
  24.6 2.7 %shard_map.97 = (f32[3,4,128,128]{3,2,1,0:T(8,128)}, f32[3,4,128,128]{3,2,1,0:T(8,128)}, f32[6,4,128,128]{3,2,1,0:T(8,128)}, f32[16,128]{1,0:T(8,128)S(1)}) custom-call(s32[3]{0:T(128)S(1)} %pad_add_fusion.role.refs_0_, f32[7,4,128,128]{3,2,1,0:T(8,128)S(1)} %get-tuple-element.26.refs_1_, f32[10,128,128]{2,1,0:T(8,128)S(1)} %get-tuple-element.27.refs_2_, ...), custom_call_target="tpu_custom_call" | custom-call | flops 1 | bytes 1 | tf_op jit(solution)/shard_map/pallas_call | solution.py:394
  27.3 14.2 %all_to_all.9 = f32[16,1,128]{2,1,0:T(1,128)S(1)} all-to-all(f32[16,1,128]{2,1,0:T(1,128)S(1)} %bitcast.6), channel_id=1, replica_groups=mesh['design'=2,'gx'=16] {'gx'}, dimensions={0} | all-to-all | bytes 16384 | tf_op jit(solution)/shard_map/all_to_all | solution.py:413
  41.5 0.5 %reduce_sum.9 = f32[128]{0:T(128)} reduce(f32[16,1,128]{2,1,0:T(1,128)S(1)} %all_to_all.9, f32[]{:T(128)} %constant.22.clone.1), dimensions={0,1}, to_apply=%region_0.1 | reduce | flops 1920 | bytes 8708 | tf_op jit(solution)/shard_map/reduce_sum | solution.py:413
Async XLA Ops:
  0.6 3.5 %copy-start = (f32[4,128,128]{2,1,0:T(8,128)S(1)}, f32[4,128,128]{2,1,0:T(8,128)}, u32[]{:S(2)}) copy-start(f32[4,128,128]{2,1,0:T(8,128)} %own_eps.1) | copy-start | bytes 786436
  0.6 9.0 %collective-permute-start = (f32[3,4,128,128]{3,2,1,0:T(8,128)}, f32[3,4,128,128]{3,2,1,0:T(8,128)S(1)}, u32[]{:S(2)}, u32[]{:S(2)}) collective-permute-start(f32[3,4,128,128]{3,2,1,0:T(8,128)} %own_e.1), channel_id=1, source_target_pairs={{0,1},{1,0},{2,3},{3,2},{4,5},{5,4},{6,7},{7,6},{8,9},{9,8},{10,11... | collective-permute-start | bytes 2359304 | tf_op jit(solution)/shard_map/ppermute | solution.py:428
  1.2 8.5 %collective-permute-start.1 = (f32[3,4,128,128]{3,2,1,0:T(8,128)}, f32[3,4,128,128]{3,2,1,0:T(8,128)S(1)}, u32[]{:S(2)}, u32[]{:S(2)}) collective-permute-start(f32[3,4,128,128]{3,2,1,0:T(8,128)} %own_m.1), channel_id=1, source_target_pairs={{0,1},{1,0},{2,3},{3,2},{4,5},{5,4},{6,7},{7,6},{8,9},{9,8},{10,11... | collective-permute-start | bytes 2359304 | tf_op jit(solution)/shard_map/ppermute | solution.py:428
  3.4 12.0 %collective-permute-start.3 = (f32[6,128,128]{2,1,0:T(8,128)S(1)}, f32[6,128,128]{2,1,0:T(8,128)S(1)}, u32[]{:S(2)}, u32[]{:S(2)}) collective-permute-start(f32[6,128,128]{2,1,0:T(8,128)S(1)} %get-tuple-element.28), channel_id=1, source_target_pairs={{1,2},{3,4},{5,6},{7,8},{9,10},{11,12},{13,14},{2,1},{4,3},{6,5},{... | collective-permute-start | bytes 1179656 | tf_op jit(solution)/shard_map/ppermute | solution.py:431
  4.1 5.5 %collective-permute-start.2 = (f32[4,128,128]{2,1,0:T(8,128)S(1)}, f32[4,128,128]{2,1,0:T(8,128)S(1)}, u32[]{:S(2)}, u32[]{:S(2)}) collective-permute-start(f32[4,128,128]{2,1,0:T(8,128)S(1)} %copy-done), channel_id=1, source_target_pairs={{0,1},{1,0},{2,3},{3,2},{4,5},{5,4},{6,7},{7,6},{8,9},{9,8},{10,11... | collective-permute-start | bytes 786440 | tf_op jit(solution)/shard_map/ppermute | solution.py:428
  8.5 13.7 %collective-permute-start.4 = (f32[4,128,128]{2,1,0:T(8,128)S(1)}, f32[4,128,128]{2,1,0:T(8,128)S(1)}, u32[]{:S(2)}, u32[]{:S(2)}) collective-permute-start(f32[4,128,128]{2,1,0:T(8,128)S(1)} %get-tuple-element.33), channel_id=1, source_target_pairs={{1,2},{3,4},{5,6},{7,8},{9,10},{11,12},{13,14},{2,1},{4,3},{6,5},{... | collective-permute-start | bytes 786440 | tf_op jit(solution)/shard_map/ppermute | solution.py:431
  14.8 9.7 %collective-permute-start.5 = (f32[2,128,128]{2,1,0:T(8,128)S(1)}, f32[2,128,128]{2,1,0:T(8,128)S(1)}, u32[]{:S(2)}, u32[]{:S(2)}) collective-permute-start(f32[2,128,128]{2,1,0:T(8,128)S(1)} %get-tuple-element.39), channel_id=1, source_target_pairs={{1,2},{3,4},{5,6},{7,8},{9,10},{11,12},{13,14},{2,1},{4,3},{6,5},{... | collective-permute-start | bytes 393224 | tf_op jit(solution)/shard_map/ppermute | solution.py:431
  17.5 7.0 %collective-permute-start.6 = (f32[2,128,128]{2,1,0:T(8,128)S(1)}, f32[2,128,128]{2,1,0:T(8,128)S(1)}, u32[]{:S(2)}, u32[]{:S(2)}) collective-permute-start(f32[2,128,128]{2,1,0:T(8,128)S(1)} %get-tuple-element.42), channel_id=1, source_target_pairs={{0,1},{1,0},{2,3},{3,2},{4,5},{5,4},{6,7},{7,6},{8,9},{9,8},{10,11... | collective-permute-start | bytes 393224 | tf_op jit(solution)/shard_map/ppermute | solution.py:428
